TPU v7x, 128 devices: a whole 4x4x4 slice. The times are simulated.
128 devices in a mesh: rep: 8 (over z_lo, y), shard: 16 (over z_hi, x, core).
Axes of the slice: x: 4, y: 4, z: 4 (z_hi: 2, z_lo: 2; z = z_hi * 2 + z_lo), core: 2. Of those that a mesh axis runs over, the one named last changes fastest.
Arguments:
- tokens: bfloat16 [16384, 2048], P(('rep', 'shard')), may hold values from -6 to 6
- cotangent: bfloat16 [16384, 2048], P(('rep', 'shard')), may hold values from -6 to 6
- starts: int32 [16384], P(('rep', 'shard')), may hold values from 0 to 2047, as said below
- attn_gain: bfloat16 [2048], P('shard'), may hold values from 0.5 to 1.5
- query_key_value_weight: bfloat16 [2048, 2560], P('shard'), may hold values from -0.125 to 0.125
- w_out: bfloat16 [2048, 2048], P('shard'), may hold values from -0.5 to 0.5
- ffn_gain: bfloat16 [2048], P('shard'), may hold values from 0.5 to 1.5
- w_gate_up: bfloat16 [2048, 11264], P('shard'), may hold values from -0.125 to 0.125
- w_down: bfloat16 [5632, 2048], P('shard'), may hold values from -0.078125 to 0.078125
Outputs:
- mixed_out: bfloat16 [16384, 2048], P(('rep', 'shard'))
- input_grad: bfloat16 [16384, 2048], P(('rep', 'shard'))
- grad_attn_gain: float32 [2048], P('shard')
- grad_qkv: float32 [2048, 2560], P('shard')
- grad_out: float32 [2048, 2048], P('shard')
- grad_ffn_gain: float32 [2048], P('shard')
- grad_gate_up: float32 [2048, 11264], P('shard')
- grad_down: float32 [5632, 2048], P('shard')
Inputs may be any that keep to these rules, and one draw needn't show every extreme that they name: Each sequence of 2048 tokens is a pack of contiguous documents; starts is the same for all tokens of a document, equals the index of its first token within the sequence, is 0 for the first document, and is never above the token's own index.
All inputs are finite; a program needn't handle non-finite values.
Results may differ from a plain program's by a relative error of at most 0.024.
Values may be sent and summed in bfloat16 or wider, within the bound.
No kernel may reach another device: no remote copies, remote signals or barrier semaphores. Data moves between devices by JAX's collectives and lax.ppermute only.
A program may use at most 576 MiB of HBM per device.

v0:
```python
import math

import jax
import jax.numpy as jnp
from jax import lax
from jax.sharding import PartitionSpec as P

QUERY_HEADS = 32
KEY_VALUE_HEADS = 4
HEAD_SIZE = 64


EPS = 1e-05
ROPE_BASE = 10000.0
NEGATIVE_FILLER = -1e30


def in_one_piece(arrays, axis, dim, along):
    widths = [math.prod(a.shape[along:]) for a in arrays]
    both = jnp.concatenate(
        [a.reshape(*a.shape[:along], w) for a, w in zip(arrays, widths)], axis=along
    )
    filled = lax.all_gather(both, axis, axis=dim, tiled=True)
    pieces = jnp.split(filled, [sum(widths[:k]) for k in range(1, len(widths))], axis=along)
    return tuple(
        (b.reshape(*filled.shape[:along], *a.shape[along:]) for a, b in zip(arrays, pieces))
    )


def side_by_side(arrays, axis, dim, along):
    ends, at = ([], 0)
    for a in arrays[:-1]:
        at += a.shape[along]
        ends.append(at)
    both = jnp.concatenate(arrays, axis=along)
    return tuple(jnp.split(lax.all_gather(both, axis, axis=dim, tiled=True), ends, axis=along))


def in_one_piece_2(arrays, axis, dim, along):
    ends, at = ([], 0)
    for a in arrays[:-1]:
        at += a.shape[along]
        ends.append(at)
    both = jnp.concatenate(arrays, axis=along)
    return tuple(
        jnp.split(lax.psum_scatter(both, axis, scatter_dimension=dim, tiled=True), ends, axis=along)
    )


def split_up(shard, dim, peers):
    before, after = (shard.shape[:dim], shard.shape[dim + 1 :])
    return jnp.moveaxis(shard.reshape(*before, peers, -1, *after), dim, 0)


def sent_and_summed(shard, axis, dim):
    pieces = split_up(shard, dim, lax.axis_size(axis))
    arrived = lax.all_to_all(pieces, axis, split_axis=0, concat_axis=0, tiled=True)
    return arrived.sum(axis=0)


def rope_tables(positions):
    half_size = HEAD_SIZE // 2
    freqs = jnp.exp(
        jnp.arange(half_size, dtype=jnp.float32) * (-2.0 * math.log(ROPE_BASE) / HEAD_SIZE)
    )
    angles = positions.astype(jnp.float32)[:, None] * freqs[None, :]
    cosine_table = jnp.concatenate([jnp.cos(angles), jnp.cos(angles)], axis=1)
    sine_table = jnp.concatenate([jnp.sin(angles), jnp.sin(angles)], axis=1)
    return (cosine_table, sine_table)


def apply_rotary(vectors, cosine_table, sine_table):
    half_size = vectors.shape[-1] // 2
    turned = jnp.concatenate([-vectors[..., half_size:], vectors[..., :half_size]], axis=-1)
    return vectors * cosine_table[:, None, :] + turned * sine_table[:, None, :]


def reverse_rotary(grads, cosine_table, sine_table):
    half_size = grads.shape[-1] // 2
    scaled = grads * sine_table[:, None, :]
    turned = jnp.concatenate([scaled[..., half_size:], -scaled[..., :half_size]], axis=-1)
    return grads * cosine_table[:, None, :] + turned


def rms_forward(value_rows):
    rstd = lax.rsqrt(jnp.mean(value_rows * value_rows, axis=1, keepdims=True) + EPS)
    return (value_rows * rstd, rstd)


def rms_backward(d_normed, scaled, rstd, gain):
    gain_term = jnp.sum(d_normed * scaled, axis=0)
    inner = d_normed * gain[None, :]
    d_values = rstd * (inner - scaled * jnp.mean(inner * scaled, axis=1, keepdims=True))
    return (d_values, gain_term)


def times_trans(left, right):
    return lax.dot_general(
        left, right, (((1,), (1,)), ((), ())), preferred_element_type=jnp.float32
    )


def trans_times(left, right):
    return lax.dot_general(
        left, right, (((0,), (0,)), ((), ())), preferred_element_type=jnp.float32
    )


def body(
    tokens, cotangent, starts, attn_gain, query_key_value_weight, w_out, ffn_gain, w_gate_up, w_down
):
    row_total = tokens.shape[0]
    model_feature_width = tokens.shape[1]
    shard_count = lax.axis_size("shard")
    seq_len = row_total * shard_count
    rows_per_block = min(512, seq_len)
    block_total = seq_len // rows_per_block
    group_members = QUERY_HEADS // KEY_VALUE_HEADS
    key_value_columns = KEY_VALUE_HEADS * HEAD_SIZE
    qkv_cols = model_feature_width + 2 * key_value_columns
    scale = 1.0 / math.sqrt(HEAD_SIZE)
    global_rows = lax.axis_index("shard") * row_total + jnp.arange(row_total, dtype=jnp.int32)
    cosine_table, sine_table = rope_tables(global_rows - starts)
    earliest = jnp.min(starts)
    latest = global_rows[row_total - 1]
    gain_one, qkv_weight, out_weight = in_one_piece(
        (attn_gain, query_key_value_weight, w_out), "shard", 0, 1
    )
    inputs = tokens.astype(jnp.float32)
    scaled_one, rstd_one = rms_forward(inputs)
    normed_one = (scaled_one * gain_one.astype(jnp.float32)[None, :]).astype(jnp.bfloat16)
    query_key_value_whole = jnp.dot(normed_one, qkv_weight, preferred_element_type=jnp.float32)
    query_matrix = apply_rotary(
        query_key_value_whole[:, :model_feature_width].reshape(row_total, QUERY_HEADS, HEAD_SIZE),
        cosine_table,
        sine_table,
    ).astype(jnp.bfloat16)
    key_rot = apply_rotary(
        query_key_value_whole[
            :, model_feature_width : model_feature_width + key_value_columns
        ].reshape(row_total, KEY_VALUE_HEADS, HEAD_SIZE),
        cosine_table,
        sine_table,
    )
    key_rot = key_rot.astype(jnp.bfloat16).reshape(row_total, key_value_columns)
    value_b = query_key_value_whole[:, model_feature_width + key_value_columns :].astype(
        jnp.bfloat16
    )
    key_rows_whole, value_rows_whole = side_by_side((key_rot, value_b), "shard", 0, 1)
    key_block_list = key_rows_whole.reshape(block_total, rows_per_block, KEY_VALUE_HEADS, HEAD_SIZE)
    value_block_list = value_rows_whole.reshape(
        block_total, rows_per_block, KEY_VALUE_HEADS, HEAD_SIZE
    )
    offsets = jnp.arange(block_total, dtype=jnp.int32) * rows_per_block
    query_four_axes = query_matrix.reshape(row_total, KEY_VALUE_HEADS, group_members, HEAD_SIZE)

    def scores_of(key_blk, offset):
        scores = (
            jnp.einsum(
                "tgmd,sgd->gmts", query_four_axes, key_blk, preferred_element_type=jnp.float32
            )
            * scale
        )
        columns = offset + jnp.arange(rows_per_block, dtype=jnp.int32)
        allowed = (columns[None, :] >= starts[:, None]) & (columns[None, :] <= global_rows[:, None])
        return (scores, allowed)

    def needed(offset):
        return (offset <= latest) & (offset + rows_per_block - 1 >= earliest)

    def stat_step(state_now, block_in):
        key_blk, offset = block_in

        def stat_live_block(state_in):
            run_max, run_sum = state_in
            scores, allowed = scores_of(key_blk, offset)
            masked = jnp.where(allowed, scores, NEGATIVE_FILLER)
            new_max = jnp.maximum(run_max, jnp.max(masked, axis=-1))
            expos = jnp.where(allowed, jnp.exp(masked - new_max[..., None]), 0.0)
            return (new_max, run_sum * jnp.exp(run_max - new_max) + jnp.sum(expos, axis=-1))

        def stat_skip_block(state_in):
            return state_in

        return (lax.cond(needed(offset), stat_live_block, stat_skip_block, state_now), None)

    stat_init = (
        jnp.full((KEY_VALUE_HEADS, group_members, row_total), NEGATIVE_FILLER, jnp.float32),
        jnp.zeros((KEY_VALUE_HEADS, group_members, row_total), jnp.float32),
    )
    (run_max, run_sum), unused = lax.scan(stat_step, stat_init, (key_block_list, offsets))
    log_total = run_max + jnp.log(run_sum)

    def out_step(summed, block_in):
        key_blk, value_blk, offset = block_in

        def out_live_block(summed_in):
            scores, allowed = scores_of(key_blk, offset)
            probs_b = jnp.where(allowed, jnp.exp(scores - log_total[..., None]), 0.0).astype(
                jnp.bfloat16
            )
            return summed_in + jnp.einsum(
                "gmts,sgd->tgmd", probs_b, value_blk, preferred_element_type=jnp.float32
            )

        def out_skip_block(summed_in):
            return summed_in

        return (lax.cond(needed(offset), out_live_block, out_skip_block, summed), None)

    attended_rows, unused = lax.scan(
        out_step,
        jnp.zeros((row_total, KEY_VALUE_HEADS, group_members, HEAD_SIZE), jnp.float32),
        (key_block_list, value_block_list, offsets),
    )
    attended_rows = attended_rows.reshape(row_total, model_feature_width)
    attended_b = attended_rows.astype(jnp.bfloat16)
    hidden_mid = inputs + jnp.dot(attended_b, out_weight, preferred_element_type=jnp.float32)
    gain_two, gate_up_weight, down_weight = (
        lax.all_gather(ffn_gain, "shard", axis=0, tiled=True),
        lax.all_gather(w_gate_up, "shard", axis=0, tiled=True),
        lax.all_gather(w_down, "shard", axis=0, tiled=True),
    )
    scaled_two, rstd_two = rms_forward(hidden_mid)
    normed_two = (scaled_two * gain_two.astype(jnp.float32)[None, :]).astype(jnp.bfloat16)
    gate_up = jnp.dot(normed_two, gate_up_weight, preferred_element_type=jnp.float32)
    ff_width = gate_up.shape[1] // 2
    gate_part = gate_up[:, :ff_width]
    up_part = gate_up[:, ff_width:]
    sigmoid_gate = jax.nn.sigmoid(gate_part)
    silu_gate = gate_part * sigmoid_gate
    activated = (silu_gate * up_part).astype(jnp.bfloat16)
    mixed = hidden_mid + jnp.dot(activated, down_weight, preferred_element_type=jnp.float32)
    normed_one_cols, attended_cols, normed_two_cols, activated_cols = (
        lax.all_to_all(normed_one, "shard", split_axis=1, concat_axis=0, tiled=True),
        lax.all_to_all(attended_b, "shard", split_axis=1, concat_axis=0, tiled=True),
        lax.all_to_all(normed_two, "shard", split_axis=1, concat_axis=0, tiled=True),
        lax.all_to_all(activated, "shard", split_axis=1, concat_axis=0, tiled=True),
    )
    d_act = times_trans(cotangent, down_weight)
    d_gate = d_act * up_part * (sigmoid_gate * (1.0 + gate_part * (1.0 - sigmoid_gate)))
    d_up = d_act * silu_gate
    d_gate_up = jnp.concatenate([d_gate, d_up], axis=1).astype(jnp.bfloat16)
    cot_rows, d_gate_up_rows = side_by_side((cotangent, d_gate_up), "shard", 0, 1)
    grad_down = trans_times(activated_cols, cot_rows)
    grad_gate_up = trans_times(normed_two_cols, d_gate_up_rows)
    d_normed_two = times_trans(d_gate_up, gate_up_weight)
    d_mid_norm, gain_two_term = rms_backward(
        d_normed_two, scaled_two, rstd_two, gain_two.astype(jnp.float32)
    )
    d_mid = cotangent.astype(jnp.float32) + d_mid_norm
    d_branch = d_mid.astype(jnp.bfloat16)
    attended_grad = times_trans(d_branch, out_weight).astype(jnp.bfloat16)
    attended_grad_four = attended_grad.reshape(row_total, KEY_VALUE_HEADS, group_members, HEAD_SIZE)
    delta = jnp.sum(
        attended_grad_four.astype(jnp.float32)
        * attended_rows.reshape(row_total, KEY_VALUE_HEADS, group_members, HEAD_SIZE),
        axis=-1,
    )
    delta = jnp.transpose(delta, (1, 2, 0))

    def back_step(d_query, block_in):
        key_blk, value_blk, offset = block_in

        def back_live_block(d_query_in):
            scores, allowed = scores_of(key_blk, offset)
            probs = jnp.where(allowed, jnp.exp(scores - log_total[..., None]), 0.0)
            d_probs = jnp.einsum(
                "tgmd,sgd->gmts", attended_grad_four, value_blk, preferred_element_type=jnp.float32
            )
            d_scores = (probs * (d_probs - delta[..., None])).astype(jnp.bfloat16)
            d_query_out = (
                d_query_in
                + jnp.einsum(
                    "gmts,sgd->tgmd", d_scores, key_blk, preferred_element_type=jnp.float32
                )
                * scale
            )
            d_key = (
                jnp.einsum(
                    "gmts,tgmd->sgd", d_scores, query_four_axes, preferred_element_type=jnp.float32
                )
                * scale
            )
            d_value = jnp.einsum(
                "gmts,tgmd->sgd",
                probs.astype(jnp.bfloat16),
                attended_grad_four,
                preferred_element_type=jnp.float32,
            )
            return (d_query_out, (d_key, d_value))

        def back_skip_block(d_query_in):
            empty_block = jnp.zeros((rows_per_block, KEY_VALUE_HEADS, HEAD_SIZE), jnp.float32)
            return (d_query_in, (empty_block, empty_block))

        return lax.cond(needed(offset), back_live_block, back_skip_block, d_query)

    d_query, (d_keys, d_values) = lax.scan(
        back_step,
        jnp.zeros((row_total, KEY_VALUE_HEADS, group_members, HEAD_SIZE), jnp.float32),
        (key_block_list, value_block_list, offsets),
    )
    d_keys = d_keys.reshape(seq_len, key_value_columns)
    d_values = d_values.reshape(seq_len, key_value_columns)
    key_grad_local, d_value_own = tuple(
        (
            part.astype(jnp.float32)
            for part in in_one_piece_2(
                (d_keys.astype(jnp.bfloat16), d_values.astype(jnp.bfloat16)), "shard", 0, 1
            )
        )
    )
    d_query_plain = reverse_rotary(
        d_query.reshape(row_total, QUERY_HEADS, HEAD_SIZE), cosine_table, sine_table
    ).reshape(row_total, model_feature_width)
    key_grad_unrotated = reverse_rotary(
        key_grad_local.reshape(row_total, KEY_VALUE_HEADS, HEAD_SIZE), cosine_table, sine_table
    ).reshape(row_total, key_value_columns)
    d_qkv = jnp.concatenate([d_query_plain, key_grad_unrotated, d_value_own], axis=1).astype(
        jnp.bfloat16
    )
    d_normed_one = times_trans(d_qkv, qkv_weight)
    d_input_norm, gain_one_term = rms_backward(
        d_normed_one, scaled_one, rstd_one, gain_one.astype(jnp.float32)
    )
    input_grad = (d_mid + d_input_norm).astype(jnp.bfloat16)
    d_qkv_rows, d_branch_rows = side_by_side((d_qkv, d_branch), "shard", 0, 1)
    grad_attn = jnp.concatenate(
        [trans_times(normed_one_cols, d_qkv_rows), trans_times(attended_cols, d_branch_rows)],
        axis=1,
    )
    gain_grad_one, gain_grad_two = (
        sent_and_summed(gain_one_term, "shard", 0),
        sent_and_summed(gain_two_term, "shard", 0),
    )
    grad_attn, grad_gate_up, grad_down, gain_grad_one, gain_grad_two = (
        lax.psum(grad_attn.astype(jnp.bfloat16), "rep").astype(jnp.float32),
        lax.psum(grad_gate_up.astype(jnp.bfloat16), "rep").astype(jnp.float32),
        lax.psum(grad_down.astype(jnp.bfloat16), "rep").astype(jnp.float32),
        lax.psum(gain_grad_one.astype(jnp.bfloat16), "rep").astype(jnp.float32),
        lax.psum(gain_grad_two.astype(jnp.bfloat16), "rep").astype(jnp.float32),
    )
    grad_qkv = grad_attn[:, :qkv_cols]
    grad_out = grad_attn[:, qkv_cols:]
    return (
        mixed.astype(jnp.bfloat16),
        input_grad,
        gain_grad_one,
        grad_qkv,
        grad_out,
        gain_grad_two,
        grad_gate_up,
        grad_down,
    )


def solution(mesh):
    in_specs = (
        P(("rep", "shard"), None),
        P(("rep", "shard"), None),
        P(("rep", "shard")),
        P("shard"),
        P("shard", None),
        P("shard", None),
        P("shard"),
        P("shard", None),
        P("shard", None),
    )
    out_specs = (
        P(("rep", "shard"), None),
        P(("rep", "shard"), None),
        P("shard"),
        P("shard", None),
        P("shard", None),
        P("shard"),
        P("shard", None),
        P("shard", None),
    )
    return jax.shard_map(body, mesh=mesh, in_specs=in_specs, out_specs=out_specs, check_vma=False)
```

profile of v0, /device:TPU:1, one launch (start us, length us, event | category | flops | bytes accessed | tf_op | source)
XLA Modules:
  0.0 1391.8 jit_solution(5973786819356722361)
XLA Ops:
  13.7 124.2 %all-gather.8.cloned.1.call-done = bf16[2048,4609]{1,0:T(8,128)(2,1)} async-done(((bf16[128,4609]{1,0:T(8,128)(2,1)}), bf16[2048,4609]{1,0:T(8,128)(2,1)}) %all-gather.8.cloned.1.call-update) | async-done | bytes 18878480 | tf_op jit(solution)/shard_map/all_gather | solution.py:23
  139.2 7.5 fusion.71
  149.8 19.7 %all-gather = bf16[16,1,128]{2,1,0:T(2,128)(2,1)S(1)} all-gather(bf16[1,1,128]{2,1,0:T(2,128)(2,1)S(1)} %bitcast.209), channel_id=1, replica_groups=mesh['rep'=8,'shard'=16] {'shard'}, dimensions={0}, use_global_device_ids=true | all-gather | bytes 4352 | tf_op jit(solution)/shard_map/all_gather | solution.py:220
  170.3 23.6 %all-gather.10.cloned.1.call-done = bf16[2048,512]{1,0:T(8,128)(2,1)} async-done(((bf16[128,512]{1,0:T(8,128)(2,1)}), bf16[2048,512]{1,0:T(8,128)(2,1)}) %all-gather.10.cloned.1.call-update) | async-done | bytes 2097168 | tf_op jit(solution)/shard_map/all_gather | solution.py:36
  206.3 17.3 %while.57 = (s32[]{:T(128)}, f32[4,8,128]{2,1,0:T(8,128)S(1)}, f32[4,8,128]{2,1,0:T(8,128)S(1)}, s32[4]{0:T(128)S(1)}, s32[]{:T(128)}, /*index=5*/s32[]{:T(128)}...) while((s32[]{:T(128)}, f32[4,8,128]{2,1,0:T(8,128)S(1)}, ...), condition=%wide.region_7.8_spmd.clone, body=%wide.region_2.7_spmd.clone.sunk | while | flops 285418112 | bytes 17980204 | solution.py:191
  223.7 17.2 %while.58 = (s32[]{:T(128)}, f32[128,4,8,64]{0,3,2,1:T(8,128)S(1)}, s32[4]{0:T(128)S(1)}, s32[]{:T(128)}, s32[]{:T(128)}, /*index=5*/s32[128]{0:T(128)S(1)}, bf1...) while((s32[]{:T(128)}, f32[128,4,8,64]{0,3,2,1:T(8,128)S(1)}, ...), condition=%wide.region_11.12_spmd.clone, body=%wide.region_8.11_spmd.clone.sunk | while | flops 545718912 | bytes 3301143 | solution.py:211
  241.9 7.3 multiply_reduce_fusion.3
  249.2 191.6 %all-gather.12.cloned.1.call-done = bf16[2048,11264]{1,0:T(8,128)(2,1)} async-done(((bf16[128,11264]{1,0:T(8,128)(2,1)}), bf16[2048,11264]{1,0:T(8,128)(2,1)}) %all-gather.12.cloned.1.call-update) | async-done | bytes 46137360 | tf_op jit(solution)/shard_map/all_gather | solution.py:221
  440.9 21.3 %fusion.128 = f32[128,11264]{1,0:T(8,128)} fusion(bf16[2048,11264]{1,0:T(8,128)(2,1)} %all-gather.12.cloned.1.call-done, f32[128,2048]{1,0:T(8,128)S(1)} %get-tuple-element.1396, f32[2048]{0:T(1024)S(1)} %bitcast.200, f32[128]{0:T(128)S(1)} %add_rsqrt_fusion), kind=kOutput, calls=%fused_computation.168 | convolution fusion | flops 5906366464 | bytes 52961792 | tf_op jit(solution)/shard_map/dot_general | solution.py:226
  462.2 117.6 %all-gather.14.cloned.1.call-done = bf16[5632,2048]{1,0:T(8,128)(2,1)} async-done(((bf16[352,2048]{1,0:T(8,128)(2,1)}), bf16[5632,2048]{1,0:T(8,128)(2,1)}) %all-gather.14.cloned.1.call-update) | async-done | bytes 23068688 | tf_op jit(solution)/shard_map/all_gather | solution.py:222
  579.8 14.7 %multiply_convert_fusion.1 = (bf16[128,5632]{1,0:T(8,128)(2,1)}, bf16[128,5632]{1,0:T(8,128)(2,1)}, bf16[128,5632]{1,0:T(8,128)(2,1)}) fusion(f32[128,11264]{1,0:T(8,128)} %fusion.128, bf16[128,2048]{1,0:T(8,128)(2,1)S(1)} %copy-done.6, bf16[5632,2048]{1,0:T(8,128)(2,1)} %all-gather.14.cloned.1.call-done), kind=kOutput, calls=%fused_computation.90 | convolution fusion | flops 2963603456 | bytes 33685504 | tf_op jit(solution)/shard_map/dot_general | solution.py:98
  594.5 22.6 %multiply_reduce_fusion = (f32[2048]{0:T(1024)}, f32[128]{0:T(128)S(1)}, f32[128,2048]{1,0:T(8,128)S(1)}) fusion(f32[128,2048]{1,0:T(8,128)S(1)} %get-tuple-element.1396, f32[128]{0:T(128)S(1)} %add_rsqrt_fusion, f32[2048]{0:T(1024)S(1)} %bitcast.201, bf16[2048,11264]{1,0:T(8,128)(2,1)} %all-gather.12.cloned.1.call-done, ...), kind=kOutput, calls=%fused_computation.125 | convolution fusion | flops 5912918016 | bytes 51135488 | tf_op jit(solution)/shard_map/dot_general | solution.py:98
  618.2 7.0 fusion.95
  627.8 29.3 %while.59 = (s32[]{:T(128)}, f32[128,4,8,64]{0,3,2,1:T(8,128)S(1)}, bf16[4,512,4,64]{1,3,2,0:T(8,128)(2,1)}, bf16[4,512,4,64]{1,3,2,0:T(8,128)(2,1)}, s32[4]{0:T...) while((s32[]{:T(128)}, f32[128,4,8,64]{0,3,2,1:T(8,128)S(1)}, ...), condition=%wide.region_18.19_spmd.clone, body=%wide.region_15.18_spmd.clone.sunk | while | flops 1364132480 | bytes 44557144 | solution.py:299
  631.1 12.7 conditional.11
  661.2 4.3 reshape.173
  669.5 4.5 reshape.172
  688.1 93.2 %reduce-scatter.2.cloned.1.call-done = bf16[128,512]{1,0:T(8,128)(2,1)} async-done(((bf16[2048,512]{1,0:T(8,128)(2,1)}), bf16[128,512]{1,0:T(8,128)(2,1)}) %reduce-scatter.2.cloned.1.call-update) | async-done | bytes 131088 | tf_op jit(solution)/shard_map/reduce_scatter | solution.py:46
  794.7 20.7 %all_to_all.91 = bf16[128,16,128]{0,2,1:T(8,128)(2,1)} all-to-all(bf16[128,16,128]{0,2,1:T(8,128)(2,1)S(1)} %bitcast.188), channel_id=1, replica_groups=mesh['rep'=8,'shard'=16] {'shard'}, dimensions={1} | all-to-all | bytes 1048576 | tf_op jit(solution)/shard_map/all_to_all | solution.py:236
  819.0 9.6 fusion.114
  831.2 5.5 all-to-all-start.1
  837.7 81.4 %all-gather.16.cloned.1.call-done = bf16[2048,4608]{1,0:T(8,128)(2,1)} async-done(((bf16[128,4608]{1,0:T(8,128)(2,1)}), bf16[2048,4608]{1,0:T(8,128)(2,1)}) %all-gather.16.cloned.1.call-update) | async-done | bytes 18874384 | tf_op jit(solution)/shard_map/all_gather | solution.py:36
  919.1 4.8 fusion.98
  928.7 7.6 fusion.81
  940.6 5.6 all-to-all-start.5
  946.2 274.4 %all-gather.18.cloned.1.call-done = bf16[2048,13312]{1,0:T(8,128)(2,1)} async-done(((bf16[128,13312]{1,0:T(8,128)(2,1)}), bf16[2048,13312]{1,0:T(8,128)(2,1)}) %all-gather.18.cloned.1.call-update) | async-done | bytes 54525968 | tf_op jit(solution)/shard_map/all_gather | solution.py:36
  1220.7 18.4 %fusion.64 = bf16[128,11264]{1,0:T(8,128)(2,1)} fusion(bf16[2048,128]{1,0:T(8,128)(2,1)S(1)} %bitcast.194, bf16[2048,13312]{1,0:T(8,128)(2,1)} %all-gather.18.cloned.1.call-done), kind=kOutput, calls=%fused_computation.68 | convolution fusion | flops 5907021824 | bytes 49545216 | tf_op jit(solution)/shard_map/dot_general | solution.py:104
  1239.1 8.1 fusion.89
  1247.9 9.7 all_to_all.92
  1261.5 11.7 fusion.101
  1273.3 17.9 %all-reduce = (bf16[128]{0:T(256)(128)(2,1)S(1)}, bf16[128]{0:T(256)(128)(2,1)S(1)}) all-reduce(bf16[128]{0:T(256)(128)(2,1)S(1)} %reduce_sum.97, bf16[128]{0:T(256)(128)(2,1)S(1)} %reduce_sum.99), channel_id=1, replica_groups=mesh['rep'=8,'shard'=16] {'rep'}, use_global_device_ids=true, to_apply=%region_23.24 | all-reduce | flops 256 | bytes 1024 | tf_op jit(solution)/shard_map/psum | solution.py:341
  1292.2 82.9 %all-reduce.4.cloned.1.call-done = (bf16[128,4608]{1,0:T(8,128)(2,1)}, bf16[128,11264]{1,0:T(8,128)(2,1)}, bf16[352,2048]{1,0:T(8,128)(2,1)}) async-done(((bf16[128,4608]{1,0:T(8,128)(2,1)}, bf16[128,11264]{1,0:T(8,128)(2,1)}, bf16[352,2048]{1,0:T(8,128)(2,1)}), (bf16[128,4608]{1,0:T(8,128)(2,1)}, bf16[128,11264]{1,0:T(8,128)(2,1)}, bf16[352,2048]{1,0:T(8,128)(2,1)})) %all-reduce.4.cloned.1.call-update) | async-done | bytes 5505040 | tf_op jit(solution)/shard_map/psum | solution.py:338
  (235 shorter events, 136.1 us)
Async XLA Ops:
  7.2 130.8 %all-gather.8.cloned.1.call-start = ((), (), s32[]{:S(2)}) async-start(), calls=%async_computation.7 | async-start | bytes 20611072 | tf_op jit(solution)/shard_map/all_gather | solution.py:23
  11.8 182.1 %all-gather.10.cloned.1.call-start = ((), (), s32[]{:S(2)}) async-start(), calls=%async_computation.8 | async-start | bytes 2228224 | tf_op jit(solution)/shard_map/all_gather | solution.py:36
  13.4 156.7 %copy-start.17 = (f32[128,64]{0,1:T(8,128)}, f32[128,64]{0,1:T(8,128)S(1)}, u32[]{:S(2)}) copy-start(f32[128,64]{0,1:T(8,128)S(1)} %get-tuple-element.1400) | copy-start | bytes 98308
  13.4 156.7 %copy-start.19 = (f32[128,64]{0,1:T(8,128)}, f32[128,64]{0,1:T(8,128)S(1)}, u32[]{:S(2)}) copy-start(f32[128,64]{0,1:T(8,128)S(1)} %get-tuple-element.1399) | copy-start | bytes 98308
  13.5 133.5 %copy-start.16 = (f32[128,256]{1,0:T(8,128)}, f32[128,256]{1,0:T(8,128)S(1)}, u32[]{:S(2)}) copy-start(f32[128,256]{1,0:T(8,128)S(1)} %copy.175) | copy-start | bytes 393220
  13.7 133.0 %copy-start.32 = (f32[128]{0:T(128)}, f32[128]{0:T(128)S(1)}, u32[]{:S(2)}) copy-start(f32[128]{0:T(128)S(1)} %add_rsqrt_fusion.1) | copy-start | bytes 1540
  147.7 293.1 %all-gather.12.cloned.1.call-start = ((), (), s32[]{:S(2)}) async-start(), calls=%async_computation.9 | async-start | bytes 49020928 | tf_op jit(solution)/shard_map/all_gather | solution.py:221
  148.5 431.3 %all-gather.14.cloned.1.call-start = ((), (), s32[]{:S(2)}) async-start(), calls=%async_computation.10 | async-start | bytes 24510464 | tf_op jit(solution)/shard_map/all_gather | solution.py:222
  149.1 632.2 %reduce-scatter.2.cloned.1.call-start = ((), (), s32[]{:S(2)}) async-start(), calls=%async_computation.11 | async-start | bytes 2228224 | tf_op jit(solution)/shard_map/reduce_scatter | solution.py:46
  197.4 8.9 copy-start.23
  240.9 8.3 copy-start.3
  249.2 367.8 %copy-start.27 = (f32[128]{0:T(128)}, f32[128]{0:T(128)S(1)}, u32[]{:S(2)}) copy-start(f32[128]{0:T(128)S(1)} %add_rsqrt_fusion) | copy-start | bytes 1540
  440.9 138.9 %copy-start.6 = (bf16[128,2048]{1,0:T(8,128)(2,1)S(1)}, bf16[128,2048]{1,0:T(8,128)(2,1)}, u32[]{:S(2)}) copy-start(bf16[128,2048]{1,0:T(8,128)(2,1)} %param.22) | copy-start | bytes 1572868
  617.1 8.1 copy-start.1
  617.1 8.1 copy-start.29
  677.1 242.0 %all-gather.16.cloned.1.call-start = ((), (), s32[]{:S(2)}) async-start(), calls=%async_computation.12 | async-start | bytes 20054016 | tf_op jit(solution)/shard_map/all_gather | solution.py:36
  685.9 105.7 %copy-start.5 = (bf16[128,5632]{1,0:T(8,128)(2,1)S(1)}, bf16[128,5632]{1,0:T(8,128)(2,1)}, u32[]{:S(2)}) copy-start(bf16[128,5632]{1,0:T(8,128)(2,1)} %get-tuple-element.1373) | copy-start | bytes 4325380
  685.9 105.7 %copy-start.7 = (bf16[128,2048]{1,0:T(8,128)(2,1)S(1)}, bf16[128,2048]{1,0:T(8,128)(2,1)}, u32[]{:S(2)}) copy-start(bf16[128,2048]{1,0:T(8,128)(2,1)} %param.22) | copy-start | bytes 1572868
  688.1 103.4 %copy-start.11 = (bf16[128,2048]{1,0:T(8,128)(2,1)}, bf16[128,2048]{1,0:T(8,128)(2,1)S(1)}, u32[]{:S(2)}) copy-start(bf16[128,2048]{1,0:T(8,128)(2,1)S(1)} %add_convert_fusion) | copy-start | bytes 1572868
  791.5 429.1 %all-gather.18.cloned.1.call-start = ((), (), s32[]{:S(2)}) async-start(), calls=%async_computation.13 | async-start | bytes 57933824 | tf_op jit(solution)/shard_map/all_gather | solution.py:36
  794.6 22.8 %copy-start.4 = (bf16[128,5632]{1,0:T(8,128)(2,1)S(1)}, bf16[128,5632]{1,0:T(8,128)(2,1)}, u32[]{:S(2)}) copy-start(bf16[128,5632]{1,0:T(8,128)(2,1)} %get-tuple-element.1375) | copy-start | bytes 4325380
  794.6 24.3 %copy-start.25 = (f32[2048]{0:T(1024)S(1)}, f32[2048]{0:T(1024)}, u32[]{:S(2)}) copy-start(f32[2048]{0:T(1024)} %copy-done.24) | copy-start | bytes 24580
  818.9 9.7 copy-start.2
  818.9 9.7 copy-start.14
  819.0 9.7 copy-start.28
  819.0 9.7 copy-start.30
  819.0 9.7 copy-start.33
  831.2 92.8 %all-to-all-start.1 = ((bf16[128,16,128]{2,0,1:T(8,128)(2,1)}), bf16[128,16,128]{2,0,1:T(8,128)(2,1)S(1)}, u32[]{:S(2)}, u32[]{:S(2)}) async-start(bf16[128,16,128]{2,0,1:T(8,128)(2,1)} %bitcast.174), calls=%async_computation.2 | async-start | bytes 1048576 | tf_op jit(solution)/shard_map/all_to_all | solution.py:235
  924.8 15.8 %all-to-all-start.4 = ((bf16[128,16,128]{2,0,1:T(8,128)(2,1)}), bf16[128,16,128]{2,0,1:T(8,128)(2,1)S(1)}, u32[]{:S(2)}, u32[]{:S(2)}) async-start(bf16[128,16,128]{2,0,1:T(8,128)(2,1)} %bitcast.173), calls=%async_computation.5 | async-start | bytes 1048576 | tf_op jit(solution)/shard_map/all_to_all | solution.py:237
  940.6 298.5 %all-to-all-start.5 = ((bf16[128,16,352]{0,2,1:T(8,128)(2,1)}), bf16[128,16,352]{0,2,1:T(8,128)(2,1)}, u32[]{:S(2)}, u32[]{:S(2)}) async-start(bf16[128,16,352]{0,2,1:T(8,128)(2,1)} %bitcast.184), calls=%async_computation.6 | async-start | bytes 2883584 | tf_op jit(solution)/shard_map/all_to_all | solution.py:238
  946.2 428.9 %all-reduce.4.cloned.1.call-start = ((), (), s32[]{:S(2)}) async-start(), calls=%async_computation.14 | async-start | bytes 11010048 | tf_op jit(solution)/shard_map/psum | solution.py:338
  1257.6 15.7 %all-to-all-start = ((f32[16,1,128]{2,1,0:T(1,128)}), f32[16,1,128]{2,1,0:T(1,128)S(1)}, u32[]{:S(2)}, u32[]{:S(2)}) async-start(f32[16,1,128]{2,1,0:T(1,128)} %bitcast.49), calls=%async_computation.1 | async-start | bytes 16384 | tf_op jit(solution)/shard_map/all_to_all | solution.py:57
  (14 other events, 53.2 us)
Sparse Core Ops, SparseCore 0:
  11.9 126.0 all-gather.7
  147.9 45.9 all-gather.9
  196.4 244.4 all-gather.11
  443.2 136.5 all-gather.13
  677.2 104.0 reduce-scatter.1
  791.7 127.4 all-gather.15
  922.2 298.4 all-gather.17
  1247.3 127.7 all-reduce.3
where the time goes:
time: 1400 us; the launch traced here: 1390 us
  waiting for transfers between devices  994 us (71%)
  matrix products  157 us (11%)
  local copies, waits for them, and re-layouts  71.8 us (5%)
  blocking collectives  68 us (5%)
  other arithmetic  35 us (2%)
  loops' own time  31.9 us (2%)
  starting transfers between devices  19.3 us (1%)
  between operations  15 us (1%)
    all_gather x3, waiting for transfers between devices, side_by_side(): lax.all_gather(both, axis, axis=dim, tiled=True)  379 us
    all_gather x1, waiting for transfers between devices, body(): lax.all_gather(w_gate_up, 'shard', axis=0, tiled=True)  192 us
    all_gather x1, waiting for transfers between devices, in_one_piece(): filled = lax.all_gather(both, axis, axis=dim, tiled=True)  124 us
    all_gather x1, waiting for transfers between devices, body(): lax.all_gather(w_down, 'shard', axis=0, tiled=True)  118 us
    reduce_scatter x1, waiting for transfers between devices, in_one_piece_2(): lax.psum_scatter(both, axis, scatter_dimension=dim, tiled=True)  93.2 us
    psum x1, waiting for transfers between devices, body(): lax.psum(grad_attn.astype(jnp.bfloat16), 'rep').astype(jnp.float32)  82.9 us
    dot_general x4, matrix products, times_trans(): lax.dot_general(left, right, (((1,), (1,)), ((), ())), preferred_element_...  53.9 us
    dot_general x4, matrix products, trans_times(): lax.dot_general(left, right, (((0,), (0,)), ((), ())), preferred_element_...  38.9 us
  transfers between devices with their start and end apart: 12, of which 9 were waited for; matrix products, arithmetic and copies ran while one was open for 10% of the time, Pallas kernels for 0%

commit v1 on v0

v1 whole, which is shorter than its diff:
```python
import math

import jax
import jax.numpy as jnp
from jax import lax
from jax.experimental import pallas as pl
from jax.experimental.pallas import tpu as pltpu
from jax.sharding import Mesh
from jax.sharding import PartitionSpec as P

QUERY_HEADS = 32
KEY_VALUE_HEADS = 4
HEAD_SIZE = 64
GROUP = QUERY_HEADS // KEY_VALUE_HEADS
EPS = 1e-05
ROPE_BASE = 10000.0
NEG = -1e30
BLOCK = 128
CHUNK = 2 * BLOCK
SCALE = 1.0 / math.sqrt(HEAD_SIZE)

AXES = ("zlo", "y", "zhi", "x", "core")
REP = ("zlo", "y")
SHARD = ("zhi", "x", "core")
CHIP = ("zhi", "x")
YZ = ("zlo", "y", "zhi")
YZC = ("zlo", "y", "zhi", "core")
NX = 4

F32 = jnp.float32
BF16 = jnp.bfloat16


def exchange(a, axes):
    return lax.all_to_all(a, axes, split_axis=0, concat_axis=0, tiled=True)


def everywhere(a, axes, n):
    return exchange(jnp.broadcast_to(a[None], (n,) + a.shape), axes)


def swap(a, axis):
    return lax.ppermute(a, axis, [(0, 1), (1, 0)])


def in_order(coord, mine, other, axis):
    return jnp.where(
        coord == 0, jnp.stack([mine, other], axis=axis), jnp.stack([other, mine], axis=axis)
    )


def mm(left, right, dims, out=F32):
    return lax.dot_general(
        left, right, ((dims[0], dims[1]), ((), ())), preferred_element_type=F32
    ).astype(out)


def rms_forward(rows):
    rstd = lax.rsqrt(jnp.mean(rows * rows, axis=1, keepdims=True) + EPS)
    return rows * rstd, rstd


def rms_backward(d_normed, scaled, rstd, gain):
    gain_term = jnp.sum(d_normed * scaled, axis=0)
    inner = d_normed * gain[None, :]
    d_values = rstd * (inner - scaled * jnp.mean(inner * scaled, axis=1, keepdims=True))
    return d_values, gain_term


def heads_to_lanes(ref):
    return jnp.concatenate(
        [ref[HEAD_SIZE * h : HEAD_SIZE * (h + 1), :] for h in range(GROUP)], axis=1
    )


def chunk_slots(c, zhi, core):
    base = ((c // 4) ^ zhi) * 8 + c % 4
    return base + 4 * core, base + 4 * (1 - core)


def allowed_mask(c, st, block):
    keys = lax.broadcasted_iota(jnp.int32, (CHUNK, 1), 0) + c * CHUNK
    lanes = lax.broadcasted_iota(jnp.int32, (1, GROUP * BLOCK), 1) % BLOCK
    return (keys >= st) & (keys <= block * BLOCK + lanes)


def attention_forward(sc, q_ref, cos_ref, sin_ref, st_ref, kv_ref, o_ref, ob_ref, qr_ref, lse_ref):
    b = pl.program_id(0)
    zhi, core, first = sc[0], sc[1], sc[2 + b]
    block = zhi * 8 + 2 * b + core
    cos, sin = cos_ref[...], sin_ref[...]
    turned = []
    for h in range(GROUP):
        u1 = q_ref[HEAD_SIZE * h : HEAD_SIZE * h + 32, :]
        u2 = q_ref[HEAD_SIZE * h + 32 : HEAD_SIZE * h + 64, :]
        turned.append(jnp.concatenate([u1 * cos - u2 * sin, u2 * cos + u1 * sin], axis=0))
    q = jnp.concatenate(turned, axis=1).astype(BF16) * jnp.asarray(SCALE, BF16)
    qr_ref[0] = q
    st = jnp.concatenate([st_ref[0]] * GROUP, axis=1)

    def step(c, state):
        m, l, acc = state
        s0, s1 = chunk_slots(c, zhi, core)
        k = jnp.concatenate([kv_ref[s0, :HEAD_SIZE, :], kv_ref[s1, :HEAD_SIZE, :]], axis=1)
        v = jnp.concatenate([kv_ref[s0, HEAD_SIZE:, :], kv_ref[s1, HEAD_SIZE:, :]], axis=1)
        s = lax.dot_general(k, q, (((0,), (0,)), ((), ())), preferred_element_type=F32)
        s = jnp.where(allowed_mask(c, st, block), s, NEG)
        m2 = jnp.maximum(m, jnp.max(s, axis=0, keepdims=True))
        p = jnp.exp(s - m2)
        al = jnp.exp(m - m2)
        l = l * al + jnp.sum(p, axis=0, keepdims=True)
        acc = acc * al + lax.dot_general(
            v, p.astype(BF16), (((1,), (0,)), ((), ())), preferred_element_type=F32
        )
        return m2, l, acc

    rows = GROUP * BLOCK
    m, l, acc = lax.fori_loop(
        first,
        block // 2 + 1,
        step,
        (
            jnp.full((1, rows), NEG, F32),
            jnp.zeros((1, rows), F32),
            jnp.zeros((HEAD_SIZE, rows), F32),
        ),
    )
    o = acc / l
    for h in range(GROUP):
        part = o[:, BLOCK * h : BLOCK * (h + 1)]
        o_ref[HEAD_SIZE * h : HEAD_SIZE * (h + 1), :] = part
        ob_ref[HEAD_SIZE * h : HEAD_SIZE * (h + 1), :] = part.astype(BF16)
    lse_ref[0] = m + jnp.log(l)


def attention_backward(
    sc, qr_ref, do_ref, o_ref, lse_ref, cos_ref, sin_ref, st_ref, kv_ref, dq_ref, dkv_ref, acc_ref
):
    b = pl.program_id(0)
    zhi, core, first = sc[0], sc[1], sc[2 + b]
    block = zhi * 8 + 2 * b + core

    @pl.when(b == 0)
    def _():
        acc_ref[...] = jnp.zeros_like(acc_ref)

    q = qr_ref[0]
    do = heads_to_lanes(do_ref)
    delta = jnp.sum(do.astype(F32) * heads_to_lanes(o_ref), axis=0, keepdims=True)
    q_rows = q.T
    do_rows = do.T
    lse = lse_ref[0]
    st = jnp.concatenate([st_ref[0]] * GROUP, axis=1)

    def step(c, dq):
        s0, s1 = chunk_slots(c, zhi, core)
        k = jnp.concatenate([kv_ref[s0, :HEAD_SIZE, :], kv_ref[s1, :HEAD_SIZE, :]], axis=1)
        v = jnp.concatenate([kv_ref[s0, HEAD_SIZE:, :], kv_ref[s1, HEAD_SIZE:, :]], axis=1)
        s = lax.dot_general(k, q, (((0,), (0,)), ((), ())), preferred_element_type=F32)
        p = jnp.exp(jnp.where(allowed_mask(c, st, block), s, NEG) - lse)
        dp = lax.dot_general(v, do, (((0,), (0,)), ((), ())), preferred_element_type=F32)
        ds = (p * (dp - delta)).astype(BF16)
        pb = p.astype(BF16)
        dk = jnp.dot(ds, q_rows, preferred_element_type=F32)
        dv = jnp.dot(pb, do_rows, preferred_element_type=F32)
        both = jnp.concatenate([dk, dv], axis=1)
        acc_ref[s0] += both[:BLOCK]
        acc_ref[s1] += both[BLOCK:]
        return dq + jnp.dot(k, ds, preferred_element_type=F32)

    dq = lax.fori_loop(
        first, block // 2 + 1, step, jnp.zeros((HEAD_SIZE, GROUP * BLOCK), F32)
    )
    dq = dq * SCALE
    cos, sin = cos_ref[...], sin_ref[...]
    for h in range(GROUP):
        g1 = dq[:32, BLOCK * h : BLOCK * (h + 1)]
        g2 = dq[32:, BLOCK * h : BLOCK * (h + 1)]
        dq_ref[HEAD_SIZE * h : HEAD_SIZE * h + 32, :] = (g1 * cos + g2 * sin).astype(BF16)
        dq_ref[HEAD_SIZE * h + 32 : HEAD_SIZE * h + 64, :] = (g2 * cos - g1 * sin).astype(BF16)

    @pl.when(b == NX - 1)
    def _():
        for n in range(16):
            dkv_ref[n] = acc_ref[n].T.astype(BF16)


VMEM_LIMIT = 48 * 1024 * 1024


def call_forward(sc, qkv_t, cos, sin, st, kv):
    rows, toks = GROUP * HEAD_SIZE, NX * BLOCK
    lanes = GROUP * BLOCK
    tile = pl.BlockSpec((rows, BLOCK), lambda b, s: (0, b))
    trig = pl.BlockSpec((32, BLOCK), lambda b, s: (0, b))
    return pl.pallas_call(
        attention_forward,
        grid_spec=pltpu.PrefetchScalarGridSpec(
            num_scalar_prefetch=1,
            grid=(NX,),
            in_specs=[
                tile,
                trig,
                trig,
                pl.BlockSpec((1, 1, BLOCK), lambda b, s: (b, 0, 0)),
                pl.BlockSpec((16, BLOCK, BLOCK), lambda b, s: (0, 0, 0)),
            ],
            out_specs=[
                tile,
                tile,
                pl.BlockSpec((1, HEAD_SIZE, lanes), lambda b, s: (b, 0, 0)),
                pl.BlockSpec((1, 1, lanes), lambda b, s: (b, 0, 0)),
            ],
        ),
        out_shape=[
            jax.ShapeDtypeStruct((rows, toks), F32),
            jax.ShapeDtypeStruct((rows, toks), BF16),
            jax.ShapeDtypeStruct((NX, HEAD_SIZE, lanes), BF16),
            jax.ShapeDtypeStruct((NX, 1, lanes), F32),
        ],
        compiler_params=pltpu.CompilerParams(
            dimension_semantics=("arbitrary",), vmem_limit_bytes=VMEM_LIMIT
        ),
        cost_estimate=pl.CostEstimate(
            flops=4 * 512 * 1024 * 512, bytes_accessed=8 << 20, transcendentals=8 << 20
        ),
        name="attention_forward",
    )(sc, qkv_t, cos, sin, st, kv)


def call_backward(sc, qr, do, o, lse, cos, sin, st, kv):
    rows, toks = GROUP * HEAD_SIZE, NX * BLOCK
    lanes = GROUP * BLOCK
    tile = pl.BlockSpec((rows, BLOCK), lambda b, s: (0, b))
    trig = pl.BlockSpec((32, BLOCK), lambda b, s: (0, b))
    whole = pl.BlockSpec((16, BLOCK, BLOCK), lambda b, s: (0, 0, 0))
    return pl.pallas_call(
        attention_backward,
        grid_spec=pltpu.PrefetchScalarGridSpec(
            num_scalar_prefetch=1,
            grid=(NX,),
            in_specs=[
                pl.BlockSpec((1, HEAD_SIZE, lanes), lambda b, s: (b, 0, 0)),
                tile,
                tile,
                pl.BlockSpec((1, 1, lanes), lambda b, s: (b, 0, 0)),
                trig,
                trig,
                pl.BlockSpec((1, 1, BLOCK), lambda b, s: (b, 0, 0)),
                whole,
            ],
            out_specs=[tile, whole],
            scratch_shapes=[pltpu.VMEM((16, BLOCK, BLOCK), F32)],
        ),
        out_shape=[
            jax.ShapeDtypeStruct((rows, toks), BF16),
            jax.ShapeDtypeStruct((16, BLOCK, BLOCK), BF16),
        ],
        compiler_params=pltpu.CompilerParams(
            dimension_semantics=("arbitrary",), vmem_limit_bytes=VMEM_LIMIT
        ),
        cost_estimate=pl.CostEstimate(
            flops=10 * 512 * 1024 * 512, bytes_accessed=8 << 20, transcendentals=8 << 20
        ),
        name="attention_backward",
    )(sc, qr, do, o, lse, cos, sin, st, kv)


def summed_x(part):
    rows = part.shape[0] // NX
    return exchange(part.reshape(NX, rows, -1), "x").astype(F32).sum(axis=0)


def gathered_x(a):
    full = everywhere(a, "x", NX)
    return full.reshape(NX * a.shape[0], *a.shape[1:])


def body(tok, cot, starts, gain_1, w_qkv, w_out, gain_2, w_gu, w_dn):
    zlo, y, zhi, x, core = (lax.axis_index(a) for a in AXES)
    replica = zlo * 4 + y
    rows, dim = tok.shape
    q_cols = GROUP * HEAD_SIZE
    ff_shard = w_dn.shape[0]
    ff = 4 * ff_shard
    slab = rows // 8

    wide = jnp.concatenate(
        [
            w_qkv[:, :dim].reshape(rows, NX, q_cols),
            w_qkv[:, dim : dim + 256].reshape(rows, NX, HEAD_SIZE),
            w_qkv[:, dim + 256 :].reshape(rows, NX, HEAD_SIZE),
        ],
        axis=2,
    ).transpose(1, 0, 2)
    qkv_cols = wide.shape[2]
    wide = jnp.broadcast_to(wide[None], (2,) + wide.shape).reshape(8, rows, qkv_cols)
    wide = exchange(wide, CHIP)
    toks = gathered_x(tok)
    gains = everywhere(jnp.stack([gain_1, gain_2]), SHARD, 16)
    st = gathered_x(starts).reshape(NX, 1, rows)
    wq = in_order(core, wide, swap(wide, "core"), 1).reshape(dim, qkv_cols)
    gain_one = gains[:, 0].reshape(dim).astype(F32)
    gain_two = gains[:, 1].reshape(dim).astype(F32)

    def to_heads(first):
        pairs = []
        for s_zhi in range(2):
            for s_x in range(NX):
                d_zhi = s_x % 2 if first else 1 - s_x % 2
                pairs.append((s_zhi * NX + s_x, d_zhi * NX + 2 * s_zhi + s_x // 2))
        return pairs

    part_a = lax.ppermute(w_out, CHIP, to_heads(True))
    part_b = lax.ppermute(w_out, CHIP, to_heads(False))
    wo = in_order(zhi, part_a, part_b, 0)
    wo = in_order(core, wo, swap(wo, "core"), 1).reshape(q_cols, dim)

    gu_slab = lax.dynamic_slice_in_dim(w_gu, replica * slab, slab, axis=0)
    gu_slab = gu_slab.reshape(slab, 2, 2, NX, 2 * ff_shard).transpose(3, 0, 1, 2, 4)
    gu_slab = exchange(gu_slab.reshape(NX, slab, 2 * ff), "x").reshape(NX * slab, 2 * ff)
    dn_slab = lax.dynamic_slice_in_dim(w_dn, replica * 256, 256, axis=1)
    dn_slab = dn_slab.reshape(11, 32, 256).transpose(1, 0, 2).reshape(32, 2 * ff)
    ffn = lax.all_gather(jnp.concatenate([gu_slab, dn_slab]), YZC, axis=0)
    wgu = ffn[:, : NX * slab].reshape(2, 4, 2, 2, NX, slab, 2 * ff)
    wgu = wgu.transpose(2, 4, 3, 0, 1, 5, 6).reshape(dim, 2 * ff)
    wdn = ffn[:, NX * slab :].reshape(2, 4, 2, 2, 32, 11, 256)
    wdn = wdn.transpose(2, 3, 5, 4, 0, 1, 6).reshape(ff, dim)

    inputs = tok.astype(F32)
    scaled_one, rstd_one = rms_forward(inputs)
    all_scaled, _ = rms_forward(toks.astype(F32))
    n1 = (all_scaled * gain_one[None, :]).astype(BF16)
    qkv_t = mm(wq, n1, ((0,), (1,)))
    block_ids = zhi * 8 + 2 * jnp.arange(NX, dtype=jnp.int32) + core
    where_at = block_ids[:, None] * rows + jnp.arange(rows, dtype=jnp.int32)[None, :]
    pos = (where_at - st[:, 0]).reshape(1, NX * rows).astype(F32)
    freqs = jnp.exp(jnp.arange(32, dtype=F32) * (-2.0 * math.log(ROPE_BASE) / HEAD_SIZE))
    angles = freqs[:, None] * pos
    cos, sin = jnp.cos(angles), jnp.sin(angles)
    k1, k2 = qkv_t[q_cols : q_cols + 32], qkv_t[q_cols + 32 : q_cols + 64]
    kv = jnp.concatenate([k1 * cos - k2 * sin, k2 * cos + k1 * sin, qkv_t[q_cols + 64 :]], axis=0)
    kv = kv.astype(BF16).reshape(2 * HEAD_SIZE, NX, rows).transpose(1, 0, 2)
    kv = jnp.concatenate([kv, swap(kv, "core")], axis=0)
    kv = jnp.concatenate([kv, swap(kv, "zhi")], axis=0)
    firsts = jnp.min(st, axis=(1, 2)) // CHUNK
    sc = jnp.concatenate([zhi[None], core[None], firsts]).astype(jnp.int32)
    o, ob, qr, lse = call_forward(sc, qkv_t, cos, sin, st, kv)
    hidden = inputs + summed_x(mm(ob, wo, ((0,), (0,)), BF16))

    cots = gathered_x(cot)
    scaled_two, rstd_two = rms_forward(hidden)
    n2 = gathered_x((scaled_two * gain_two[None, :]).astype(BF16))
    d_act = mm(cots, wdn, ((1,), (1,)))
    gate_up = mm(n2, wgu, ((1,), (0,)))
    gate, up = gate_up[:, :ff], gate_up[:, ff:]
    sig = jax.nn.sigmoid(gate)
    silu = gate * sig
    act = (silu * up).astype(BF16)
    d_gate = d_act * up * (sig * (1.0 + gate * (1.0 - sig)))
    d_gu = jnp.concatenate([d_gate, d_act * silu], axis=1).astype(BF16)
    d_n2 = summed_x(mm(d_gu, wgu, ((1,), (1,)), BF16))
    mixed = hidden + summed_x(mm(act, wdn, ((1,), (0,)), BF16))

    g_gu = mm(n2, d_gu, ((0,), (0,)), BF16)
    g_dn = mm(act, cots, ((0,), (0,)), BF16)

    def over_tokens(t):
        t = exchange(t, "core").astype(F32).sum(axis=0).astype(BF16)
        return exchange(t, YZ).astype(F32).sum(axis=0).astype(BF16)

    g_gu = g_gu.reshape(2, NX, 2, 2, 4, slab, 2 * ff).transpose(2, 3, 4, 0, 1, 5, 6)
    g_gu = over_tokens(g_gu.reshape(2, 16, NX, slab, 2 * ff))
    g_dn = g_dn.reshape(2, 2, ff_shard, 2, 4, 256).transpose(1, 3, 4, 0, 2, 5)
    g_dn = over_tokens(g_dn.reshape(2, 16, ff_shard, 256))
    g_gu = exchange(g_gu, "x").reshape(NX, slab, 2, 2, 2 * ff_shard)
    g_gu = lax.all_gather(g_gu, REP, axis=0)
    g_gu = g_gu.transpose(0, 2, 3, 4, 1, 5).reshape(rows, w_gu.shape[1]).astype(F32)
    g_dn = lax.all_gather(g_dn, REP, axis=0)
    g_dn = g_dn.transpose(1, 0, 2).reshape(ff_shard, dim).astype(F32)

    d_mid, gain_two_term = rms_backward(d_n2, scaled_two, rstd_two, gain_two)
    d_mid = cot.astype(F32) + d_mid
    d_br = gathered_x(d_mid.astype(BF16))
    do = mm(wo, d_br, ((1,), (1,)), BF16)
    dq, dkv = call_backward(sc, qr, do, o, lse, cos, sin, st, kv)
    g_out = mm(ob, d_br, ((1,), (0,)), BF16)
    dkv = dkv.reshape(2, 2, NX, 2 * HEAD_SIZE, rows)
    dkv = dkv[:, 0].astype(F32) + swap(dkv[:, 1], "core").astype(F32)
    dkv = dkv[0] + swap(dkv[1].astype(BF16), "zhi").astype(F32)
    dkv = dkv.transpose(1, 0, 2).reshape(2 * HEAD_SIZE, NX * rows)
    k1, k2 = dkv[:32], dkv[32:64]
    dkv = jnp.concatenate([k1 * cos + k2 * sin, k2 * cos - k1 * sin, dkv[64:]], axis=0)
    d_qkv = jnp.concatenate([dq, dkv.astype(BF16)], axis=0)
    d_n1 = summed_x(mm(d_qkv, wq, ((0,), (1,)), BF16))
    g_qkv = mm(n1, d_qkv, ((0,), (1,)), BF16)
    d_in, gain_one_term = rms_backward(d_n1, scaled_one, rstd_one, gain_one)
    input_grad = (d_mid + d_in).astype(BF16)

    g_qkv = g_qkv.reshape(2, NX, 2, 2, 4, slab, qkv_cols).transpose(2, 3, 4, 0, 1, 5, 6)
    g_qkv = over_tokens(g_qkv.reshape(2, 16, NX, slab, qkv_cols))
    g_qkv = exchange(g_qkv, "x")
    g_qkv = everywhere(g_qkv, REP, 8).transpose(0, 2, 1, 3).reshape(rows, NX, qkv_cols)
    g_qkv = jnp.concatenate(
        [
            g_qkv[:, :, :q_cols].reshape(rows, dim),
            g_qkv[:, :, q_cols : q_cols + HEAD_SIZE].reshape(rows, 256),
            g_qkv[:, :, q_cols + HEAD_SIZE :].reshape(rows, 256),
        ],
        axis=1,
    ).astype(F32)
    g_out = g_out.reshape(2, 2, rows, 2, 4, 2, 128).transpose(1, 3, 4, 5, 0, 2, 6)
    g_out = over_tokens(g_out.reshape(2, 16, 2, rows, 128))

    def to_owners(first):
        return [(d, s) for s, d in to_heads(first)]

    same = jnp.where(zhi == 0, g_out[0], g_out[1])
    cross = jnp.where(zhi == 0, g_out[1], g_out[0])
    same = lax.ppermute(same, CHIP, to_owners(True))
    cross = lax.ppermute(cross, CHIP, to_owners(False))
    g_out = in_order(x % 2, same, cross, 1).reshape(rows, 256)
    g_out = everywhere(g_out, REP, 8).transpose(1, 0, 2).reshape(rows, dim).astype(F32)

    terms = jnp.stack([gain_one_term, gain_two_term]).reshape(2, 16, rows).transpose(1, 0, 2)
    terms = exchange(terms, SHARD).sum(axis=0)
    terms = everywhere(terms.astype(BF16), REP, 8).astype(F32).sum(axis=0)

    return (
        mixed.astype(BF16),
        input_grad,
        terms[0],
        g_qkv,
        g_out,
        terms[1],
        g_gu,
        g_dn,
    )


def solution(mesh):
    fine = Mesh(mesh.devices.reshape(2, 4, 2, 4, 2), AXES)
    row, two = P(AXES), P(AXES, None)
    vec, mat = P(SHARD), P(SHARD, None)
    return jax.shard_map(
        body,
        mesh=fine,
        in_specs=(two, two, row, vec, mat, mat, vec, mat, mat),
        out_specs=(two, two, vec, mat, mat, vec, mat, mat),
        check_vma=False,
    )
```

time: 1400 us -> 867 us (0.62)
  waiting for transfers between devices: 994 us -> 233 us
  starting transfers between devices: 19.3 us -> 166 us
  matrix products: 157 us -> 83.4 us
  blocking collectives: 68 us -> 139 us
  local copies, waits for them, and re-layouts: 71.8 us -> 132 us
  loops' own time: 31.9 us -> 0 us
  other arithmetic: 35 us -> 64.8 us
  Pallas kernels: 0 us -> 20 us
    all_gather x6 -> x3, waiting for transfers between devices: 813 us -> 0.02 us  [the longest x1 0.02 us: body(): ffn = lax.all_gather(jnp.concatenate([gu_slab, dn_slab]), YZC, axis=0)]
    all_to_all x4 -> x20, waiting for transfers between devices: 3.26 us -> 151 us  [exchange(): return lax.all_to_all(a, axes, split_axis=0, concat_axis=0, tiled=True)]
    all_to_all x2 -> x6, blocking collectives: 30.3 us -> 139 us  [exchange(): return lax.all_to_all(a, axes, split_axis=0, concat_axis=0, tiled=True)]
    all_to_all x4 -> x20, starting transfers between devices: 19 us -> 121 us  [exchange(): return lax.all_to_all(a, axes, split_axis=0, concat_axis=0, tiled=True)]
    reduce_scatter x1 -> x0, waiting for transfers between devices: 93.2 us -> none  [in_one_piece_2(): lax.psum_scatter(both, axis, scatter_dimension=dim, tiled=True)]
    psum x1 -> x0, waiting for transfers between devices: 82.9 us -> none  [body(): lax.psum(grad_attn.astype(jnp.bfloat16), 'rep').astype(jnp.float32)]
    ppermute x0 -> x10, waiting for transfers between devices: none -> 81.9 us  [the longest x1 35.1 us: body(): cross = lax.ppermute(cross, CHIP, to_owners(False))]
    dot_general x19 -> x12, matrix products: 157 us -> 83.4 us  [mm(): lax.dot_general(left, right, ((dims[0], dims[1]), ((), ())), preferred_el...]
  transfers between devices with their start and end apart: 12 -> 33, of which waited for: 9 -> 20; matrix products, arithmetic and copies ran while one was open for 10% -> 27% of each run, Pallas kernels for 0% -> 2%
where the time goes in v1:
time: 867 us; the launch traced here: 852 us
  waiting for transfers between devices  233 us (27%)
  starting transfers between devices  166 us (19%)
  blocking collectives  139 us (16%)
  local copies, waits for them, and re-layouts  132 us (15%)
  matrix products  83.4 us (10%)
  other arithmetic  64.8 us (7%)
  Pallas kernels  20 us (2%)
  between operations  15.2 us (2%)
    all_to_all x20, waiting for transfers between devices, exchange(): return lax.all_to_all(a, axes, split_axis=0, concat_axis=0, tiled=True)  151 us
    all_to_all x6, blocking collectives, exchange(): return lax.all_to_all(a, axes, split_axis=0, concat_axis=0, tiled=True)  139 us
    all_to_all x20, starting transfers between devices, exchange(): return lax.all_to_all(a, axes, split_axis=0, concat_axis=0, tiled=True)  121 us
    dot_general x12, matrix products, mm(): lax.dot_general(left, right, ((dims[0], dims[1]), ((), ())), preferred_el...  83.4 us
    ppermute x6, starting transfers between devices, swap(): return lax.ppermute(a, axis, [(0, 1), (1, 0)])  36.6 us
    ppermute x1, waiting for transfers between devices, body(): cross = lax.ppermute(cross, CHIP, to_owners(False))  35.1 us
    ppermute x1, waiting for transfers between devices, body(): part_b = lax.ppermute(w_out, CHIP, to_heads(False))  28 us
    reduce_sum x4, other arithmetic, over_tokens(): t = exchange(t, 'core').astype(F32).sum(axis=0).astype(BF16)  21.1 us
  transfers between devices with their start and end apart: 33, of which 20 were waited for; matrix products, arithmetic and copies ran while one was open for 27% of the time, Pallas kernels for 2%

profile of v1, /device:TPU:1, one launch (start us, length us, event | category | flops | bytes accessed | tf_op | source)
XLA Modules:
  0.0 852.2 jit_solution(17425374822197952361)
XLA Ops:
  31.7 9.1 %all-to-all-start.3 = ((bf16[16,2,128]{2,1,0:T(2,128)(2,1)}), bf16[16,2,128]{2,1,0:T(2,128)(2,1)S(1)}, u32[]{:S(2)}, u32[]{:S(2)}) async-start(bf16[16,2,128]{2,1,0:T(2,128)(2,1)} %broadcast_in_dim.29), calls=%async_computation.3 | async-start | bytes 16384 | tf_op jit(solution)/shard_map/all_to_all | solution.py:35
  47.8 24.7 %all_to_all.134 = bf16[8,128,640]{2,1,0:T(8,128)(2,1)} all-to-all(bf16[8,128,640]{2,1,0:T(8,128)(2,1)S(1)} %bitcast.181), channel_id=1, replica_groups=mesh['zlo'=2,'y'=4,'zhi'=2,'x'=4,'core'=2] {'zhi','x'}, dimensions={0} | all-to-all | bytes 2621440 | tf_op jit(solution)/shard_map/all_to_all | solution.py:35
  85.5 28.0 %collective-permute-done.4 = bf16[128,2048]{1,0:T(8,128)(2,1)S(1)} collective-permute-done((bf16[128,2048]{1,0:T(8,128)(2,1)}, bf16[128,2048]{1,0:T(8,128)(2,1)S(1)}, u32[]{:S(2)}, u32[]{:S(2)}) %collective-permute-start.4) | collective-permute-done | bytes 524320 | tf_op jit(solution)/shard_map/ppermute | solution.py:315
  129.2 12.6 %collective-permute-start.2 = (bf16[8,128,128]{2,1,0:T(8,128)(2,1)S(1)}, bf16[8,128,128]{2,1,0:T(8,128)(2,1)S(1)}, u32[]{:S(2)}, u32[]{:S(2)}) collective-permute-start(bf16[8,128,128]{2,1,0:T(8,128)(2,1)S(1)} %pad_maximum_fusion.6), channel_id=1, source_target_pairs={{0,8},{8,0},{1,9},{9,1},{2,10},{10,2},{3,11},{11,3},{4,12},{12,4},... | collective-permute-start | bytes 786440 | tf_op jit(solution)/shard_map/ppermute | solution.py:43
  143.8 10.2 %collective-permute-done.2 = bf16[8,128,128]{2,1,0:T(8,128)(2,1)S(1)} collective-permute-done((bf16[8,128,128]{2,1,0:T(8,128)(2,1)S(1)}, bf16[8,128,128]{2,1,0:T(8,128)(2,1)S(1)}, u32[]{:S(2)}, u32[]{:S(2)}) %collective-permute-start.2) | collective-permute-done | bytes 262176 | tf_op jit(solution)/shard_map/ppermute | solution.py:43
  154.1 8.7 %attention_forward.1 = (f32[512,512]{1,0:T(8,128)S(1)}, bf16[512,512]{1,0:T(8,128)(2,1)S(1)}, bf16[4,64,1024]{2,1,0:T(8,128)(2,1)S(1)}, f32[4,1,1024]{2,1,0:T(1,128)S(1)}) custom-call(s32[6]{0:T(128)S(1)} %pad_add_fusion.sc, f32[640,512]{1,0:T(8,128)S(1)} %fusion.46.q_ref, f32[32,512]{1,0:T(8,128)S(1)} %get-tuple-element.105.cos_ref, ...), custom_call_target="tpu_custom_call" | custom-call | flops 1073741824 | bytes 8388608 | tf_op jit(solution)/shard_map/attention_forward/pallas_call | solution.py:196
  164.1 43.6 %all_to_all.135 = bf16[4,128,2048]{2,1,0:T(8,128)(2,1)S(1)} all-to-all(bf16[4,128,2048]{2,1,0:T(8,128)(2,1)S(1)} %bitcast.199), channel_id=1, replica_groups=mesh['zlo'=2,'y'=4,'zhi'=2,'x'=4,'core'=2] {'x'}, dimensions={0} | all-to-all | bytes 4194304 | tf_op jit(solution)/shard_map/all_to_all | solution.py:35
  210.3 27.2 %all_to_all.136 = bf16[4,128,2048]{2,1,0:T(8,128)(2,1)} all-to-all(bf16[4,128,2048]{2,1,0:T(8,128)(2,1)S(1)} %broadcast_in_dim.30), channel_id=1, replica_groups=mesh['zlo'=2,'y'=4,'zhi'=2,'x'=4,'core'=2] {'x'}, dimensions={0} | all-to-all | bytes 4194304 | tf_op jit(solution)/shard_map/all_to_all | solution.py:35
  260.8 11.7 %reshape.382 = bf16[2,4,2,2,32,11,256]{6,5,4,3,2,1,0:T(8,128)(2,1)} reshape(bf16[32,32,2816]{2,1,0:T(8,128)(2,1)} %slice.129) | data formatting | bytes 11534336 | tf_op jit(solution)/shard_map/reshape | solution.py:327
  272.4 10.7 %copy.264 = bf16[2,2,11,32,2,4,256]{6,5,4,3,2,1,0:T(4,128)(2,1)} copy(bf16[2,2,11,32,2,4,256]{6,2,3,1,0,5,4:T(8,128)(2,1)} %bitcast.171) | data formatting | bytes 11534336 | tf_op jit(solution)/shard_map/transpose | solution.py:328
  283.1 10.4 %reshape.383 = bf16[1408,2048]{1,0:T(8,128)(2,1)} reshape(bf16[2,2,11,32,2,4,256]{6,5,4,3,2,1,0:T(4,128)(2,1)} %copy.264) | data formatting | bytes 11534336 | tf_op jit(solution)/shard_map/reshape | solution.py:328
  293.5 23.2 %fusion.47 = f32[512,2816]{1,0:T(8,128)} fusion(bf16[512,2048]{1,0:T(8,128)(2,1)} %bitcast.194, bf16[2048,2816]{1,0:T(8,128)(2,1)} %bitcast.175), kind=kOutput, calls=%fused_computation.129 | convolution fusion | flops 5905580032 | bytes 19398656 | tf_op jit(solution)/shard_map/dot_general | solution.py:53
  316.7 10.3 %multiply_convert_fusion.2 = (bf16[512,1408]{1,0:T(8,128)(2,1)S(1)}, bf16[512,1408]{1,0:T(8,128)(2,1)S(1)}, bf16[512,1408]{1,0:T(8,128)(2,1)}) fusion(f32[512,2816]{1,0:T(8,128)} %fusion.47, bf16[1408,2048]{1,0:T(8,128)(2,1)} %reshape.383, bf16[512,2048]{1,0:T(8,128)(2,1)} %bitcast.35), kind=kOutput, calls=%fused_computation.22 | convolution fusion | flops 2963603456 | bytes 17956864 | tf_op jit(solution)/shard_map/dot_general | solution.py:53
  327.1 11.0 %convolution_convert_fusion.4 = bf16[512,2048]{1,0:T(8,128)(2,1)} fusion(bf16[2048,2816]{1,0:T(8,128)(2,1)} %bitcast.176, bf16[512,1408]{1,0:T(8,128)(2,1)S(1)} %get-tuple-element.83, bf16[512,1408]{1,0:T(8,128)(2,1)S(1)} %get-tuple-element.82), kind=kOutput, calls=%fused_computation.15 | convolution fusion | flops 5912395776 | bytes 16515072 | tf_op jit(solution)/shard_map/dot_general | solution.py:53
  350.3 10.5 %reshape.400 = bf16[2,2,352,2,4,256]{5,4,3,2,1,0:T(4,128)(2,1)} reshape(bf16[1408,2048]{1,0:T(8,128)(2,1)} %convolution_convert_fusion.1) | data formatting | bytes 11534336 | tf_op jit(solution)/shard_map/reshape | solution.py:374
  379.7 9.8 %all-to-all-start.24 = ((bf16[2,16,352,256]{3,2,1,0:T(8,128)(2,1)}), bf16[2,16,352,256]{3,2,1,0:T(8,128)(2,1)}, u32[]{:S(2)}, u32[]{:S(2)}) async-start(bf16[2,16,352,256]{3,2,1,0:T(8,128)(2,1)} %bitcast.172), calls=%async_computation.24 | async-start | bytes 11534336 | tf_op jit(solution)/shard_map/all_to_all | solution.py:35
  394.7 23.5 %all_to_all.137 = bf16[2,16,4,16,2816]{4,3,2,1,0:T(8,128)(2,1)} all-to-all(bf16[2,16,4,16,2816]{4,3,2,1,0:T(8,128)(2,1)} %bitcast.169), channel_id=1, replica_groups=mesh['zlo'=2,'y'=4,'zhi'=2,'x'=4,'core'=2] {'core'}, dimensions={0} | all-to-all | bytes 23068672 | tf_op jit(solution)/shard_map/all_to_all | solution.py:35
  424.8 7.8 convolution_convert_fusion.7
  432.6 18.4 %all-to-all-done.10 = bf16[4,128,2048]{2,1,0:T(8,128)(2,1)} async-done(((bf16[4,128,2048]{2,1,0:T(8,128)(2,1)}), bf16[4,128,2048]{2,1,0:T(8,128)(2,1)}, u32[]{:S(2)}, u32[]{:S(2)}) %all-to-all-start.10) | async-done | bytes 2097184 | tf_op jit(solution)/shard_map/all_to_all | solution.py:35
  480.6 10.4 %all_to_all.138 = bf16[2,16,2,128,128]{4,1,3,2,0:T(8,128)(2,1)} all-to-all(bf16[2,16,2,128,128]{4,1,3,2,0:T(8,128)(2,1)} %bitcast.179), channel_id=1, replica_groups=mesh['zlo'=2,'y'=4,'zhi'=2,'x'=4,'core'=2] {'core'}, dimensions={0} | all-to-all | bytes 4194304 | tf_op jit(solution)/shard_map/all_to_all | solution.py:35
  491.0 16.1 %all-to-all-start.25 = ((bf16[16,352,256]{2,1,0:T(8,128)(2,1)}), bf16[16,352,256]{2,1,0:T(8,128)(2,1)}, u32[]{:S(2)}, u32[]{:S(2)}) async-start(bf16[16,352,256]{2,1,0:T(8,128)(2,1)} %reduce_sum.232), calls=%async_computation.25 | async-start | bytes 5767168 | tf_op jit(solution)/shard_map/all_to_all | solution.py:35
  507.2 11.3 %attention_backward.1 = (bf16[512,512]{1,0:T(8,128)(2,1)S(1)}, bf16[16,128,128]{2,1,0:T(8,128)(2,1)S(1)}) custom-call(s32[6]{0:T(128)S(1)} %pad_add_fusion.sc, bf16[4,64,1024]{2,1,0:T(8,128)(2,1)S(1)} %get-tuple-element.15.qr_ref, bf16[512,512]{1,0:T(8,128)(2,1)S(1)} %convolution_convert_fusion.8.do_ref, f32[512,512]{1,0:T(8,128)S(1)} %get-tuple-element.16.o_ref, ...), custom_call_target="tpu_custom_call" | custom-call | flops 2684354560 | bytes 8388608 | tf_op jit(solution)/shard_map/attention_backward/pallas_call | solution.py:237
  521.0 18.6 %collective-permute-start.7 = (bf16[4,128,128]{2,0,1:T(4,128)(2,1)S(1)}, bf16[4,128,128]{2,0,1:T(4,128)(2,1)S(1)}, u32[]{:S(2)}, u32[]{:S(2)}) collective-permute-start(bf16[4,128,128]{2,0,1:T(4,128)(2,1)S(1)} %fusion.15), channel_id=1, source_target_pairs={{0,8},{8,0},{1,9},{9,1},{2,10},{10,2},{3,11},{11,3},{4,12},{12,4},... | collective-permute-start | bytes 393224 | tf_op jit(solution)/shard_map/ppermute | solution.py:43
  556.7 9.5 %all_to_all.139 = bf16[2,16,4,16,640]{4,3,2,1,0:T(8,128)(2,1)} all-to-all(bf16[2,16,4,16,640]{4,3,2,1,0:T(8,128)(2,1)} %bitcast.178), channel_id=1, replica_groups=mesh['zlo'=2,'y'=4,'zhi'=2,'x'=4,'core'=2] {'core'}, dimensions={0} | all-to-all | bytes 5242880 | tf_op jit(solution)/shard_map/all_to_all | solution.py:35
  573.9 10.6 %reduce_sum.230 = bf16[16,4,16,2816]{3,2,1,0:T(8,128)(2,1)} reduce(bf16[2,16,4,16,2816]{4,3,2,1,0:T(8,128)(2,1)} %all_to_all.137, bf16[]{:T(256)} %constant.86.clone.1), dimensions={0}, to_apply=%region_18.19 | reduce | flops 2883584 | bytes 17301506 | tf_op jit(solution)/shard_map/reduce_sum | solution.py:369
  601.6 35.1 %collective-permute-done.9 = bf16[128,128]{1,0:T(8,128)(2,1)S(1)} collective-permute-done((bf16[128,128]{1,0:T(8,128)(2,1)S(1)}, bf16[128,128]{1,0:T(8,128)(2,1)S(1)}, u32[]{:S(2)}, u32[]{:S(2)}) %collective-permute-start.9) | collective-permute-done | bytes 32800 | tf_op jit(solution)/shard_map/ppermute | solution.py:421
  637.0 48.7 %all-to-all-done.22 = bf16[16,4,16,2816]{3,2,1,0:T(8,128)(2,1)} async-done(((bf16[16,4,16,2816]{3,2,1,0:T(8,128)(2,1)}), bf16[16,4,16,2816]{3,2,1,0:T(8,128)(2,1)}, u32[]{:S(2)}, u32[]{:S(2)}) %all-to-all-start.22) | async-done | bytes 5767200 | tf_op jit(solution)/shard_map/all_to_all | solution.py:35
  686.5 8.0 all-to-all-start.20
  723.5 15.9 %all-to-all-done.11 = bf16[4,128,2048]{2,1,0:T(8,128)(2,1)} async-done(((bf16[4,128,2048]{2,1,0:T(8,128)(2,1)}), bf16[4,128,2048]{2,1,0:T(8,128)(2,1)}, u32[]{:S(2)}, u32[]{:S(2)}) %all-to-all-start.11) | async-done | bytes 2097184 | tf_op jit(solution)/shard_map/all_to_all | solution.py:35
  747.0 27.6 %all-to-all-done.15 = bf16[16,4,16,640]{3,2,1,0:T(8,128)(2,1)} async-done(((bf16[16,4,16,640]{3,2,1,0:T(8,128)(2,1)}), bf16[16,4,16,640]{3,2,1,0:T(8,128)(2,1)}, u32[]{:S(2)}, u32[]{:S(2)}) %all-to-all-start.15) | async-done | bytes 1310752 | tf_op jit(solution)/shard_map/all_to_all | solution.py:35
  774.6 10.0 %all-to-all-start.12 = ((f32[16,2,128]{2,1,0:T(2,128)}), f32[16,2,128]{2,1,0:T(2,128)S(1)}, u32[]{:S(2)}, u32[]{:S(2)}) async-start(f32[16,2,128]{2,1,0:T(2,128)} %maximum_bitcast_fusion.2), calls=%async_computation.12 | async-start | bytes 32768 | tf_op jit(solution)/shard_map/all_to_all | solution.py:35
  836.5 8.8 %reshape.407 = f32[128,11264]{1,0:T(8,128)} reshape(f32[8,16,2,2,4,704]{5,4,3,2,1,0:T(4,128)} %copy.282) | data formatting | bytes 11534336 | tf_op jit(solution)/shard_map/convert_element_type | solution.py:378
  (258 shorter events, 295.0 us)
Async XLA Ops:
  11.0 11.4 %all-to-all-start.6 = ((bf16[4,16,2816]{2,1,0:T(8,128)(2,1)}), bf16[4,16,2816]{2,1,0:T(8,128)(2,1)S(1)}, u32[]{:S(2)}, u32[]{:S(2)}) async-start(bf16[4,16,2816]{2,1,0:T(8,128)(2,1)} %reshape.376), calls=%async_computation.6 | async-start | bytes 720896 | tf_op jit(solution)/shard_map/all_to_all | solution.py:35
  15.9 227.7 %all-gather.8.cloned.1.call-start = ((), (), s32[]{:S(2)}) async-start(), calls=%async_computation.27 | async-start | bytes 17842176 | tf_op jit(solution)/shard_map/all_gather | solution.py:324
  23.8 7.2 all-to-all-start
  31.7 16.0 %all-to-all-start.3 = ((bf16[16,2,128]{2,1,0:T(2,128)(2,1)}), bf16[16,2,128]{2,1,0:T(2,128)(2,1)S(1)}, u32[]{:S(2)}, u32[]{:S(2)}) async-start(bf16[16,2,128]{2,1,0:T(2,128)(2,1)} %broadcast_in_dim.29), calls=%async_computation.3 | async-start | bytes 16384 | tf_op jit(solution)/shard_map/all_to_all | solution.py:35
  74.1 45.3 %all-to-all-start.2 = ((bf16[4,128,2048]{2,1,0:T(8,128)(2,1)}), bf16[4,128,2048]{2,1,0:T(8,128)(2,1)S(1)}, u32[]{:S(2)}, u32[]{:S(2)}) async-start(bf16[4,128,2048]{2,1,0:T(8,128)(2,1)} %broadcast_in_dim.28), calls=%async_computation.2 | async-start | bytes 4194304 | tf_op jit(solution)/shard_map/all_to_all | solution.py:35
  78.3 35.2 %collective-permute-start.4 = (bf16[128,2048]{1,0:T(8,128)(2,1)}, bf16[128,2048]{1,0:T(8,128)(2,1)S(1)}, u32[]{:S(2)}, u32[]{:S(2)}) collective-permute-start(bf16[128,2048]{1,0:T(8,128)(2,1)} %param.14), channel_id=1, source_target_pairs={{0,8},{2,0},{4,10},{6,2},{8,12},{10,4},{12,14},{14,6},{1,9},{3,1},... | collective-permute-start | bytes 1572872 | tf_op jit(solution)/shard_map/ppermute | solution.py:315
  78.5 35.0 %collective-permute-start.3 = (bf16[128,2048]{1,0:T(8,128)(2,1)}, bf16[128,2048]{1,0:T(8,128)(2,1)}, u32[]{:S(2)}, u32[]{:S(2)}) collective-permute-start(bf16[128,2048]{1,0:T(8,128)(2,1)} %param.14), channel_id=1, source_target_pairs={{0,0},{2,8},{4,2},{6,10},{8,4},{10,12},{12,6},{14,14},{1,1},{3,9},... | collective-permute-start | bytes 1572872 | tf_op jit(solution)/shard_map/ppermute | solution.py:314
  84.2 36.9 %collective-permute-start = (bf16[8,128,640]{2,1,0:T(8,128)(2,1)}, bf16[8,128,640]{2,1,0:T(8,128)(2,1)}, u32[]{:S(2)}, u32[]{:S(2)}) collective-permute-start(bf16[8,128,640]{2,1,0:T(8,128)(2,1)} %all_to_all.134), channel_id=1, source_target_pairs={{0,1},{1,0},{2,3},{3,2},{4,5},{5,4},{6,7},{7,6},{8,9},{9,8},{10,11... | collective-permute-start | bytes 3932168 | tf_op jit(solution)/shard_map/ppermute | solution.py:43
  116.0 25.8 %collective-permute-start.5 = (bf16[2,128,2048]{2,1,0:T(8,128)(2,1)}, bf16[2,128,2048]{2,1,0:T(8,128)(2,1)}, u32[]{:S(2)}, u32[]{:S(2)}) collective-permute-start(bf16[2,128,2048]{2,1,0:T(8,128)(2,1)} %maximum_select_fusion.3), channel_id=1, source_target_pairs={{0,1},{1,0},{2,3},{3,2},{4,5},{5,4},{6,7},{7,6},{8,9},{9,8},{10,11... | collective-permute-start | bytes 3145736 | tf_op jit(solution)/shard_map/ppermute | solution.py:43
  129.2 24.8 %collective-permute-start.2 = (bf16[8,128,128]{2,1,0:T(8,128)(2,1)S(1)}, bf16[8,128,128]{2,1,0:T(8,128)(2,1)S(1)}, u32[]{:S(2)}, u32[]{:S(2)}) collective-permute-start(bf16[8,128,128]{2,1,0:T(8,128)(2,1)S(1)} %pad_maximum_fusion.6), channel_id=1, source_target_pairs={{0,8},{8,0},{1,9},{9,1},{2,10},{10,2},{3,11},{11,3},{4,12},{12,4},... | collective-permute-start | bytes 786440 | tf_op jit(solution)/shard_map/ppermute | solution.py:43
  239.1 77.6 %all-to-all-start.8 = ((bf16[4,128,2048]{2,1,0:T(8,128)(2,1)}), bf16[4,128,2048]{2,1,0:T(8,128)(2,1)}, u32[]{:S(2)}, u32[]{:S(2)}) async-start(bf16[4,128,2048]{2,1,0:T(8,128)(2,1)} %broadcast_in_dim.31), calls=%async_computation.8 | async-start | bytes 4194304 | tf_op jit(solution)/shard_map/all_to_all | solution.py:35
  338.1 41.6 %all-to-all-start.9 = ((bf16[4,128,2048]{2,1,0:T(8,128)(2,1)}), bf16[4,128,2048]{2,1,0:T(8,128)(2,1)}, u32[]{:S(2)}, u32[]{:S(2)}) async-start(bf16[4,128,2048]{2,1,0:T(8,128)(2,1)} %bitcast.198), calls=%async_computation.9 | async-start | bytes 4194304 | tf_op jit(solution)/shard_map/all_to_all | solution.py:35
  379.7 15.1 %all-to-all-start.24 = ((bf16[2,16,352,256]{3,2,1,0:T(8,128)(2,1)}), bf16[2,16,352,256]{3,2,1,0:T(8,128)(2,1)}, u32[]{:S(2)}, u32[]{:S(2)}) async-start(bf16[2,16,352,256]{3,2,1,0:T(8,128)(2,1)} %bitcast.172), calls=%async_computation.24 | async-start | bytes 11534336 | tf_op jit(solution)/shard_map/all_to_all | solution.py:35
  419.9 31.2 %all-to-all-start.10 = ((bf16[4,128,2048]{2,1,0:T(8,128)(2,1)}), bf16[4,128,2048]{2,1,0:T(8,128)(2,1)}, u32[]{:S(2)}, u32[]{:S(2)}) async-start(bf16[4,128,2048]{2,1,0:T(8,128)(2,1)} %broadcast_in_dim.32), calls=%async_computation.10 | async-start | bytes 4194304 | tf_op jit(solution)/shard_map/all_to_all | solution.py:35
  451.0 29.6 %all-to-all-start.7 = ((bf16[4,128,2048]{2,1,0:T(8,128)(2,1)}), bf16[4,128,2048]{2,1,0:T(8,128)(2,1)}, u32[]{:S(2)}, u32[]{:S(2)}) async-start(bf16[4,128,2048]{2,1,0:T(8,128)(2,1)} %bitcast.197), calls=%async_computation.7 | async-start | bytes 4194304 | tf_op jit(solution)/shard_map/all_to_all | solution.py:35
  491.0 65.6 %all-to-all-start.25 = ((bf16[16,352,256]{2,1,0:T(8,128)(2,1)}), bf16[16,352,256]{2,1,0:T(8,128)(2,1)}, u32[]{:S(2)}, u32[]{:S(2)}) async-start(bf16[16,352,256]{2,1,0:T(8,128)(2,1)} %reduce_sum.232), calls=%async_computation.25 | async-start | bytes 5767168 | tf_op jit(solution)/shard_map/all_to_all | solution.py:35
  518.8 1.9 collective-permute-start.6
  521.0 31.4 %collective-permute-start.7 = (bf16[4,128,128]{2,0,1:T(4,128)(2,1)S(1)}, bf16[4,128,128]{2,0,1:T(4,128)(2,1)S(1)}, u32[]{:S(2)}, u32[]{:S(2)}) collective-permute-start(bf16[4,128,128]{2,0,1:T(4,128)(2,1)S(1)} %fusion.15), channel_id=1, source_target_pairs={{0,8},{8,0},{1,9},{9,1},{2,10},{10,2},{3,11},{11,3},{4,12},{12,4},... | collective-permute-start | bytes 393224 | tf_op jit(solution)/shard_map/ppermute | solution.py:43
  566.1 24.5 %all-to-all-start.19 = ((bf16[16,2,128,128]{3,2,1,0:T(8,128)(2,1)}), bf16[16,2,128,128]{3,2,1,0:T(8,128)(2,1)S(1)}, u32[]{:S(2)}, u32[]{:S(2)}) async-start(bf16[16,2,128,128]{3,2,1,0:T(8,128)(2,1)} %copy.276), calls=%async_computation.19 | async-start | bytes 2097152 | tf_op jit(solution)/shard_map/all_to_all | solution.py:35
  590.6 95.1 %all-to-all-start.22 = ((bf16[16,4,16,2816]{3,2,1,0:T(8,128)(2,1)}), bf16[16,4,16,2816]{3,2,1,0:T(8,128)(2,1)}, u32[]{:S(2)}, u32[]{:S(2)}) async-start(bf16[16,4,16,2816]{3,2,1,0:T(8,128)(2,1)} %reduce_sum.230), calls=%async_computation.22 | async-start | bytes 11534336 | tf_op jit(solution)/shard_map/all_to_all | solution.py:35
  596.2 220.4 %all-gather.10.cloned.1.call-start = ((), (), s32[]{:S(2)}) async-start(), calls=%async_computation.28 | async-start | bytes 1622016 | tf_op jit(solution)/shard_map/all_gather | solution.py:379
  599.3 2.3 collective-permute-start.8
  600.0 36.7 %collective-permute-start.9 = (bf16[128,128]{1,0:T(8,128)(2,1)S(1)}, bf16[128,128]{1,0:T(8,128)(2,1)S(1)}, u32[]{:S(2)}, u32[]{:S(2)}) collective-permute-start(bf16[128,128]{1,0:T(8,128)(2,1)S(1)} %get-tuple-element.101), channel_id=1, source_target_pairs={{8,0},{0,2},{10,4},{2,6},{12,8},{4,10},{14,12},{6,14},{9,1},{1,3},... | collective-permute-start | bytes 98312 | tf_op jit(solution)/shard_map/ppermute | solution.py:421
  686.5 15.9 %all-to-all-start.20 = ((bf16[8,128,256]{2,1,0:T(8,128)(2,1)}), bf16[8,128,256]{2,1,0:T(8,128)(2,1)S(1)}, u32[]{:S(2)}, u32[]{:S(2)}) async-start(bf16[8,128,256]{2,1,0:T(8,128)(2,1)} %broadcast_in_dim.35), calls=%async_computation.20 | async-start | bytes 1048576 | tf_op jit(solution)/shard_map/all_to_all | solution.py:35
  702.4 9.7 %all-to-all-start.23 = ((bf16[4,16,2816]{2,1,0:T(8,128)(2,1)}), bf16[4,16,2816]{2,1,0:T(8,128)(2,1)S(1)}, u32[]{:S(2)}, u32[]{:S(2)}) async-start(bf16[4,16,2816]{2,1,0:T(8,128)(2,1)} %reduce_sum.231), calls=%async_computation.23 | async-start | bytes 720896 | tf_op jit(solution)/shard_map/all_to_all | solution.py:35
  712.8 26.6 %all-to-all-start.11 = ((bf16[4,128,2048]{2,1,0:T(8,128)(2,1)}), bf16[4,128,2048]{2,1,0:T(8,128)(2,1)}, u32[]{:S(2)}, u32[]{:S(2)}) async-start(bf16[4,128,2048]{2,1,0:T(8,128)(2,1)} %bitcast.196), calls=%async_computation.11 | async-start | bytes 4194304 | tf_op jit(solution)/shard_map/all_to_all | solution.py:35
  717.5 109.4 %all-gather.6.cloned.1.call-start = ((), (), s32[]{:S(2)}) async-start(), calls=%async_computation.26 | async-start | bytes 3538944 | tf_op jit(solution)/shard_map/all_gather | solution.py:377
  739.4 35.2 %all-to-all-start.15 = ((bf16[16,4,16,640]{3,2,1,0:T(8,128)(2,1)}), bf16[16,4,16,640]{3,2,1,0:T(8,128)(2,1)}, u32[]{:S(2)}, u32[]{:S(2)}) async-start(bf16[16,4,16,640]{3,2,1,0:T(8,128)(2,1)} %reduce_sum.226), calls=%async_computation.15 | async-start | bytes 2621440 | tf_op jit(solution)/shard_map/all_to_all | solution.py:35
  774.6 19.2 %all-to-all-start.12 = ((f32[16,2,128]{2,1,0:T(2,128)}), f32[16,2,128]{2,1,0:T(2,128)S(1)}, u32[]{:S(2)}, u32[]{:S(2)}) async-start(f32[16,2,128]{2,1,0:T(2,128)} %maximum_bitcast_fusion.2), calls=%async_computation.12 | async-start | bytes 32768 | tf_op jit(solution)/shard_map/all_to_all | solution.py:35
  793.8 8.7 %all-to-all-start.16 = ((bf16[4,16,640]{2,1,0:T(8,128)(2,1)}), bf16[4,16,640]{2,1,0:T(8,128)(2,1)S(1)}, u32[]{:S(2)}, u32[]{:S(2)}) async-start(bf16[4,16,640]{2,1,0:T(8,128)(2,1)} %reduce_sum.227), calls=%async_computation.16 | async-start | bytes 163840 | tf_op jit(solution)/shard_map/all_to_all | solution.py:35
  803.1 8.2 all-to-all-start.13
  812.2 12.5 %all-to-all-start.17 = ((bf16[8,4,16,640]{3,2,1,0:T(8,128)(2,1)}), bf16[8,4,16,640]{3,2,1,0:T(8,128)(2,1)S(1)}, u32[]{:S(2)}, u32[]{:S(2)}) async-start(bf16[8,4,16,640]{3,2,1,0:T(8,128)(2,1)} %broadcast_in_dim.34), calls=%async_computation.17 | async-start | bytes 1310720 | tf_op jit(solution)/shard_map/all_to_all | solution.py:35
  (43 other events, 591.4 us)
Sparse Core Ops, SparseCore 0:
  23.4 144.4 all-gather.7
  599.3 71.9 all-gather.9
  721.7 59.2 all-gather.5

commit v2 on v1

v2 whole, which is shorter than its diff:
```python
import math

import jax
import jax.numpy as jnp
from jax import lax
from jax.experimental import pallas as pl
from jax.experimental.pallas import tpu as pltpu
from jax.sharding import Mesh
from jax.sharding import PartitionSpec as P

QUERY_HEADS = 32
KEY_VALUE_HEADS = 4
HEAD_SIZE = 64
GROUP = QUERY_HEADS // KEY_VALUE_HEADS
EPS = 1e-05
ROPE_BASE = 10000.0
NEG = -1e30
BLOCK = 128
CHUNK = 2 * BLOCK
SCALE = 1.0 / math.sqrt(HEAD_SIZE)

AXES = ("zlo", "y", "zhi", "x", "core")
REP = ("zlo", "y")
SHARD = ("zhi", "x", "core")
CHIP = ("zhi", "x")
YZ = ("zlo", "y", "zhi")
YZC = ("zlo", "y", "zhi", "core")
NX = 4

F32 = jnp.float32
BF16 = jnp.bfloat16


def exchange(a, axes):
    return lax.all_to_all(a, axes, split_axis=0, concat_axis=0, tiled=True)


def everywhere(a, axes, n):
    return exchange(jnp.broadcast_to(a[None], (n,) + a.shape), axes)


def swap(a, axis):
    return lax.ppermute(a, axis, [(0, 1), (1, 0)])


def in_order(coord, mine, other, axis):
    return jnp.where(
        coord == 0, jnp.stack([mine, other], axis=axis), jnp.stack([other, mine], axis=axis)
    )


def mm(left, right, dims, out=F32):
    return lax.dot_general(
        left, right, ((dims[0], dims[1]), ((), ())), preferred_element_type=F32
    ).astype(out)


def rms_forward(rows):
    rstd = lax.rsqrt(jnp.mean(rows * rows, axis=1, keepdims=True) + EPS)
    return rows * rstd, rstd


def rms_backward(d_normed, scaled, rstd, gain):
    gain_term = jnp.sum(d_normed * scaled, axis=0)
    inner = d_normed * gain[None, :]
    d_values = rstd * (inner - scaled * jnp.mean(inner * scaled, axis=1, keepdims=True))
    return d_values, gain_term


def heads_to_lanes(ref):
    return jnp.concatenate(
        [ref[HEAD_SIZE * h : HEAD_SIZE * (h + 1), :] for h in range(GROUP)], axis=1
    )


def chunk_slots(c, zhi, x, core):
    base = ((c // 4) ^ zhi) * 8 + ((c - x) & 3)
    return base + 4 * core, base + 4 * (1 - core)


def allowed_mask(c, st, block):
    keys = lax.broadcasted_iota(jnp.int32, (CHUNK, 1), 0) + c * CHUNK
    lanes = lax.broadcasted_iota(jnp.int32, (1, GROUP * BLOCK), 1) % BLOCK
    return (keys >= st) & (keys <= block * BLOCK + lanes)


def over_chunks(step, state, first, clear, last):
    clear = jnp.minimum(clear, last)
    state = lax.fori_loop(first, clear, lambda c, v: step(c, v, True), state)
    state = lax.fori_loop(clear, last, lambda c, v: step(c, v, False), state)
    return step(last, state, True)


def attention_forward(sc, q_ref, cos_ref, sin_ref, st_ref, kv_ref, o_ref, ob_ref, qr_ref, lse_ref):
    b = pl.program_id(0)
    zhi, x, core, first = sc[0], sc[1], sc[2], sc[3 + b]
    block = zhi * 8 + 2 * ((x + b) & 3) + core
    cos, sin = cos_ref[...], sin_ref[...]
    turned = []
    for h in range(GROUP):
        u1 = q_ref[HEAD_SIZE * h : HEAD_SIZE * h + 32, :]
        u2 = q_ref[HEAD_SIZE * h + 32 : HEAD_SIZE * h + 64, :]
        turned.append(jnp.concatenate([u1 * cos - u2 * sin, u2 * cos + u1 * sin], axis=0))
    q = jnp.concatenate(turned, axis=1).astype(BF16) * jnp.asarray(SCALE, BF16)
    qr_ref[0] = q
    st = jnp.concatenate([st_ref[0]] * GROUP, axis=1)

    def step(c, state, masked):
        m, l, acc = state
        s0, s1 = chunk_slots(c, zhi, x, core)
        k = jnp.concatenate([kv_ref[s0, :HEAD_SIZE, :], kv_ref[s1, :HEAD_SIZE, :]], axis=1)
        v = jnp.concatenate([kv_ref[s0, HEAD_SIZE:, :], kv_ref[s1, HEAD_SIZE:, :]], axis=1)
        s = lax.dot_general(k, q, (((0,), (0,)), ((), ())), preferred_element_type=F32)
        if masked:
            s = jnp.where(allowed_mask(c, st, block), s, NEG)
        m2 = jnp.maximum(m, jnp.max(s, axis=0, keepdims=True))
        p = jnp.exp(s - m2)
        al = jnp.exp(m - m2)
        l = l * al + jnp.sum(p, axis=0, keepdims=True)
        acc = acc * al + lax.dot_general(
            v, p.astype(BF16), (((1,), (0,)), ((), ())), preferred_element_type=F32
        )
        return m2, l, acc

    rows = GROUP * BLOCK
    state = (
        jnp.full((1, rows), NEG, F32),
        jnp.zeros((1, rows), F32),
        jnp.zeros((HEAD_SIZE, rows), F32),
    )
    m, l, acc = over_chunks(step, state, first, sc[7 + b], block // 2)
    o = acc / l
    for h in range(GROUP):
        part = o[:, BLOCK * h : BLOCK * (h + 1)]
        o_ref[HEAD_SIZE * h : HEAD_SIZE * (h + 1), :] = part
        ob_ref[HEAD_SIZE * h : HEAD_SIZE * (h + 1), :] = part.astype(BF16)
    lse_ref[0] = m + jnp.log(l)


def attention_backward(
    sc, qr_ref, do_ref, o_ref, lse_ref, cos_ref, sin_ref, st_ref, kv_ref, dq_ref, dkv_ref, acc_ref
):
    b = pl.program_id(0)
    zhi, x, core, first = sc[0], sc[1], sc[2], sc[3 + b]
    block = zhi * 8 + 2 * ((x + b) & 3) + core

    @pl.when(b == 0)
    def _():
        acc_ref[...] = jnp.zeros_like(acc_ref)

    q = qr_ref[0]
    do = heads_to_lanes(do_ref)
    delta = jnp.sum(do.astype(F32) * heads_to_lanes(o_ref), axis=0, keepdims=True)
    q_rows = q.T
    do_rows = do.T
    lse = lse_ref[0]
    st = jnp.concatenate([st_ref[0]] * GROUP, axis=1)

    def step(c, dq, masked):
        s0, s1 = chunk_slots(c, zhi, x, core)
        k = jnp.concatenate([kv_ref[s0, :HEAD_SIZE, :], kv_ref[s1, :HEAD_SIZE, :]], axis=1)
        v = jnp.concatenate([kv_ref[s0, HEAD_SIZE:, :], kv_ref[s1, HEAD_SIZE:, :]], axis=1)
        s = lax.dot_general(k, q, (((0,), (0,)), ((), ())), preferred_element_type=F32)
        if masked:
            s = jnp.where(allowed_mask(c, st, block), s, NEG)
        p = jnp.exp(s - lse)
        dp = lax.dot_general(v, do, (((0,), (0,)), ((), ())), preferred_element_type=F32)
        ds = (p * (dp - delta)).astype(BF16)
        pb = p.astype(BF16)
        dk = jnp.dot(ds, q_rows, preferred_element_type=F32)
        dv = jnp.dot(pb, do_rows, preferred_element_type=F32)
        both = jnp.concatenate([dk, dv], axis=1)
        acc_ref[s0] += both[:BLOCK]
        acc_ref[s1] += both[BLOCK:]
        return dq + jnp.dot(k, ds, preferred_element_type=F32)

    dq = jnp.zeros((HEAD_SIZE, GROUP * BLOCK), F32)
    dq = over_chunks(step, dq, first, sc[7 + b], block // 2)
    dq = dq * SCALE
    cos, sin = cos_ref[...], sin_ref[...]
    for h in range(GROUP):
        g1 = dq[:32, BLOCK * h : BLOCK * (h + 1)]
        g2 = dq[32:, BLOCK * h : BLOCK * (h + 1)]
        dq_ref[HEAD_SIZE * h : HEAD_SIZE * h + 32, :] = (g1 * cos + g2 * sin).astype(BF16)
        dq_ref[HEAD_SIZE * h + 32 : HEAD_SIZE * h + 64, :] = (g2 * cos - g1 * sin).astype(BF16)

    @pl.when(b == NX - 1)
    def _():
        for n in range(16):
            dkv_ref[n] = acc_ref[n].T.astype(BF16)


VMEM_LIMIT = 48 * 1024 * 1024


def call_forward(sc, qkv_t, cos, sin, st, kv):
    rows, toks = GROUP * HEAD_SIZE, NX * BLOCK
    lanes = GROUP * BLOCK
    tile = pl.BlockSpec((rows, BLOCK), lambda b, s: (0, b))
    trig = pl.BlockSpec((32, BLOCK), lambda b, s: (0, b))
    return pl.pallas_call(
        attention_forward,
        grid_spec=pltpu.PrefetchScalarGridSpec(
            num_scalar_prefetch=1,
            grid=(NX,),
            in_specs=[
                tile,
                trig,
                trig,
                pl.BlockSpec((1, 1, BLOCK), lambda b, s: (b, 0, 0)),
                pl.BlockSpec((16, BLOCK, BLOCK), lambda b, s: (0, 0, 0)),
            ],
            out_specs=[
                tile,
                tile,
                pl.BlockSpec((1, HEAD_SIZE, lanes), lambda b, s: (b, 0, 0)),
                pl.BlockSpec((1, 1, lanes), lambda b, s: (b, 0, 0)),
            ],
        ),
        out_shape=[
            jax.ShapeDtypeStruct((rows, toks), F32),
            jax.ShapeDtypeStruct((rows, toks), BF16),
            jax.ShapeDtypeStruct((NX, HEAD_SIZE, lanes), BF16),
            jax.ShapeDtypeStruct((NX, 1, lanes), F32),
        ],
        compiler_params=pltpu.CompilerParams(
            dimension_semantics=("arbitrary",), vmem_limit_bytes=VMEM_LIMIT
        ),
        cost_estimate=cost(1 << 20, 1 << 16),
        name="attention_forward",
    )(sc, qkv_t, cos, sin, st, kv)


def call_backward(sc, qr, do, o, lse, cos, sin, st, kv):
    rows, toks = GROUP * HEAD_SIZE, NX * BLOCK
    lanes = GROUP * BLOCK
    tile = pl.BlockSpec((rows, BLOCK), lambda b, s: (0, b))
    trig = pl.BlockSpec((32, BLOCK), lambda b, s: (0, b))
    whole = pl.BlockSpec((16, BLOCK, BLOCK), lambda b, s: (0, 0, 0))
    return pl.pallas_call(
        attention_backward,
        grid_spec=pltpu.PrefetchScalarGridSpec(
            num_scalar_prefetch=1,
            grid=(NX,),
            in_specs=[
                pl.BlockSpec((1, HEAD_SIZE, lanes), lambda b, s: (b, 0, 0)),
                tile,
                tile,
                pl.BlockSpec((1, 1, lanes), lambda b, s: (b, 0, 0)),
                trig,
                trig,
                pl.BlockSpec((1, 1, BLOCK), lambda b, s: (b, 0, 0)),
                whole,
            ],
            out_specs=[tile, whole],
            scratch_shapes=[pltpu.VMEM((16, BLOCK, BLOCK), F32)],
        ),
        out_shape=[
            jax.ShapeDtypeStruct((rows, toks), BF16),
            jax.ShapeDtypeStruct((16, BLOCK, BLOCK), BF16),
        ],
        compiler_params=pltpu.CompilerParams(
            dimension_semantics=("arbitrary",), vmem_limit_bytes=VMEM_LIMIT
        ),
        cost_estimate=cost(1 << 20, 1 << 16),
        name="attention_backward",
    )(sc, qr, do, o, lse, cos, sin, st, kv)


def project(
    sc, t0, t1, t2a, t2b, t3, mine, other, cos_ref, sin_ref, n_ref, q_ref, kv_ref, w_ref, gain_ref
):
    for ref, c in ((mine, sc[0]), (other, 1 - sc[0])):
        for chip in range(8):
            at = pl.ds(pl.multiple_of((2 * chip + c) * BLOCK, BLOCK), BLOCK)
            w_ref[at, :] = ref[chip, :BLOCK, :]
            info = ref[chip, BLOCK:, :].astype(F32)
            gain_ref[0:1, at] = info[0:1, :BLOCK]
            gain_ref[1:2, at] = info[0:1, BLOCK : 2 * BLOCK]
    for j, t_refs in enumerate(((t0,), (t1,), (t2a, t2b), (t3,))):
        cols = slice(BLOCK * j, BLOCK * (j + 1))
        v = jnp.concatenate([t[...] for t in t_refs], axis=0).astype(F32)
        rstd = lax.rsqrt(jnp.mean(v * v, axis=1, keepdims=True) + EPS)
        n = (v * rstd * gain_ref[0:1, :]).astype(BF16)
        n_ref[cols, :] = n
        qkv = jnp.dot(n, w_ref[...], preferred_element_type=F32).T
        rows = GROUP * HEAD_SIZE
        q_ref[:, cols] = qkv[:rows]
        cos, sin = cos_ref[:, cols], sin_ref[:, cols]
        k1, k2 = qkv[rows : rows + 32], qkv[rows + 32 : rows + 64]
        kv_ref[j, :32, :] = (k1 * cos - k2 * sin).astype(BF16)
        kv_ref[j, 32:64, :] = (k2 * cos + k1 * sin).astype(BF16)
        kv_ref[j, 64:, :] = qkv[rows + 64 :].astype(BF16)


def params(*semantics):
    return pltpu.CompilerParams(
        dimension_semantics=semantics or None, vmem_limit_bytes=VMEM_LIMIT
    )


def cost(flops, moved):
    return pl.CostEstimate(flops=flops, bytes_accessed=moved, transcendentals=0)


def call_project(sc, toks, mine, other, cos, sin):
    dim, cols = toks[0].shape[1], mine.shape[2]
    vmem = pl.BlockSpec(memory_space=pltpu.VMEM)
    return pl.pallas_call(
        project,
        in_specs=[pl.BlockSpec(memory_space=pltpu.SMEM)] + [vmem] * 9,
        out_specs=[vmem] * 5,
        out_shape=[
            jax.ShapeDtypeStruct((NX * BLOCK, dim), BF16),
            jax.ShapeDtypeStruct((GROUP * HEAD_SIZE, NX * BLOCK), F32),
            jax.ShapeDtypeStruct((NX, 2 * HEAD_SIZE, BLOCK), BF16),
            jax.ShapeDtypeStruct((dim, cols), BF16),
            jax.ShapeDtypeStruct((2, dim), F32),
        ],
        compiler_params=params(),
        cost_estimate=cost(1 << 20, 1 << 16),
        name="project",
    )(sc, *toks, mine, other, cos, sin)


def out_project(sc, o_ref, a_ref, b_ref, a2_ref, b2_ref, p0, p1, p2, p3, w_ref):
    first, core = sc[0], sc[1]
    for ref, p, c in (
        (a_ref, first, core),
        (b_ref, 1 - first, core),
        (a2_ref, first, 1 - core),
        (b2_ref, 1 - first, 1 - core),
    ):
        w_ref[pl.ds(pl.multiple_of((2 * p + c) * BLOCK, BLOCK), BLOCK), :] = ref[...]
    for half in range(2):
        at = slice(1024 * half, 1024 * (half + 1))
        d = lax.dot_general(
            o_ref[...], w_ref[:, at], (((0,), (0,)), ((), ())), preferred_element_type=F32
        ).astype(BF16)
        for j, p in enumerate((p0, p1, p2, p3)):
            p[:, at] = d[BLOCK * j : BLOCK * (j + 1)]


def call_out_project(sc, o, *w):
    vmem = pl.BlockSpec(memory_space=pltpu.VMEM)
    return pl.pallas_call(
        out_project,
        in_specs=[pl.BlockSpec(memory_space=pltpu.SMEM)] + [vmem] * 5,
        out_specs=[vmem] * 5,
        out_shape=[jax.ShapeDtypeStruct((BLOCK, 2048), BF16)] * 4
        + [jax.ShapeDtypeStruct((4 * BLOCK, 2048), BF16)],
        compiler_params=params(),
        cost_estimate=cost(1 << 20, 1 << 16),
        name="out_project",
    )(sc, o, *w)


def spread(in_ref, gu_ref, dn_ref, qkv_ref, out_ref, terms_ref):
    for x in range(NX):
        for half in range(2):
            at, to = FF_TILE * (2 * x + half), FF_TILE * (4 * half + x)
            gu_ref[:, to : to + FF_TILE] = in_ref[0, :, at : at + FF_TILE].astype(F32)
    base = 8 * FF_TILE
    for t in range(22):
        at = base + 2 * FF_TILE * (t % 2) + 256 * (t // 2)
        dn_ref[16 * t : 16 * (t + 1), :] = in_ref[0, :, at : at + 256].astype(F32)
    base += 4 * FF_TILE
    k, v = [], []
    for x in range(NX):
        at = base + 640 * x
        qkv_ref[:, 512 * x : 512 * (x + 1)] = in_ref[0, :, at : at + 512].astype(F32)
        k.append(in_ref[0, :, at + 512 : at + 576].astype(F32))
        v.append(in_ref[0, :, at + 576 : at + 640].astype(F32))
    qkv_ref[:, 2048:2304] = jnp.concatenate(k, axis=1)
    qkv_ref[:, 2304:] = jnp.concatenate(v, axis=1)
    base += 640 * NX
    for t in range(8):
        at = base + 256 * t
        out_ref[16 * t : 16 * (t + 1), :] = in_ref[0, :, at : at + 256].astype(F32)
    base += 2048
    row = in_ref[0, :, base : base + 256].astype(F32)
    terms = jnp.concatenate([row[0:1, :BLOCK], row[0:1, BLOCK:]], axis=0)

    @pl.when(pl.program_id(0) == 0)
    def _():
        terms_ref[...] = terms

    @pl.when(pl.program_id(0) > 0)
    def _():
        terms_ref[...] += terms


def call_spread(both):
    return pl.pallas_call(
        spread,
        grid=(8,),
        in_specs=[pl.BlockSpec((1, 16, both.shape[2]), lambda r: (r, 0, 0))],
        out_specs=[
            pl.BlockSpec((16, 8 * FF_TILE), lambda r: (r, 0)),
            pl.BlockSpec((352, 256), lambda r: (0, r)),
            pl.BlockSpec((16, 2560), lambda r: (r, 0)),
            pl.BlockSpec((BLOCK, 256), lambda r: (0, r)),
            pl.BlockSpec((2, BLOCK), lambda r: (0, 0)),
        ],
        out_shape=[
            jax.ShapeDtypeStruct((BLOCK, 8 * FF_TILE), F32),
            jax.ShapeDtypeStruct((352, 2048), F32),
            jax.ShapeDtypeStruct((BLOCK, 2560), F32),
            jax.ShapeDtypeStruct((BLOCK, 2048), F32),
            jax.ShapeDtypeStruct((2, BLOCK), F32),
        ],
        compiler_params=params("arbitrary"),
        cost_estimate=cost(1 << 20, 1 << 16),
        name="spread",
    )(both)


FF_TILE = 1408


def pack(sc, w_ref, g1_ref, g2_ref, st_ref, gu_ref, dn_ref, wide_ref, gus_ref, dns_ref):
    st = st_ref[...]
    info = [g1_ref[...].astype(F32), g2_ref[...].astype(F32)]
    info += [(st // 256).astype(F32), (st % 256).astype(F32), jnp.zeros((1, BLOCK), F32)]
    info = jnp.broadcast_to(jnp.concatenate(info, axis=1), (16, 5 * BLOCK)).astype(BF16)
    for x in range(NX):
        j = (x - sc[1]) & 3
        k = w_ref[:, 2048 + 64 * x : 2048 + 64 * (x + 1)]
        v = w_ref[:, 2304 + 64 * x : 2304 + 64 * (x + 1)]
        kv = jnp.concatenate([k, v], axis=1)
        for zhi in range(2):
            wide_ref[NX * zhi + x, :BLOCK, :512] = w_ref[:, 512 * x : 512 * (x + 1)]
            wide_ref[NX * zhi + x, :BLOCK, 512:] = kv
            wide_ref[NX * zhi + x, BLOCK:, :] = info
        gus_ref[j, :, :FF_TILE] = gu_ref[:, FF_TILE * x : FF_TILE * (x + 1)]
        up = 4 * FF_TILE + FF_TILE * x
        gus_ref[j, :, FF_TILE:] = gu_ref[:, up : up + FF_TILE]
    for j in range(11):
        dns_ref[:, 256 * j : 256 * (j + 1)] = dn_ref[32 * j : 32 * (j + 1), :]


def call_pack(sc, w_qkv, gain_1, gain_2, starts, w_gu, w_dn):
    vec = pl.BlockSpec((1, BLOCK), lambda i, s: (0, 0))
    return pl.pallas_call(
        pack,
        grid_spec=pltpu.PrefetchScalarGridSpec(
            num_scalar_prefetch=1,
            grid=(1,),
            in_specs=[
                pl.BlockSpec((BLOCK, 2560), lambda i, s: (0, 0)),
                vec,
                vec,
                vec,
                pl.BlockSpec((16, 8 * FF_TILE), lambda i, s: (s[0], 0)),
                pl.BlockSpec((352, 256), lambda i, s: (0, s[0])),
            ],
            out_specs=[
                pl.BlockSpec((8, BLOCK + 16, 640), lambda i, s: (0, 0, 0)),
                pl.BlockSpec((NX, 16, 2 * FF_TILE), lambda i, s: (0, 0, 0)),
                pl.BlockSpec((32, 2 * FF_TILE), lambda i, s: (0, 0)),
            ],
        ),
        out_shape=[
            jax.ShapeDtypeStruct((8, BLOCK + 16, 640), BF16),
            jax.ShapeDtypeStruct((NX, 16, 2 * FF_TILE), BF16),
            jax.ShapeDtypeStruct((32, 2 * FF_TILE), BF16),
        ],
        compiler_params=params("arbitrary"),
        cost_estimate=cost(1 << 20, 1 << 16),
        name="pack",
    )(sc, w_qkv, gain_1[None], gain_2[None], starts[None], w_gu, w_dn)


def down_back(c0, c1, c2, c3, w_ref, d_ref, wdn_ref):
    r = pl.program_id(0)
    for p in range(2):
        for c in range(2):
            for j in range(11):
                at = (2 * p + c) * 352 + 32 * j
                wdn_ref[at : at + 32, :] = w_ref[0, p, c, :, 256 * j : 256 * (j + 1)]
    cots = jnp.concatenate([c0[...], c1[...], c2[...], c3[...]], axis=0)
    part = lax.dot_general(
        cots, wdn_ref[...], (((1,), (1,)), ((), ())), preferred_element_type=F32
    )

    @pl.when(r == 0)
    def _():
        d_ref[...] = part

    @pl.when(r > 0)
    def _():
        d_ref[...] += part


def call_down_back(cots, ffn):
    return pl.pallas_call(
        down_back,
        grid=(8,),
        in_specs=[pl.BlockSpec((BLOCK, 256), lambda r: (0, r))] * 4
        + [pl.BlockSpec((1, 2, 2, 32, 2 * FF_TILE), lambda r: (r, 0, 0, 2, 0))],
        out_specs=[
            pl.BlockSpec((NX * BLOCK, FF_TILE), lambda r: (0, 0)),
            pl.BlockSpec((FF_TILE, 256), lambda r: (0, r)),
        ],
        out_shape=[
            jax.ShapeDtypeStruct((NX * BLOCK, FF_TILE), F32),
            jax.ShapeDtypeStruct((FF_TILE, 2048), BF16),
        ],
        compiler_params=params("arbitrary"),
        cost_estimate=cost(1 << 33, 1 << 20),
        name="down_back",
    )(*cots, ffn)


def natural(w_ref, pick, me):
    parts = []
    for zhi, x, c in pick:
        at = pl.ds(pl.multiple_of(((me - x) & 3) * 16, 16), 16)
        parts.append(w_ref[:, zhi, c, at, :].reshape(BLOCK, BLOCK))
    return jnp.concatenate(parts, axis=0)


ORDER = [(zhi, x, c) for zhi in range(2) for x in range(NX) for c in range(2)]
FF_STEPS = FF_TILE // BLOCK


def feed_forward(
    sc, n0, n1, n2, n3, wg_ref, wu_ref, w_ref, d_ref, o0, o1, o2, o3, act_ref, dgu_ref, n_s, act_s, dg_s
):
    k = pl.program_id(0)

    @pl.when(k == 0)
    def _():
        for j, n in enumerate((n0, n1, n2, n3)):
            n_s[BLOCK * j : BLOCK * (j + 1), :] = n[...]

    @pl.when(k < FF_STEPS)
    def _():
        w = [natural(ref, ORDER, sc[0]) for ref in (wg_ref, wu_ref)]
        w = jnp.concatenate(w, axis=1)
        both = jnp.dot(n_s[...], w, preferred_element_type=F32)
        gate, up = both[:, :BLOCK], both[:, BLOCK:]
        d_act = d_ref[...]
        sig = 1.0 / (1.0 + jnp.exp(-gate))
        silu = gate * sig
        at = pl.ds(pl.multiple_of(k * BLOCK, BLOCK), BLOCK)
        up_at = pl.ds(pl.multiple_of(FF_TILE + k * BLOCK, BLOCK), BLOCK)
        act_s[:, at] = (silu * up).astype(BF16)
        d_gate = d_act * up * (sig * (1.0 + gate * (1.0 - sig)))
        dg_s[:, at] = d_gate.astype(BF16)
        dg_s[:, up_at] = (d_act * silu).astype(BF16)

    @pl.when(k == FF_STEPS)
    def _():
        act_ref[...] = act_s[...]
        dgu_ref[...] = dg_s[...]

    @pl.when(k >= FF_STEPS)
    def _():
        w = jnp.concatenate(
            [w_ref[:, 0, c].reshape(BLOCK, 2 * FF_TILE) for c in range(2)], axis=0
        )
        d = lax.dot_general(
            dg_s[...], w, (((1,), (1,)), ((), ())), preferred_element_type=F32
        ).astype(BF16)
        for j, o in enumerate((o0, o1, o2, o3)):
            o[...] = d[BLOCK * j : BLOCK * (j + 1)]


def call_feed_forward(x, n2, ffn, d_act):
    def tile(k):
        return jnp.minimum(k, FF_STEPS - 1)

    def later(k):
        return jnp.maximum(k - FF_STEPS, 0)

    def row_block(k, s):
        return (0, later(k) >> 2, 0, (s[0] - later(k)) & 3, 0)

    whole = pl.BlockSpec((BLOCK, 2048), lambda k, s: (0, 0))
    out = pl.BlockSpec((BLOCK, 256), lambda k, s: (0, later(k)))
    return pl.pallas_call(
        feed_forward,
        grid_spec=pltpu.PrefetchScalarGridSpec(
            num_scalar_prefetch=1,
            grid=(FF_STEPS + 8,),
            in_specs=[whole] * 4
            + [
                pl.BlockSpec((8, 2, 2, 64, BLOCK), lambda k, s: (0, 0, 0, 0, tile(k))),
                pl.BlockSpec((8, 2, 2, 64, BLOCK), lambda k, s: (0, 0, 0, 0, FF_STEPS + tile(k))),
                pl.BlockSpec((8, 1, 2, 16, 2 * FF_TILE), row_block),
                pl.BlockSpec((NX * BLOCK, BLOCK), lambda k, s: (0, tile(k))),
            ],
            out_specs=[out] * 4
            + [
                pl.BlockSpec((NX * BLOCK, FF_TILE), lambda k, s: (0, 0)),
                pl.BlockSpec((NX * BLOCK, 2 * FF_TILE), lambda k, s: (0, 0)),
            ],
            scratch_shapes=[
                pltpu.VMEM((NX * BLOCK, 2048), BF16),
                pltpu.VMEM((NX * BLOCK, FF_TILE), BF16),
                pltpu.VMEM((NX * BLOCK, 2 * FF_TILE), BF16),
            ],
        ),
        out_shape=[jax.ShapeDtypeStruct((BLOCK, 2048), BF16)] * 4
        + [
            jax.ShapeDtypeStruct((NX * BLOCK, FF_TILE), BF16),
            jax.ShapeDtypeStruct((NX * BLOCK, 2 * FF_TILE), BF16),
        ],
        compiler_params=params("arbitrary"),
        cost_estimate=cost(1 << 20, 1 << 16),
        name="feed_forward",
    )(x[None], *n2, ffn, ffn, ffn, d_act)


def ffn_grads(sc, n0, n1, n2, n3, dgu_ref, act_ref, c0, c1, c2, c3, *rest):
    i = pl.program_id(0)
    added, outs, act_t, g_ref = rest[:-4], rest[-4:-2], rest[-2], rest[-1]

    def put(which, place, value):
        if added:
            value = value + added[which][place].astype(F32)
        outs[which][place] = value.astype(BF16)

    @pl.when(i < NX)
    def _():
        lhs = []
        for zhi in range(2):
            shard = (zhi * NX + jnp.minimum(i, NX - 1)) * 2 + sc[0]
            at = pl.ds(pl.multiple_of(shard * BLOCK, BLOCK), BLOCK)
            lhs.append(jnp.concatenate([n[:, at] for n in (n0, n1, n2, n3)], axis=0))
        lhs = jnp.concatenate(lhs, axis=1)
        for half in range(2):
            cols = slice(FF_TILE * half, FF_TILE * (half + 1))
            g_ref[:, :FF_TILE] = lax.dot_general(
                lhs, dgu_ref[:, cols], (((0,), (0,)), ((), ())), preferred_element_type=F32
            )
            for zhi in range(2):
                for zlo in range(2):
                    for y in range(4):
                        row = zhi * BLOCK + (zlo * 4 + y) * 16
                        part = g_ref[row : row + 16, :FF_TILE]
                        put(0, (y, zlo * 2 + zhi, slice(None), cols), part)

    @pl.when(i == NX)
    def _():
        act_t[...] = act_ref[...].T

    @pl.when(i >= NX)
    def _():
        lhs = []
        for p in range(2):
            for j in range(11):
                row = (2 * p + sc[0]) * 352 + 32 * j + 16 * (i - NX)
                lhs.append(act_t[pl.ds(pl.multiple_of(row, 16), 16), :])
        lhs = jnp.concatenate(lhs, axis=0)
        for zlo in range(2):
            cols = slice(1024 * zlo, 1024 * (zlo + 1))
            cots = jnp.concatenate([c[:, cols] for c in (c0, c1, c2, c3)], axis=0)
            g = jnp.dot(lhs, cots, preferred_element_type=F32)
            for p in range(2):
                for j in range(11):
                    row = p * 176 + 16 * j
                    for y in range(4):
                        part = g[row : row + 16, 256 * y : 256 * (y + 1)]
                        to = slice(256 * j, 256 * (j + 1))
                        put(1, (zlo * 2 + p, y, slice(None), to), part)


def call_ffn_grads(core, n2, d_gu, act, cots, *added):
    const = pl.BlockSpec((BLOCK, 2048), lambda i, s: (0, 0))
    tile = (4, 4, 16, 2 * FF_TILE)
    outs = [
        pl.BlockSpec(tile, lambda i, s: (0, 0, jnp.minimum(i, NX - 1), 0)),
        pl.BlockSpec(tile, lambda i, s: (0, 0, jnp.maximum(i - NX, 0), 0)),
    ]
    return pl.pallas_call(
        ffn_grads,
        grid_spec=pltpu.PrefetchScalarGridSpec(
            num_scalar_prefetch=1,
            grid=(NX + 2,),
            in_specs=[const] * 4
            + [pl.BlockSpec((NX * BLOCK, 2 * FF_TILE), lambda i, s: (0, 0))]
            + [pl.BlockSpec((NX * BLOCK, FF_TILE), lambda i, s: (0, 0))]
            + [const] * 4
            + outs[: len(added)],
            out_specs=outs,
            scratch_shapes=[
                pltpu.VMEM((FF_TILE, NX * BLOCK), BF16),
                pltpu.VMEM((2 * BLOCK, FF_TILE), F32),
            ],
        ),
        out_shape=[
            jax.ShapeDtypeStruct((4, 4, 64, 2 * FF_TILE), BF16),
            jax.ShapeDtypeStruct((4, 4, 32, 2 * FF_TILE), BF16),
        ],
        compiler_params=params("arbitrary"),
        cost_estimate=cost(1 << 33, 1 << 20),
        name="ffn_grads_mine" if added else "ffn_grads_other",
    )(core[None], *n2, d_gu, act, *cots, *added)


def attention_grads(sc, n_ref, dq_ref, o_ref, db_ref, *rest):
    added, out_ref, qkv_s, out_s = rest[:-3], rest[-3], rest[-2], rest[-1]

    def put(place, value):
        if added:
            value = value + added[0][place].astype(F32)
        out_ref[place] = value.astype(BF16)

    for zhi in range(2):
        lhs = []
        for x in range(NX):
            at = pl.ds(pl.multiple_of(((zhi * NX + x) * 2 + sc[0]) * BLOCK, BLOCK), BLOCK)
            lhs.append(n_ref[:, at])
        lhs = jnp.concatenate(lhs, axis=1)
        qkv_s[...] = lax.dot_general(
            lhs, dq_ref[...], (((0,), (1,)), ((), ())), preferred_element_type=F32
        )
        for x in range(NX):
            for replica in range(8):
                row = BLOCK * x + 16 * replica
                to = slice(16 * x, 16 * (x + 1))
                put((replica % 4, replica // 4 * 2 + zhi, to, slice(0, 640)), qkv_s[row : row + 16, :])
    for p in range(2):
        rows = o_ref[pl.ds(pl.multiple_of((2 * p + sc[0]) * BLOCK, BLOCK), BLOCK), :]
        out_s[...] = jnp.dot(rows, db_ref[...], preferred_element_type=F32)
        for replica in range(8):
            for half in range(2):
                part = out_s[64 * half : 64 * (half + 1), 256 * replica : 256 * (replica + 1)]
                at = 640 + 256 * half
                put((replica % 4, replica // 4 * 2 + p, slice(None), slice(at, at + 256)), part)


def call_attention_grads(core, n1, d_qkv, ob, d_br, *added):
    vmem = pl.BlockSpec(memory_space=pltpu.VMEM)
    return pl.pallas_call(
        attention_grads,
        in_specs=[pl.BlockSpec(memory_space=pltpu.SMEM)] + [vmem] * (4 + len(added)),
        out_specs=vmem,
        out_shape=jax.ShapeDtypeStruct((4, 4, 64, 1152), BF16),
        scratch_shapes=[pltpu.VMEM((4 * BLOCK, 640), F32), pltpu.VMEM((BLOCK, 2048), F32)],
        compiler_params=params(),
        cost_estimate=cost(1 << 33, 1 << 20),
        name="attention_grads_mine" if added else "attention_grads_other",
    )(core[None], n1, d_qkv, ob, d_br, *added)


def shift_x(a, k):
    return lax.ppermute(a, "x", [(i, (i + k) % NX) for i in range(NX)])


def gathered_x(a, between=lambda: ()):
    half = a.shape[0] // 2
    t1, t3 = shift_x(a, 3), shift_x(a, 1)
    t1, t3 = lax.optimization_barrier((t1, t3, *between()))[:2]
    return [a, t1, jnp.concatenate([shift_x(t1[:half], 3), shift_x(t3[half:], 1)]), t3]


def moved_x(parts):
    half = parts[2].shape[0] // 2
    up, down = shift_x(parts[2][:half], 1), shift_x(parts[2][half:], 3)
    up = (parts[1][:half].astype(F32) + up.astype(F32)).astype(BF16)
    down = (parts[3][half:].astype(F32) + down.astype(F32)).astype(BF16)
    up = jnp.concatenate([up, parts[1][half:]])
    down = jnp.concatenate([parts[3][:half], down])
    return [parts[0], shift_x(up, 1), shift_x(down, 3)]


def added(parts):
    return sum(p.astype(F32) for p in parts)


def summed_x(parts):
    return added(moved_x(parts))


def sent(parts, axes, me=0):
    out = []
    for j in range(4):
        part = lax.dynamic_index_in_dim(parts, (me + j) % 4, 0, keepdims=False)
        out.append(lax.ppermute(part, axes, [(i, (i + j) % 4) for i in range(4)]) if j else part)
    return out


def total(parts):
    return parts.astype(F32).sum(axis=0).astype(BF16)


def pieces(a):
    return [a[BLOCK * j : BLOCK * (j + 1)] for j in range(NX)]


def summed(t, axes):
    return exchange(t, axes).astype(F32).sum(axis=0).astype(BF16)


def to_heads(first):
    pairs = []
    for s_zhi in range(2):
        for s_x in range(NX):
            d_zhi = s_x % 2 if first else 1 - s_x % 2
            pairs.append((s_zhi * NX + s_x, d_zhi * NX + 2 * s_zhi + s_x // 2))
    return pairs


def to_owners(first):
    return [(d, s) for s, d in to_heads(first)]


def after(a, *others):
    return lax.optimization_barrier((a, *others))[0]


def body(tok, cot, starts, gain_1, w_qkv, w_out, gain_2, w_gu, w_dn):
    zlo, y, zhi, x, core = (lax.axis_index(a) for a in AXES)
    replica = zlo * 4 + y
    rows, dim = tok.shape
    q_cols = GROUP * HEAD_SIZE
    ff_shard = w_dn.shape[0]
    slab = rows // 8

    t1, t3 = shift_x(tok, 3), shift_x(tok, 1)
    toks = [tok, t1, shift_x(t1[: rows // 2], 3), shift_x(t3[rows // 2 :], 1), t3]
    w_far = swap(w_out, "zhi")
    place = jnp.stack([replica, x])
    wide, gu_slab, dn_slab = call_pack(place, w_qkv, gain_1, gain_2, starts, w_gu, w_dn)
    qkv_cols = wide.shape[2]
    wide = exchange(wide, CHIP)

    gu_slab = jnp.concatenate(sent(gu_slab, "x"), axis=0)
    dn_slab = lax.ppermute(dn_slab, CHIP, to_heads(True))
    slabs = jnp.concatenate([gu_slab, dn_slab])
    slabs = after(slabs, wide, t1, t3)
    ffn = lax.all_gather(slabs, YZC, axis=0)
    ffn = ffn.reshape(8, 2, 2, NX * slab + 32, 2 * FF_TILE)

    inputs = tok.astype(F32)
    scaled_one, rstd_one = rms_forward(inputs)
    blocks = (x + jnp.arange(NX, dtype=jnp.int32)) % NX
    block_ids = zhi * 8 + 2 * blocks + core
    st = lax.dynamic_slice_in_dim(wide, zhi * NX, NX, 0)[:, rows, 2 * rows : 4 * rows]
    st = st.astype(F32).reshape(NX, 2, rows)
    st = (st[:, 0] * 256.0 + st[:, 1]).astype(jnp.int32)[blocks]
    where_at = block_ids[:, None] * rows + jnp.arange(rows, dtype=jnp.int32)[None, :]
    pos = (where_at - st).reshape(1, NX * rows).astype(F32)
    freqs = jnp.exp(jnp.arange(32, dtype=F32) * (-2.0 * math.log(ROPE_BASE) / HEAD_SIZE))
    angles = freqs[:, None] * pos
    cos, sin = jnp.cos(angles), jnp.sin(angles)
    n1, q_t, kv, wq, gains = call_project(core[None], toks, wide, swap(wide, "core"), cos, sin)
    gain_one, gain_two = gains[0], gains[1]
    kv = jnp.concatenate([kv, swap(kv, "core")], axis=0)
    near, far = jnp.where(zhi == 0, w_out, w_far), jnp.where(zhi == 0, w_far, w_out)
    even = x % 2 == 0
    part_a, part_b = jnp.where(even, near, far), jnp.where(even, far, near)
    part_a, part_b, cot_in = lax.optimization_barrier((part_a, part_b, cot, kv))[:3]
    kv = jnp.concatenate([kv, swap(kv, "zhi")], axis=0)
    part_a = lax.ppermute(part_a, "x", [(0, 0), (1, 2), (2, 1), (3, 3)])
    part_b = lax.ppermute(part_b, "x", [(0, 2), (1, 0), (2, 3), (3, 1)])
    firsts = jnp.min(st, axis=1) // CHUNK
    clears = (jnp.max(st, axis=1) + CHUNK - 1) // CHUNK
    sc = jnp.concatenate([zhi[None], x[None], core[None], firsts, clears]).astype(jnp.int32)
    st = st[:, None, :]
    o, ob, qr, lse = call_forward(sc, q_t, cos, sin, st, kv)
    cots = [cot_in, shift_x(cot_in, 3), shift_x(cot_in, 2), shift_x(cot_in, 1)]
    ob, *cots = lax.optimization_barrier((ob, *cots))
    part_a, part_b = after(part_a, ob), after(part_b, ob)
    *parts, wo = call_out_project(
        jnp.stack([x // 2, core]), ob, part_a, part_b, swap(part_a, "core"), swap(part_b, "core")
    )
    hidden = inputs + summed_x(parts)

    d_act, wdn = call_down_back(cots, ffn)
    scaled_two, rstd_two = rms_forward(hidden)
    n2 = gathered_x((scaled_two * gain_two[None, :]).astype(BF16))
    *d_n2, act, d_gu = call_feed_forward(x, n2, ffn, d_act)

    other = call_ffn_grads(1 - core, n2, d_gu, act, cots)
    d_n2 = moved_x(d_n2)
    other = lax.optimization_barrier((*other, *d_n2[1:]))[:2]
    other = [swap(g, "core") for g in other]
    g_gu, g_dn = call_ffn_grads(core, n2, d_gu, act, cots, *other)
    d_mid, gain_two_term = rms_backward(added(d_n2), scaled_two, rstd_two, gain_two)
    d_mid = cot.astype(F32) + d_mid
    d_br = gathered_x(d_mid.astype(BF16), lambda: (g_gu, g_dn))
    z = zlo * 2 + zhi
    g_gu = exchange(g_gu.reshape(4, 4 * 64, 2 * FF_TILE), "y")
    g_dn = sent(g_dn, ("zlo", "zhi"), z)
    d_br = jnp.concatenate(d_br)

    do = mm(wo, d_br, ((1,), (1,)), BF16)
    dq, dkv = call_backward(sc, qr, do, o, lse, cos, sin, st, kv)
    dkv, *g_dn = lax.optimization_barrier((dkv, *g_dn))
    dkv = dkv.reshape(2, 2, NX, 2 * HEAD_SIZE, rows)
    dkv = dkv[:, 0].astype(F32) + swap(dkv[:, 1], "core").astype(F32)
    dkv = dkv[0] + swap(dkv[1].astype(BF16), "zhi").astype(F32)
    g_dn = added(g_dn).astype(BF16)
    dkv = dkv.transpose(1, 0, 2).reshape(2 * HEAD_SIZE, NX * rows)
    k1, k2 = dkv[:32], dkv[32:64]
    dkv = jnp.concatenate([k1 * cos + k2 * sin, k2 * cos - k1 * sin, dkv[64:]], axis=0)
    d_qkv = jnp.concatenate([dq, dkv.astype(BF16)], axis=0)
    d_qkv, g_gu = lax.optimization_barrier((d_qkv, g_gu))
    g_gu = exchange(total(g_gu.reshape(4, 4, 64, 2 * FF_TILE)), ("zlo", "zhi"))
    d_n1 = mm(d_qkv, wq, ((0,), (1,)), BF16)
    d_qkv, ob, g_dn = lax.optimization_barrier((d_qkv, ob, g_dn, d_n1))[:3]
    d_n1 = moved_x(pieces(d_n1))
    other = swap(call_attention_grads(1 - core, n1, d_qkv, ob, d_br), "core")
    g_attn = call_attention_grads(core, n1, d_qkv, ob, d_br, other)
    g_dn = sent(g_dn, "y", y)

    g_gu = after(g_gu, g_attn)
    g_attn = sent(g_attn, "y", y)
    d_n1 = lax.optimization_barrier((*d_n1, *g_attn))[:3]
    act = after(act, *d_n1)
    mixed = moved_x(pieces(mm(act, wdn, ((1,), (0,)), BF16)))
    d_in, gain_one_term = rms_backward(added(d_n1), scaled_one, rstd_one, gain_one)
    input_grad = (d_mid + d_in).astype(BF16)
    g_attn = sent(added(g_attn).astype(BF16), ("zlo", "zhi"), z)
    g_gu = exchange(total(g_gu).reshape(NX, slab, 2 * FF_TILE), "x")
    g_dn = lax.ppermute(added(g_dn).astype(BF16), CHIP, to_owners(True))
    both = [g_gu[j] for j in range(NX)] + [g_dn[:slab], g_dn[slab:]]
    g_attn = added(g_attn).astype(BF16)
    g_out = lax.ppermute(g_attn[:, 640:], CHIP, to_owners(True))
    g_out = [g_out[slab * j : slab * (j + 1), 256 * h : 256 * h + 256] for h in (0, 1) for j in range(4)]
    g_qkv = exchange(g_attn[:, :640].reshape(NX, slab, qkv_cols), "x")
    terms = jnp.stack([gain_one_term, gain_two_term]).reshape(2, 16, rows).transpose(1, 0, 2)
    terms = exchange(terms, SHARD).sum(axis=0).reshape(1, 2 * rows)
    terms = jnp.broadcast_to(terms, (slab, 2 * rows)).astype(BF16)
    both += [g_qkv[j] for j in range(NX)] + g_out + [terms]
    both = lax.all_gather(jnp.concatenate(both, axis=1), REP, axis=0)
    g_gu, g_dn, g_qkv, g_out, terms = call_spread(both)
    mixed = hidden + added(mixed)

    return (
        mixed.astype(BF16),
        input_grad,
        terms[0],
        g_qkv,
        g_out,
        terms[1],
        g_gu,
        g_dn,
    )


def solution(mesh):
    fine = Mesh(mesh.devices.reshape(2, 4, 2, 4, 2), AXES)
    row, two = P(AXES), P(AXES, None)
    vec, mat = P(SHARD), P(SHARD, None)
    return jax.shard_map(
        body,
        mesh=fine,
        in_specs=(two, two, row, vec, mat, mat, vec, mat, mat),
        out_specs=(two, two, vec, mat, mat, vec, mat, mat),
        check_vma=False,
    )
```

time: 867 us -> 576 us (0.66)
  blocking collectives: 139 us -> 0 us
  Pallas kernels: 20 us -> 103 us
  local copies, waits for them, and re-layouts: 132 us -> 54.9 us
  matrix products: 83.4 us -> 11.3 us
  waiting for transfers between devices: 233 us -> 204 us
  other arithmetic: 64.8 us -> 36.2 us
  starting transfers between devices: 166 us -> 141 us
    all_to_all x6 -> x0, blocking collectives: 139 us -> none  [exchange(): return lax.all_to_all(a, axes, split_axis=0, concat_axis=0, tiled=True)]
    all_to_all x20 -> x6, waiting for transfers between devices: 151 us -> 28 us  [exchange(): return lax.all_to_all(a, axes, split_axis=0, concat_axis=0, tiled=True)]
    all_to_all x20 -> x6, starting transfers between devices: 121 us -> 32.8 us  [exchange(): return lax.all_to_all(a, axes, split_axis=0, concat_axis=0, tiled=True)]
    pallas_call x0 -> x10, Pallas kernels: none -> 83.3 us  [the longest x1 25 us: call_feed_forward(): pl.pallas_call(feed_forward, grid_spec=pltpu.PrefetchScalarGridSpec(num_s...]
    ppermute x4 -> x51, starting transfers between devices: 7.86 us -> 81.1 us  [the longest x31 50.9 us: shift_x(): return lax.ppermute(a, 'x', [(i, (i + k) % NX) for i in range(NX)])]
    dot_general x12 -> x3, matrix products: 83.4 us -> 11.3 us  [mm(): lax.dot_general(left, right, ((dims[0], dims[1]), ((), ())), preferred_el...]
    ppermute x4 -> x51, waiting for transfers between devices: 63.1 us -> 120 us  [the longest x15 57.2 us: sent(): lax.ppermute(part, axes, [(i, (i + j) % 4) for i in range(4)])]
    reshape x13 -> x0, local copies, waits for them, and re-layouts: 53.6 us -> none  [the longest x2 17.2 us: body(): g_dn = g_dn.reshape(2, 2, ff_shard, 2, 4, 256).transpose(1, 3, 4, 0, 2, 5)]
  transfers between devices with their start and end apart: 33 -> 70, of which waited for: 20 -> 33; matrix products, arithmetic and copies ran while one was open for 27% -> 12% of each run, Pallas kernels for 2% -> 10%
where the time goes in v2:
time: 576 us; the launch traced here: 566 us
  waiting for transfers between devices  204 us (35%)
  starting transfers between devices  141 us (24%)
  Pallas kernels  103 us (18%)
  local copies, waits for them, and re-layouts  54.9 us (10%)
  other arithmetic  36.2 us (6%)
  between operations  15.4 us (3%)
  matrix products  11.3 us (2%)
    ppermute x15, waiting for transfers between devices, sent(): lax.ppermute(part, axes, [(i, (i + j) % 4) for i in range(4)])  57.2 us
    ppermute x31, waiting for transfers between devices, shift_x(): return lax.ppermute(a, 'x', [(i, (i + k) % NX) for i in range(NX)])  54.3 us
    ppermute x31, starting transfers between devices, shift_x(): return lax.ppermute(a, 'x', [(i, (i + k) % NX) for i in range(NX)])  50.9 us
    unnamed x131, local copies, waits for them, and re-layouts  37.4 us
    all_gather x1, waiting for transfers between devices, body(): both = lax.all_gather(jnp.concatenate(both, axis=1), REP, axis=0)  37.3 us
    all_to_all x6, starting transfers between devices, exchange(): return lax.all_to_all(a, axes, split_axis=0, concat_axis=0, tiled=True)  32.8 us
    all_to_all x6, waiting for transfers between devices, exchange(): return lax.all_to_all(a, axes, split_axis=0, concat_axis=0, tiled=True)  28 us
    ppermute x11, starting transfers between devices, swap(): return lax.ppermute(a, axis, [(0, 1), (1, 0)])  27.2 us
  transfers between devices with their start and end apart: 70, of which 33 were waited for; matrix products, arithmetic and copies ran while one was open for 12% of the time, Pallas kernels for 10%

profile of v2, /device:TPU:1, one launch (start us, length us, event | category | flops | bytes accessed | tf_op | source)
XLA Modules:
  0.0 566.0 jit_solution(18140113174293143112)
XLA Ops:
  18.5 7.3 %all-to-all-start = ((bf16[8,144,640]{2,1,0:T(8,128)(2,1)}), bf16[8,144,640]{2,1,0:T(8,128)(2,1)S(1)}, u32[]{:S(2)}, u32[]{:S(2)}) async-start(bf16[8,144,640]{2,1,0:T(8,128)(2,1)} %get-tuple-element.76), calls=%async_computation | async-start | bytes 2949120 | tf_op jit(solution)/shard_map/all_to_all | solution.py:35
  31.5 16.6 %collective-permute-done.23 = bf16[16,2816]{1,0:T(8,128)(2,1)S(1)} collective-permute-done((bf16[16,2816]{1,0:T(8,128)(2,1)S(1)}, bf16[16,2816]{1,0:T(8,128)(2,1)S(1)}, u32[]{:S(2)}, u32[]{:S(2)}) %collective-permute-start.23) | collective-permute-done | bytes 90144 | tf_op jit(solution)/shard_map/ppermute | solution.py:782
  53.3 9.8 %collective-permute-start.7 = (bf16[128,2048]{1,0:T(8,128)(2,1)}, bf16[128,2048]{1,0:T(8,128)(2,1)}, u32[]{:S(2)}, u32[]{:S(2)}) collective-permute-start(bf16[128,2048]{1,0:T(8,128)(2,1)} %param.14), channel_id=1, source_target_pairs={{0,8},{8,0},{1,9},{9,1},{2,10},{10,2},{3,11},{11,3},{4,12},{12,4},... | collective-permute-start | bytes 1572872 | tf_op jit(solution)/shard_map/ppermute | solution.py:43
  73.9 5.6 project.1
  92.2 5.6 collective-permute-done.6
  97.9 5.4 collective-permute-start.11
  103.4 8.6 %attention_forward.1 = (f32[512,512]{1,0:T(8,128)S(1)}, bf16[512,512]{1,0:T(8,128)(2,1)S(1)}, bf16[4,64,1024]{2,1,0:T(8,128)(2,1)S(1)}, f32[4,1,1024]{2,1,0:T(1,128)S(1)}) custom-call(s32[11]{0:T(128)S(1)} %concatenate.53.sc, f32[512,512]{1,0:T(8,128)S(1)} %copy-done.9, f32[32,512]{1,0:T(8,128)S(1)} %get-tuple-element.207.cos_ref, ...), custom_call_target="tpu_custom_call" | custom-call | flops 1048576 | bytes 65536 | tf_op jit(solution)/shard_map/attention_forward/pallas_call | solution.py:201
  113.6 8.7 %collective-permute-done.12.b_ref = bf16[128,2048]{1,0:T(8,128)(2,1)} collective-permute-done((bf16[128,2048]{1,0:T(8,128)(2,1)}, bf16[128,2048]{1,0:T(8,128)(2,1)}, u32[]{:S(2)}, u32[]{:S(2)}) %collective-permute-start.12) | collective-permute-done | bytes 524320 | tf_op jit(solution)/shard_map/ppermute | solution.py:859
  133.0 12.3 %collective-permute-start.15 = (bf16[64,2048]{1,0:T(8,128)(2,1)S(1)}, bf16[64,2048]{1,0:T(8,128)(2,1)S(1)}, u32[]{:S(2)}, u32[]{:S(2)}) collective-permute-start(bf16[64,2048]{1,0:T(8,128)(2,1)S(1)} %get-tuple-element.189), channel_id=1, source_target_pairs={{0,2},{2,4},{4,6},{6,0},{1,3},{3,5},{5,7},{7,1},{8,10},{10,12},{12... | collective-permute-start | bytes 786440 | tf_op jit(solution)/shard_map/ppermute | solution.py:750
  145.4 5.2 collective-permute-done.15
  154.3 9.9 %collective-permute-done.16 = bf16[128,2048]{1,0:T(8,128)(2,1)S(1)} collective-permute-done((bf16[128,2048]{1,0:T(8,128)(2,1)S(1)}, bf16[128,2048]{1,0:T(8,128)(2,1)S(1)}, u32[]{:S(2)}, u32[]{:S(2)}) %collective-permute-start.16) | collective-permute-done | bytes 524320 | tf_op jit(solution)/shard_map/ppermute | solution.py:750
  170.6 9.1 %collective-permute-done.19.n1 = bf16[128,2048]{1,0:T(8,128)(2,1)S(1)} collective-permute-done((bf16[128,2048]{1,0:T(8,128)(2,1)S(1)}, bf16[128,2048]{1,0:T(8,128)(2,1)S(1)}, u32[]{:S(2)}, u32[]{:S(2)}) %collective-permute-start.19) | collective-permute-done | bytes 524320 | tf_op jit(solution)/shard_map/ppermute | solution.py:750
  189.7 11.2 %down_back.1 = (f32[512,1408]{1,0:T(8,128)S(1)}, bf16[1408,2048]{1,0:T(8,128)(2,1)}) custom-call(bf16[128,2048]{1,0:T(8,128)(2,1)} %c0.2, bf16[128,2048]{1,0:T(8,128)(2,1)} %collective-permute-done.8.c1, bf16[128,2048]{1,0:T(8,128)(2,1)} %collective-permute-done.9.c2, bf16[128,2048]{1,0:T(8,128)(2,1)} %collective-permute-done.10.c3, ...), custom_call_target="tpu_custom_call" | custom-call | flops 8589934592 | bytes 1048576 | tf_op jit(solution)/shard_map/down_back/pallas_call | solution.py:496
  203.6 25.0 %feed_forward.1 = (bf16[128,2048]{1,0:T(8,128)(2,1)S(1)}, bf16[128,2048]{1,0:T(8,128)(2,1)S(1)}, bf16[128,2048]{1,0:T(8,128)(2,1)S(1)}, bf16[128,2048]{1,0:T(8,1...) custom-call(s32[1]{0:T(128)} %bitcast.3.sc, bf16[128,2048]{1,0:T(8,128)(2,1)S(1)} %multiply_convert_fusion.n0, ...), custom_call_target="tpu_custom_call" | custom-call | flops 1048576 | bytes 65536 | tf_op jit(solution)/shard_map/feed_forward/pallas_call | solution.py:582
  243.1 10.7 %ffn_grads_other.1 = (bf16[4,4,64,2816]{3,2,1,0:T(8,128)(2,1)}, bf16[4,4,32,2816]{3,2,1,0:T(8,128)(2,1)}) custom-call(s32[1]{0:T(128)} %bitcast.19.sc, bf16[128,2048]{1,0:T(8,128)(2,1)S(1)} %multiply_convert_fusion.n0, bf16[128,2048]{1,0:T(8,128)(2,1)S(1)} %collective-permute-done.19.n1, bf16[128,2048]{1,0:T(8,128)(2,1)S(1)} %copy-done.6, ...), custom_call_target="tpu_custom_call" | custom-call | flops 8589934592 | bytes 1048576 | tf_op jit(solution)/shard_map/ffn_grads_other/pallas_call | solution.py:677
  253.8 7.3 %collective-permute-start.33 = (bf16[4,4,64,2816]{3,2,1,0:T(8,128)(2,1)}, bf16[4,4,64,2816]{3,2,1,0:T(8,128)(2,1)}, u32[]{:S(2)}, u32[]{:S(2)}) collective-permute-start(bf16[4,4,64,2816]{3,2,1,0:T(8,128)(2,1)} %get-tuple-element.111), channel_id=1, source_target_pairs={{0,1},{1,0},{2,3},{3,2},{4,5},{5,4},{6,7},{7,6},{8,9},{9,8},{10,11... | collective-permute-start | bytes 17301512 | tf_op jit(solution)/shard_map/ppermute | solution.py:43
  268.1 6.5 %collective-permute-done.34.rest_1_ = bf16[4,4,32,2816]{3,2,1,0:T(8,128)(2,1)} collective-permute-done((bf16[4,4,32,2816]{3,2,1,0:T(8,128)(2,1)}, bf16[4,4,32,2816]{3,2,1,0:T(8,128)(2,1)}, u32[]{:S(2)}, u32[]{:S(2)}) %collective-permute-start.34) | collective-permute-done | bytes 2883616 | tf_op jit(solution)/shard_map/ppermute | solution.py:43
  274.6 12.6 %ffn_grads_mine.1 = (bf16[4,4,64,2816]{3,2,1,0:T(8,128)(2,1)}, bf16[4,4,32,2816]{3,2,1,0:T(8,128)(2,1)}) custom-call(s32[1]{0:T(128)} %bitcast.1.sc, bf16[128,2048]{1,0:T(8,128)(2,1)S(1)} %multiply_convert_fusion.n0, bf16[128,2048]{1,0:T(8,128)(2,1)S(1)} %collective-permute-done.19.n1, bf16[128,2048]{1,0:T(8,128)(2,1)S(1)} %copy-done.7, ...), custom_call_target="tpu_custom_call" | custom-call | flops 8589934592 | bytes 1048576 | tf_op jit(solution)/shard_map/ffn_grads_mine/pallas_call | solution.py:677
  290.9 5.1 all-to-all-start.1
  304.6 10.7 %attention_backward.1 = (bf16[512,512]{1,0:T(8,128)(2,1)S(1)}, bf16[16,128,128]{2,1,0:T(8,128)(2,1)S(1)}) custom-call(s32[11]{0:T(128)S(1)} %concatenate.53.sc, bf16[4,64,1024]{2,1,0:T(8,128)(2,1)S(1)} %copy-done.20, bf16[512,512]{1,0:T(8,128)(2,1)S(1)} %convolution_convert_fusion.2.do_ref, f32[512,512]{1,0:T(8,128)S(1)} %copy-done.11, ...), custom_call_target="tpu_custom_call" | custom-call | flops 1048576 | bytes 65536 | tf_op jit(solution)/shard_map/attention_backward/pallas_call | solution.py:240
  316.7 14.7 %collective-permute-done.38 = bf16[4,32,2816]{2,1,0:T(8,128)(2,1)S(1)} collective-permute-done((bf16[4,32,2816]{2,1,0:T(8,128)(2,1)S(1)}, bf16[4,32,2816]{2,1,0:T(8,128)(2,1)S(1)}, u32[]{:S(2)}, u32[]{:S(2)}) %collective-permute-start.38) | collective-permute-done | bytes 720928 | tf_op jit(solution)/shard_map/ppermute | solution.py:782
  344.6 16.3 %all-to-all-done.1 = bf16[4,256,2816]{2,1,0:T(8,128)(2,1)} async-done(((bf16[4,256,2816]{2,1,0:T(8,128)(2,1)}), bf16[4,256,2816]{2,1,0:T(8,128)(2,1)}, u32[]{:S(2)}, u32[]{:S(2)}) %all-to-all-start.1) | async-done | bytes 5767200 | tf_op jit(solution)/shard_map/all_to_all | solution.py:35
  374.9 5.0 reduce_sum.93
  405.5 6.0 %all-to-all-start.3 = ((bf16[4,16,2816]{2,1,0:T(8,128)(2,1)}), bf16[4,16,2816]{2,1,0:T(8,128)(2,1)S(1)}, u32[]{:S(2)}, u32[]{:S(2)}) async-start(bf16[4,16,2816]{2,1,0:T(8,128)(2,1)} %bitcast.37), calls=%async_computation.3 | async-start | bytes 720896 | tf_op jit(solution)/shard_map/all_to_all | solution.py:35
  420.0 9.5 %collective-permute-done.47 = bf16[4,64,1152]{2,1,0:T(8,128)(2,1)} collective-permute-done((bf16[4,64,1152]{2,1,0:T(8,128)(2,1)}, bf16[4,64,1152]{2,1,0:T(8,128)(2,1)}, u32[]{:S(2)}, u32[]{:S(2)}) %collective-permute-start.47) | collective-permute-done | bytes 589856 | tf_op jit(solution)/shard_map/ppermute | solution.py:782
  429.5 12.4 %collective-permute-done.48 = bf16[4,64,1152]{2,1,0:T(8,128)(2,1)} collective-permute-done((bf16[4,64,1152]{2,1,0:T(8,128)(2,1)}, bf16[4,64,1152]{2,1,0:T(8,128)(2,1)}, u32[]{:S(2)}, u32[]{:S(2)}) %collective-permute-start.48) | collective-permute-done | bytes 589856 | tf_op jit(solution)/shard_map/ppermute | solution.py:782
  450.5 7.6 %all-to-all-start.5 = ((f32[16,2,128]{2,1,0:T(2,128)}), f32[16,2,128]{2,1,0:T(2,128)S(1)}, u32[]{:S(2)}, u32[]{:S(2)}) async-start(f32[16,2,128]{2,1,0:T(2,128)} %maximum_bitcast_fusion), calls=%async_computation.5 | async-start | bytes 32768 | tf_op jit(solution)/shard_map/all_to_all | solution.py:35
  459.7 5.6 all-to-all-done.5
  481.1 6.3 %convolution_convert_fusion = bf16[512,2048]{1,0:T(8,128)(2,1)S(1)} fusion(bf16[512,1408]{1,0:T(8,128)(2,1)S(1)} %copy-done.37, bf16[1408,2048]{1,0:T(8,128)(2,1)} %get-tuple-element.135), kind=kOutput, calls=%fused_computation.1 | convolution fusion | flops 2953838592 | bytes 9306112 | tf_op jit(solution)/shard_map/dot_general | solution.py:53
  504.0 7.0 %collective-permute-done.51 = bf16[128,2048]{1,0:T(8,128)(2,1)S(1)} collective-permute-done((bf16[128,2048]{1,0:T(8,128)(2,1)S(1)}, bf16[128,2048]{1,0:T(8,128)(2,1)S(1)}, u32[]{:S(2)}, u32[]{:S(2)}) %collective-permute-start.51) | collective-permute-done | bytes 524320 | tf_op jit(solution)/shard_map/ppermute | solution.py:750
  513.3 37.3 %all-gather.7.cloned.1.call-done = bf16[128,21760]{1,0:T(8,128)(2,1)} async-done(((bf16[16,21760]{1,0:T(8,128)(2,1)}), bf16[128,21760]{1,0:T(8,128)(2,1)}) %all-gather.7.cloned.1.call-update) | async-done | bytes 5570576 | tf_op jit(solution)/shard_map/all_gather | solution.py:930
  553.2 5.0 spread.1
  (342 shorter events, 224.8 us)
Async XLA Ops:
  7.2 45.2 %collective-permute-start = (bf16[128,2048]{1,0:T(8,128)(2,1)}, bf16[128,2048]{1,0:T(8,128)(2,1)S(1)}, u32[]{:S(2)}, u32[]{:S(2)}) collective-permute-start(bf16[128,2048]{1,0:T(8,128)(2,1)} %t0.1), channel_id=1, source_target_pairs={{0,6},{2,0},{4,2},{6,4},{1,7},{3,1},{5,3},{7,5},{8,14},{10,8},{12,... | collective-permute-start | bytes 1572872 | tf_op jit(solution)/shard_map/ppermute | solution.py:750
  10.5 41.8 %collective-permute-start.2 = (bf16[128,2048]{1,0:T(8,128)(2,1)}, bf16[128,2048]{1,0:T(8,128)(2,1)S(1)}, u32[]{:S(2)}, u32[]{:S(2)}) collective-permute-start(bf16[128,2048]{1,0:T(8,128)(2,1)} %t0.1), channel_id=1, source_target_pairs={{0,2},{2,4},{4,6},{6,0},{1,3},{3,5},{5,7},{7,1},{8,10},{10,12},{12... | collective-permute-start | bytes 1572872 | tf_op jit(solution)/shard_map/ppermute | solution.py:750
  18.5 33.8 %all-to-all-start = ((bf16[8,144,640]{2,1,0:T(8,128)(2,1)}), bf16[8,144,640]{2,1,0:T(8,128)(2,1)S(1)}, u32[]{:S(2)}, u32[]{:S(2)}) async-start(bf16[8,144,640]{2,1,0:T(8,128)(2,1)} %get-tuple-element.76), calls=%async_computation | async-start | bytes 2949120 | tf_op jit(solution)/shard_map/all_to_all | solution.py:35
  25.8 164.0 %all-gather.5.cloned.1.call-start = ((), (), s32[]{:S(2)}) async-start(), calls=%async_computation.6 | async-start | bytes 17842176 | tf_op jit(solution)/shard_map/all_gather | solution.py:835
  25.8 22.3 %collective-permute-start.23 = (bf16[16,2816]{1,0:T(8,128)(2,1)S(1)}, bf16[16,2816]{1,0:T(8,128)(2,1)S(1)}, u32[]{:S(2)}, u32[]{:S(2)}) collective-permute-start(bf16[16,2816]{1,0:T(8,128)(2,1)S(1)} %get-tuple-element.193), channel_id=1, source_target_pairs={{0,2},{2,4},{4,6},{6,0},{1,3},{3,5},{5,7},{7,1},{8,10},{10,12},{12... | collective-permute-start | bytes 270344 | tf_op jit(solution)/shard_map/ppermute | solution.py:782
  27.3 23.0 %collective-permute-start.24 = (bf16[16,2816]{1,0:T(8,128)(2,1)S(1)}, bf16[16,2816]{1,0:T(8,128)(2,1)S(1)}, u32[]{:S(2)}, u32[]{:S(2)}) collective-permute-start(bf16[16,2816]{1,0:T(8,128)(2,1)S(1)} %get-tuple-element.192), channel_id=1, source_target_pairs={{0,4},{2,6},{4,0},{6,2},{1,5},{3,7},{5,1},{7,3},{8,12},{10,14},{12... | collective-permute-start | bytes 270344 | tf_op jit(solution)/shard_map/ppermute | solution.py:782
  29.7 21.3 %collective-permute-start.25 = (bf16[16,2816]{1,0:T(8,128)(2,1)S(1)}, bf16[16,2816]{1,0:T(8,128)(2,1)S(1)}, u32[]{:S(2)}, u32[]{:S(2)}) collective-permute-start(bf16[16,2816]{1,0:T(8,128)(2,1)S(1)} %get-tuple-element.191), channel_id=1, source_target_pairs={{0,6},{2,0},{4,2},{6,4},{1,7},{3,1},{5,3},{7,5},{8,14},{10,8},{12,... | collective-permute-start | bytes 270344 | tf_op jit(solution)/shard_map/ppermute | solution.py:782
  52.4 21.5 %collective-permute-start.4 = (bf16[8,144,640]{2,1,0:T(8,128)(2,1)S(1)}, bf16[8,144,640]{2,1,0:T(8,128)(2,1)}, u32[]{:S(2)}, u32[]{:S(2)}) collective-permute-start(bf16[8,144,640]{2,1,0:T(8,128)(2,1)S(1)} %all-to-all-done.mine), channel_id=1, source_target_pairs={{0,1},{1,0},{2,3},{3,2},{4,5},{5,4},{6,7},{7,6},{8,9},{9,8},{10,11... | collective-permute-start | bytes 4423688 | tf_op jit(solution)/shard_map/ppermute | solution.py:43
  53.3 31.0 %collective-permute-start.7 = (bf16[128,2048]{1,0:T(8,128)(2,1)}, bf16[128,2048]{1,0:T(8,128)(2,1)}, u32[]{:S(2)}, u32[]{:S(2)}) collective-permute-start(bf16[128,2048]{1,0:T(8,128)(2,1)} %param.14), channel_id=1, source_target_pairs={{0,8},{8,0},{1,9},{9,1},{2,10},{10,2},{3,11},{11,3},{4,12},{12,4},... | collective-permute-start | bytes 1572872 | tf_op jit(solution)/shard_map/ppermute | solution.py:43
  86.6 27.0 %collective-permute-start.10 = (bf16[128,2048]{1,0:T(8,128)(2,1)}, bf16[128,2048]{1,0:T(8,128)(2,1)}, u32[]{:S(2)}, u32[]{:S(2)}) collective-permute-start(bf16[128,2048]{1,0:T(8,128)(2,1)} %c0.2), channel_id=1, source_target_pairs={{0,2},{2,4},{4,6},{6,0},{1,3},{3,5},{5,7},{7,1},{8,10},{10,12},{12... | collective-permute-start | bytes 1572872 | tf_op jit(solution)/shard_map/ppermute | solution.py:750
  86.6 27.0 %collective-permute-start.8 = (bf16[128,2048]{1,0:T(8,128)(2,1)}, bf16[128,2048]{1,0:T(8,128)(2,1)}, u32[]{:S(2)}, u32[]{:S(2)}) collective-permute-start(bf16[128,2048]{1,0:T(8,128)(2,1)} %c0.2), channel_id=1, source_target_pairs={{0,6},{2,0},{4,2},{6,4},{1,7},{3,1},{5,3},{7,5},{8,14},{10,8},{12,... | collective-permute-start | bytes 1572872 | tf_op jit(solution)/shard_map/ppermute | solution.py:750
  89.3 24.3 %collective-permute-start.9 = (bf16[128,2048]{1,0:T(8,128)(2,1)}, bf16[128,2048]{1,0:T(8,128)(2,1)}, u32[]{:S(2)}, u32[]{:S(2)}) collective-permute-start(bf16[128,2048]{1,0:T(8,128)(2,1)} %c0.2), channel_id=1, source_target_pairs={{0,4},{2,6},{4,0},{6,2},{1,5},{3,7},{5,1},{7,3},{8,12},{10,14},{12... | collective-permute-start | bytes 1572872 | tf_op jit(solution)/shard_map/ppermute | solution.py:750
  89.3 33.0 %collective-permute-start.12 = (bf16[128,2048]{1,0:T(8,128)(2,1)}, bf16[128,2048]{1,0:T(8,128)(2,1)}, u32[]{:S(2)}, u32[]{:S(2)}) collective-permute-start(bf16[128,2048]{1,0:T(8,128)(2,1)} %get-tuple-element.84), channel_id=1, source_target_pairs={{0,4},{2,0},{4,6},{6,2},{1,5},{3,1},{5,7},{7,3},{8,12},{10,8},{12,... | collective-permute-start | bytes 1572872 | tf_op jit(solution)/shard_map/ppermute | solution.py:859
  97.9 25.9 %collective-permute-start.11 = (bf16[128,2048]{1,0:T(8,128)(2,1)}, bf16[128,2048]{1,0:T(8,128)(2,1)}, u32[]{:S(2)}, u32[]{:S(2)}) collective-permute-start(bf16[128,2048]{1,0:T(8,128)(2,1)} %get-tuple-element.82), channel_id=1, source_target_pairs={{0,0},{2,4},{4,2},{6,6},{1,1},{3,5},{5,3},{7,7},{8,8},{10,12},{12,... | collective-permute-start | bytes 1572872 | tf_op jit(solution)/shard_map/ppermute | solution.py:858
  133.0 17.6 %collective-permute-start.15 = (bf16[64,2048]{1,0:T(8,128)(2,1)S(1)}, bf16[64,2048]{1,0:T(8,128)(2,1)S(1)}, u32[]{:S(2)}, u32[]{:S(2)}) collective-permute-start(bf16[64,2048]{1,0:T(8,128)(2,1)S(1)} %get-tuple-element.189), channel_id=1, source_target_pairs={{0,2},{2,4},{4,6},{6,0},{1,3},{3,5},{5,7},{7,1},{8,10},{10,12},{12... | collective-permute-start | bytes 786440 | tf_op jit(solution)/shard_map/ppermute | solution.py:750
  253.8 20.8 %collective-permute-start.33 = (bf16[4,4,64,2816]{3,2,1,0:T(8,128)(2,1)}, bf16[4,4,64,2816]{3,2,1,0:T(8,128)(2,1)}, u32[]{:S(2)}, u32[]{:S(2)}) collective-permute-start(bf16[4,4,64,2816]{3,2,1,0:T(8,128)(2,1)} %get-tuple-element.111), channel_id=1, source_target_pairs={{0,1},{1,0},{2,3},{3,2},{4,5},{5,4},{6,7},{7,6},{8,9},{9,8},{10,11... | collective-permute-start | bytes 17301512 | tf_op jit(solution)/shard_map/ppermute | solution.py:43
  266.7 20.6 %collective-permute-start.31 = (bf16[128,2048]{1,0:T(8,128)(2,1)S(1)}, bf16[128,2048]{1,0:T(8,128)(2,1)S(1)}, u32[]{:S(2)}, u32[]{:S(2)}) collective-permute-start(bf16[128,2048]{1,0:T(8,128)(2,1)S(1)} %get-tuple-element.153), channel_id=1, source_target_pairs={{0,6},{2,0},{4,2},{6,4},{1,7},{3,1},{5,3},{7,5},{8,14},{10,8},{12,... | collective-permute-start | bytes 1572872 | tf_op jit(solution)/shard_map/ppermute | solution.py:750
  266.7 20.6 %collective-permute-start.32 = (bf16[128,2048]{1,0:T(8,128)(2,1)S(1)}, bf16[128,2048]{1,0:T(8,128)(2,1)S(1)}, u32[]{:S(2)}, u32[]{:S(2)}) collective-permute-start(bf16[128,2048]{1,0:T(8,128)(2,1)S(1)} %get-tuple-element.153), channel_id=1, source_target_pairs={{0,2},{2,4},{4,6},{6,0},{1,3},{3,5},{5,7},{7,1},{8,10},{10,12},{12... | collective-permute-start | bytes 1572872 | tf_op jit(solution)/shard_map/ppermute | solution.py:750
  290.9 70.0 %all-to-all-start.1 = ((bf16[4,256,2816]{2,1,0:T(8,128)(2,1)}), bf16[4,256,2816]{2,1,0:T(8,128)(2,1)}, u32[]{:S(2)}, u32[]{:S(2)}) async-start(bf16[4,256,2816]{2,1,0:T(8,128)(2,1)} %bitcast.173), calls=%async_computation.1 | async-start | bytes 11534336 | tf_op jit(solution)/shard_map/all_to_all | solution.py:35
  298.6 18.1 %collective-permute-start.37 = (bf16[4,32,2816]{2,1,0:T(8,128)(2,1)S(1)}, bf16[4,32,2816]{2,1,0:T(8,128)(2,1)S(1)}, u32[]{:S(2)}, u32[]{:S(2)}) collective-permute-start(bf16[4,32,2816]{2,1,0:T(8,128)(2,1)S(1)} %get-tuple-element.159), channel_id=1, source_target_pairs={{0,8},{8,64},{64,72},{72,0},{1,9},{9,65},{65,73},{73,1},{2,10},{10... | collective-permute-start | bytes 2162696 | tf_op jit(solution)/shard_map/ppermute | solution.py:782
  299.9 31.5 %collective-permute-start.38 = (bf16[4,32,2816]{2,1,0:T(8,128)(2,1)S(1)}, bf16[4,32,2816]{2,1,0:T(8,128)(2,1)S(1)}, u32[]{:S(2)}, u32[]{:S(2)}) collective-permute-start(bf16[4,32,2816]{2,1,0:T(8,128)(2,1)S(1)} %get-tuple-element.158), channel_id=1, source_target_pairs={{0,64},{8,72},{64,0},{72,8},{1,65},{9,73},{65,1},{73,9},{2,66},{10... | collective-permute-start | bytes 2162696 | tf_op jit(solution)/shard_map/ppermute | solution.py:782
  300.6 32.5 %collective-permute-start.39 = (bf16[4,32,2816]{2,1,0:T(8,128)(2,1)S(1)}, bf16[4,32,2816]{2,1,0:T(8,128)(2,1)S(1)}, u32[]{:S(2)}, u32[]{:S(2)}) collective-permute-start(bf16[4,32,2816]{2,1,0:T(8,128)(2,1)S(1)} %get-tuple-element.157), channel_id=1, source_target_pairs={{0,72},{8,0},{64,8},{72,64},{1,73},{9,1},{65,9},{73,65},{2,74},{10... | collective-permute-start | bytes 2162696 | tf_op jit(solution)/shard_map/ppermute | solution.py:782
  367.7 29.8 %collective-permute-start.46 = (bf16[4,4,64,1152]{3,2,1,0:T(8,128)(2,1)}, bf16[4,4,64,1152]{3,2,1,0:T(8,128)(2,1)}, u32[]{:S(2)}, u32[]{:S(2)}) collective-permute-start(bf16[4,4,64,1152]{3,2,1,0:T(8,128)(2,1)} %attention_grads_other.1), channel_id=1, source_target_pairs={{0,1},{1,0},{2,3},{3,2},{4,5},{5,4},{6,7},{7,6},{8,9},{9,8},{10,11... | collective-permute-start | bytes 7077896 | tf_op jit(solution)/shard_map/ppermute | solution.py:43
  370.7 15.5 %collective-permute-start.55 = (bf16[32,2816]{1,0:T(8,128)(2,1)}, bf16[32,2816]{1,0:T(8,128)(2,1)}, u32[]{:S(2)}, u32[]{:S(2)}) collective-permute-start(bf16[32,2816]{1,0:T(8,128)(2,1)} %get-tuple-element.180), channel_id=1, source_target_pairs={{0,32},{16,48},{32,0},{48,16},{1,33},{17,49},{33,1},{49,17},{2,34}... | collective-permute-start | bytes 540680 | tf_op jit(solution)/shard_map/ppermute | solution.py:782
  374.9 16.3 %collective-permute-start.42 = (bf16[64,2048]{1,0:T(8,128)(2,1)}, bf16[64,2048]{1,0:T(8,128)(2,1)}, u32[]{:S(2)}, u32[]{:S(2)}) collective-permute-start(bf16[64,2048]{1,0:T(8,128)(2,1)} %get-tuple-element.173), channel_id=1, source_target_pairs={{0,2},{2,4},{4,6},{6,0},{1,3},{3,5},{5,7},{7,1},{8,10},{10,12},{12... | collective-permute-start | bytes 786440 | tf_op jit(solution)/shard_map/ppermute | solution.py:750
  379.9 24.6 %all-to-all-start.2 = ((bf16[4,64,2816]{2,1,0:T(8,128)(2,1)}), bf16[4,64,2816]{2,1,0:T(8,128)(2,1)S(1)}, u32[]{:S(2)}, u32[]{:S(2)}) async-start(bf16[4,64,2816]{2,1,0:T(8,128)(2,1)} %bitcast.36), calls=%async_computation.2 | async-start | bytes 2883584 | tf_op jit(solution)/shard_map/all_to_all | solution.py:35
  388.2 29.8 %collective-permute-start.57 = (bf16[32,2816]{1,0:T(8,128)(2,1)}, bf16[32,2816]{1,0:T(8,128)(2,1)}, u32[]{:S(2)}, u32[]{:S(2)}) collective-permute-start(bf16[32,2816]{1,0:T(8,128)(2,1)} %fusion.12), channel_id=1, source_target_pairs={{0,0},{8,2},{2,4},{10,6},{4,8},{12,10},{6,12},{14,14},{1,1},{9,3},... | collective-permute-start | bytes 540680 | tf_op jit(solution)/shard_map/ppermute | solution.py:920
  393.4 51.3 %collective-permute-start.45 = (bf16[128,2048]{1,0:T(8,128)(2,1)}, bf16[128,2048]{1,0:T(8,128)(2,1)}, u32[]{:S(2)}, u32[]{:S(2)}) collective-permute-start(bf16[128,2048]{1,0:T(8,128)(2,1)} %pad_maximum_fusion.6), channel_id=1, source_target_pairs={{0,6},{2,0},{4,2},{6,4},{1,7},{3,1},{5,3},{7,5},{8,14},{10,8},{12,... | collective-permute-start | bytes 1572872 | tf_op jit(solution)/shard_map/ppermute | solution.py:750
  397.5 47.1 %collective-permute-start.43 = (bf16[128,2048]{1,0:T(8,128)(2,1)}, bf16[128,2048]{1,0:T(8,128)(2,1)}, u32[]{:S(2)}, u32[]{:S(2)}) collective-permute-start(bf16[128,2048]{1,0:T(8,128)(2,1)} %pad_maximum_fusion.5), channel_id=1, source_target_pairs={{0,2},{2,4},{4,6},{6,0},{1,3},{3,5},{5,7},{7,1},{8,10},{10,12},{12... | collective-permute-start | bytes 1572872 | tf_op jit(solution)/shard_map/ppermute | solution.py:750
  414.8 27.1 %collective-permute-start.48 = (bf16[4,64,1152]{2,1,0:T(8,128)(2,1)}, bf16[4,64,1152]{2,1,0:T(8,128)(2,1)}, u32[]{:S(2)}, u32[]{:S(2)}) collective-permute-start(bf16[4,64,1152]{2,1,0:T(8,128)(2,1)} %get-tuple-element.163), channel_id=1, source_target_pairs={{0,32},{16,48},{32,0},{48,16},{1,33},{17,49},{33,1},{49,17},{2,34}... | collective-permute-start | bytes 1769480 | tf_op jit(solution)/shard_map/ppermute | solution.py:782
  418.0 24.9 %collective-permute-start.49 = (bf16[4,64,1152]{2,1,0:T(8,128)(2,1)S(1)}, bf16[4,64,1152]{2,1,0:T(8,128)(2,1)S(1)}, u32[]{:S(2)}, u32[]{:S(2)}) collective-permute-start(bf16[4,64,1152]{2,1,0:T(8,128)(2,1)S(1)} %get-tuple-element.162), channel_id=1, source_target_pairs={{0,48},{16,0},{32,16},{48,32},{1,49},{17,1},{33,17},{49,33},{2,50}... | collective-permute-start | bytes 1769480 | tf_op jit(solution)/shard_map/ppermute | solution.py:782
  468.7 81.9 %all-gather.7.cloned.1.call-start = ((), (), s32[]{:S(2)}) async-start(), calls=%async_computation.7 | async-start | bytes 6266880 | tf_op jit(solution)/shard_map/all_gather | solution.py:930
  (89 other events, 779.5 us)
Sparse Core Ops, SparseCore 0:
  52.5 118.4 all-gather.4
  481.2 69.3 all-gather.6

commit v3 on v2

--- a/solution.py
+++ b/solution.py
@@ -16,7 +16,7 @@
 ROPE_BASE = 10000.0
 NEG = -1e30
 BLOCK = 128
-CHUNK = 2 * BLOCK
+CHUNK = 4 * BLOCK
 SCALE = 1.0 / math.sqrt(HEAD_SIZE)
 
 AXES = ("zlo", "y", "zhi", "x", "core")
@@ -74,8 +74,11 @@
 
 
 def chunk_slots(c, zhi, x, core):
-    base = ((c // 4) ^ zhi) * 8 + ((c - x) & 3)
-    return base + 4 * core, base + 4 * (1 - core)
+    slots = []
+    for i in range(CHUNK // BLOCK):
+        n = c * (CHUNK // BLOCK) + i
+        slots.append(((n >> 3) ^ zhi) * 8 + ((n & 1) ^ core) * 4 + (((n >> 1) - x) & 3))
+    return slots
 
 
 def allowed_mask(c, st, block):
@@ -107,9 +110,9 @@
 
     def step(c, state, masked):
         m, l, acc = state
-        s0, s1 = chunk_slots(c, zhi, x, core)
-        k = jnp.concatenate([kv_ref[s0, :HEAD_SIZE, :], kv_ref[s1, :HEAD_SIZE, :]], axis=1)
-        v = jnp.concatenate([kv_ref[s0, HEAD_SIZE:, :], kv_ref[s1, HEAD_SIZE:, :]], axis=1)
+        slots = chunk_slots(c, zhi, x, core)
+        k = jnp.concatenate([kv_ref[n, :HEAD_SIZE, :] for n in slots], axis=1)
+        v = jnp.concatenate([kv_ref[n, HEAD_SIZE:, :] for n in slots], axis=1)
         s = lax.dot_general(k, q, (((0,), (0,)), ((), ())), preferred_element_type=F32)
         if masked:
             s = jnp.where(allowed_mask(c, st, block), s, NEG)
@@ -128,7 +131,7 @@
         jnp.zeros((1, rows), F32),
         jnp.zeros((HEAD_SIZE, rows), F32),
     )
-    m, l, acc = over_chunks(step, state, first, sc[7 + b], block // 2)
+    m, l, acc = over_chunks(step, state, first, sc[7 + b], block // (CHUNK // BLOCK))
     o = acc / l
     for h in range(GROUP):
         part = o[:, BLOCK * h : BLOCK * (h + 1)]
@@ -157,9 +160,9 @@
     st = jnp.concatenate([st_ref[0]] * GROUP, axis=1)
 
     def step(c, dq, masked):
-        s0, s1 = chunk_slots(c, zhi, x, core)
-        k = jnp.concatenate([kv_ref[s0, :HEAD_SIZE, :], kv_ref[s1, :HEAD_SIZE, :]], axis=1)
-        v = jnp.concatenate([kv_ref[s0, HEAD_SIZE:, :], kv_ref[s1, HEAD_SIZE:, :]], axis=1)
+        slots = chunk_slots(c, zhi, x, core)
+        k = jnp.concatenate([kv_ref[n, :HEAD_SIZE, :] for n in slots], axis=1)
+        v = jnp.concatenate([kv_ref[n, HEAD_SIZE:, :] for n in slots], axis=1)
         s = lax.dot_general(k, q, (((0,), (0,)), ((), ())), preferred_element_type=F32)
         if masked:
             s = jnp.where(allowed_mask(c, st, block), s, NEG)
@@ -170,12 +173,12 @@
         dk = jnp.dot(ds, q_rows, preferred_element_type=F32)
         dv = jnp.dot(pb, do_rows, preferred_element_type=F32)
         both = jnp.concatenate([dk, dv], axis=1)
-        acc_ref[s0] += both[:BLOCK]
-        acc_ref[s1] += both[BLOCK:]
+        for i, n in enumerate(slots):
+            acc_ref[n] += both[BLOCK * i : BLOCK * (i + 1)]
         return dq + jnp.dot(k, ds, preferred_element_type=F32)
 
     dq = jnp.zeros((HEAD_SIZE, GROUP * BLOCK), F32)
-    dq = over_chunks(step, dq, first, sc[7 + b], block // 2)
+    dq = over_chunks(step, dq, first, sc[7 + b], block // (CHUNK // BLOCK))
     dq = dq * SCALE
     cos, sin = cos_ref[...], sin_ref[...]
     for h in range(GROUP):
@@ -356,29 +359,29 @@
 
 
 def spread(in_ref, gu_ref, dn_ref, qkv_ref, out_ref, terms_ref):
+    def part(row, rows, at, width):
+        return in_ref[0, row : row + rows, at : at + width].astype(F32)
+
     for x in range(NX):
         for half in range(2):
-            at, to = FF_TILE * (2 * x + half), FF_TILE * (4 * half + x)
-            gu_ref[:, to : to + FF_TILE] = in_ref[0, :, at : at + FF_TILE].astype(F32)
-    base = 8 * FF_TILE
-    for t in range(22):
-        at = base + 2 * FF_TILE * (t % 2) + 256 * (t // 2)
-        dn_ref[16 * t : 16 * (t + 1), :] = in_ref[0, :, at : at + 256].astype(F32)
-    base += 4 * FF_TILE
+            to = FF_TILE * (4 * half + x)
+            gu_ref[:, to : to + FF_TILE] = part(16 * x, 16, FF_TILE * half, FF_TILE)
+    for j in range(11):
+        dn_ref[32 * j : 32 * (j + 1), :] = part(64, 32, 256 * j, 256)
     k, v = [], []
     for x in range(NX):
-        at = base + 640 * x
-        qkv_ref[:, 512 * x : 512 * (x + 1)] = in_ref[0, :, at : at + 512].astype(F32)
-        k.append(in_ref[0, :, at + 512 : at + 576].astype(F32))
-        v.append(in_ref[0, :, at + 576 : at + 640].astype(F32))
+        row, at = 96 + 16 * (x % 2), 1152 * (x // 2)
+        qkv_ref[:, 512 * x : 512 * (x + 1)] = part(row, 16, at, 512)
+        k.append(part(row, 16, at + 512, 64))
+        v.append(part(row, 16, at + 576, 64))
     qkv_ref[:, 2048:2304] = jnp.concatenate(k, axis=1)
     qkv_ref[:, 2304:] = jnp.concatenate(v, axis=1)
-    base += 640 * NX
-    for t in range(8):
-        at = base + 256 * t
-        out_ref[16 * t : 16 * (t + 1), :] = in_ref[0, :, at : at + 256].astype(F32)
-    base += 2048
-    row = in_ref[0, :, base : base + 256].astype(F32)
+    for upper in range(2):
+        for half in range(2):
+            at = 1152 * upper + 640 + 256 * half
+            to = 64 * half + 32 * upper
+            out_ref[to : to + 32, :] = part(96, 32, at, 256)
+    row = part(96, 16, 2304, 256)
     terms = jnp.concatenate([row[0:1, :BLOCK], row[0:1, BLOCK:]], axis=0)
 
     @pl.when(pl.program_id(0) == 0)
@@ -394,7 +397,7 @@
     return pl.pallas_call(
         spread,
         grid=(8,),
-        in_specs=[pl.BlockSpec((1, 16, both.shape[2]), lambda r: (r, 0, 0))],
+        in_specs=[pl.BlockSpec((1,) + both.shape[1:], lambda r: (r, 0, 0))],
         out_specs=[
             pl.BlockSpec((16, 8 * FF_TILE), lambda r: (r, 0)),
             pl.BlockSpec((352, 256), lambda r: (0, r)),
@@ -872,7 +875,7 @@
 
     d_act, wdn = call_down_back(cots, ffn)
     scaled_two, rstd_two = rms_forward(hidden)
-    n2 = gathered_x((scaled_two * gain_two[None, :]).astype(BF16))
+    n2 = gathered_x((scaled_two * gain_two[None, :]).astype(BF16), lambda: (d_act,))
     *d_n2, act, d_gu = call_feed_forward(x, n2, ffn, d_act)
 
     other = call_ffn_grads(1 - core, n2, d_gu, act, cots)
@@ -900,34 +903,37 @@
     dkv = jnp.concatenate([k1 * cos + k2 * sin, k2 * cos - k1 * sin, dkv[64:]], axis=0)
     d_qkv = jnp.concatenate([dq, dkv.astype(BF16)], axis=0)
     d_qkv, g_gu = lax.optimization_barrier((d_qkv, g_gu))
-    g_gu = exchange(total(g_gu.reshape(4, 4, 64, 2 * FF_TILE)), ("zlo", "zhi"))
     d_n1 = mm(d_qkv, wq, ((0,), (1,)), BF16)
     d_qkv, ob, g_dn = lax.optimization_barrier((d_qkv, ob, g_dn, d_n1))[:3]
     d_n1 = moved_x(pieces(d_n1))
     other = swap(call_attention_grads(1 - core, n1, d_qkv, ob, d_br), "core")
     g_attn = call_attention_grads(core, n1, d_qkv, ob, d_br, other)
-    g_dn = sent(g_dn, "y", y)
-
-    g_gu = after(g_gu, g_attn)
+
+    g_gu, g_attn = lax.optimization_barrier((g_gu, g_attn))
+    g_gu = exchange(total(g_gu.reshape(4, 4, 64, 2 * FF_TILE)), ("zlo", "zhi"))
     g_attn = sent(g_attn, "y", y)
+    g_dn = sent(after(g_dn, g_attn[1]), "y", y)
+    g_attn = sent(added(g_attn).astype(BF16), ("zlo", "zhi"), z)
+    g_gu = exchange(total(g_gu).reshape(NX, slab, 2 * FF_TILE), "x")
+    g_dn = lax.ppermute(added(g_dn).astype(BF16), CHIP, to_owners(True))
+    *g_attn, g_gu, g_dn = lax.optimization_barrier((*g_attn, g_gu, g_dn))
     d_n1 = lax.optimization_barrier((*d_n1, *g_attn))[:3]
     act = after(act, *d_n1)
     mixed = moved_x(pieces(mm(act, wdn, ((1,), (0,)), BF16)))
     d_in, gain_one_term = rms_backward(added(d_n1), scaled_one, rstd_one, gain_one)
     input_grad = (d_mid + d_in).astype(BF16)
-    g_attn = sent(added(g_attn).astype(BF16), ("zlo", "zhi"), z)
-    g_gu = exchange(total(g_gu).reshape(NX, slab, 2 * FF_TILE), "x")
-    g_dn = lax.ppermute(added(g_dn).astype(BF16), CHIP, to_owners(True))
-    both = [g_gu[j] for j in range(NX)] + [g_dn[:slab], g_dn[slab:]]
     g_attn = added(g_attn).astype(BF16)
     g_out = lax.ppermute(g_attn[:, 640:], CHIP, to_owners(True))
-    g_out = [g_out[slab * j : slab * (j + 1), 256 * h : 256 * h + 256] for h in (0, 1) for j in range(4)]
-    g_qkv = exchange(g_attn[:, :640].reshape(NX, slab, qkv_cols), "x")
+    g_qkv = jnp.stack(sent(g_attn[:, :640].reshape(NX, slab, qkv_cols), "x", x))
+    g_qkv = g_qkv[(x - jnp.arange(NX, dtype=jnp.int32)) % NX]
     terms = jnp.stack([gain_one_term, gain_two_term]).reshape(2, 16, rows).transpose(1, 0, 2)
     terms = exchange(terms, SHARD).sum(axis=0).reshape(1, 2 * rows)
-    terms = jnp.broadcast_to(terms, (slab, 2 * rows)).astype(BF16)
-    both += [g_qkv[j] for j in range(NX)] + g_out + [terms]
-    both = lax.all_gather(jnp.concatenate(both, axis=1), REP, axis=0)
+    terms = jnp.broadcast_to(terms, (32, 2 * rows)).astype(BF16)
+    g_qkv = g_qkv.reshape(NX * slab, qkv_cols)
+    attn = [g_qkv[:32], g_out[:32], g_qkv[32:], g_out[32:], terms, jnp.zeros_like(terms)]
+    attn = jnp.concatenate(attn, axis=1)
+    both = jnp.concatenate([g_gu.reshape(NX * slab, 2 * FF_TILE), g_dn, attn])
+    both = lax.all_gather(both, REP, axis=0)
     g_gu, g_dn, g_qkv, g_out, terms = call_spread(both)
     mixed = hidden + added(mixed)
 

time: 576 us -> 551 us (0.957)
  waiting for transfers between devices: 204 us -> 178 us
  starting transfers between devices: 141 us -> 149 us
  local copies, waits for them, and re-layouts: 54.9 us -> 47.3 us
    ppermute x31, waiting for transfers between devices: 54.3 us -> 42.1 us  [shift_x(): return lax.ppermute(a, 'x', [(i, (i + k) % NX) for i in range(NX)])]
    all_to_all x6 -> x5, waiting for transfers between devices: 28 us -> 17 us  [exchange(): return lax.all_to_all(a, axes, split_axis=0, concat_axis=0, tiled=True)]
    ppermute x15 -> x18, waiting for transfers between devices: 57.2 us -> 48.1 us  [sent(): lax.ppermute(part, axes, [(i, (i + j) % 4) for i in range(4)])]
    unnamed x131 -> x106, local copies, waits for them, and re-layouts: 37.4 us -> 28.4 us
    ppermute x15 -> x18, starting transfers between devices: 16.6 us -> 24.3 us  [sent(): lax.ppermute(part, axes, [(i, (i + j) % 4) for i in range(4)])]
    all_to_all x6 -> x5, starting transfers between devices: 32.8 us -> 35.3 us  [exchange(): return lax.all_to_all(a, axes, split_axis=0, concat_axis=0, tiled=True)]
  transfers between devices with their start and end apart: 70 -> 72, of which waited for: 33 -> 30; matrix products, arithmetic and copies ran while one was open for 12% -> 11% of each run, Pallas kernels for 10% -> 13%
where the time goes in v3:
time: 551 us; the launch traced here: 542 us
  waiting for transfers between devices  178 us (32%)
  starting transfers between devices  149 us (27%)
  Pallas kernels  103 us (19%)
  local copies, waits for them, and re-layouts  47.3 us (9%)
  other arithmetic  36.8 us (7%)
  between operations  15.1 us (3%)
  matrix products  12.6 us (2%)
    ppermute x31, starting transfers between devices, shift_x(): return lax.ppermute(a, 'x', [(i, (i + k) % NX) for i in range(NX)])  51.3 us
    ppermute x18, waiting for transfers between devices, sent(): lax.ppermute(part, axes, [(i, (i + j) % 4) for i in range(4)])  48.1 us
    ppermute x31, waiting for transfers between devices, shift_x(): return lax.ppermute(a, 'x', [(i, (i + k) % NX) for i in range(NX)])  42.1 us
    all_gather x1, waiting for transfers between devices, body(): both = lax.all_gather(both, REP, axis=0)  41.1 us
    all_to_all x5, starting transfers between devices, exchange(): return lax.all_to_all(a, axes, split_axis=0, concat_axis=0, tiled=True)  35.3 us
    unnamed x106, local copies, waits for them, and re-layouts  28.4 us
    ppermute x11, starting transfers between devices, swap(): return lax.ppermute(a, axis, [(0, 1), (1, 0)])  25.6 us
    pallas_call x1, Pallas kernels, call_feed_forward(): pl.pallas_call(feed_forward, grid_spec=pltpu.PrefetchScalarGridSpec(num_s...  25.2 us
  transfers between devices with their start and end apart: 72, of which 30 were waited for; matrix products, arithmetic and copies ran while one was open for 11% of the time, Pallas kernels for 13%

profile of v3, /device:TPU:1, one launch (start us, length us, event | category | flops | bytes accessed | tf_op | source)
XLA Modules:
  0.0 542.3 jit_solution(12450928613241596505)
XLA Ops:
  18.5 7.3 %all-to-all-start = ((bf16[8,144,640]{2,1,0:T(8,128)(2,1)}), bf16[8,144,640]{2,1,0:T(8,128)(2,1)S(1)}, u32[]{:S(2)}, u32[]{:S(2)}) async-start(bf16[8,144,640]{2,1,0:T(8,128)(2,1)} %get-tuple-element.84), calls=%async_computation | async-start | bytes 2949120 | tf_op jit(solution)/shard_map/all_to_all | solution.py:35
  31.5 16.6 %collective-permute-done.21 = bf16[16,2816]{1,0:T(8,128)(2,1)S(1)} collective-permute-done((bf16[16,2816]{1,0:T(8,128)(2,1)S(1)}, bf16[16,2816]{1,0:T(8,128)(2,1)S(1)}, u32[]{:S(2)}, u32[]{:S(2)}) %collective-permute-start.21) | collective-permute-done | bytes 90144 | tf_op jit(solution)/shard_map/ppermute | solution.py:785
  53.3 9.8 %collective-permute-start.7 = (bf16[128,2048]{1,0:T(8,128)(2,1)}, bf16[128,2048]{1,0:T(8,128)(2,1)}, u32[]{:S(2)}, u32[]{:S(2)}) collective-permute-start(bf16[128,2048]{1,0:T(8,128)(2,1)} %param.14), channel_id=1, source_target_pairs={{0,8},{8,0},{1,9},{9,1},{2,10},{10,2},{3,11},{11,3},{4,12},{12,4},... | collective-permute-start | bytes 1572872 | tf_op jit(solution)/shard_map/ppermute | solution.py:43
  73.9 5.6 %project.1 = (bf16[512,2048]{1,0:T(8,128)(2,1)}, f32[512,512]{1,0:T(8,128)S(1)}, bf16[4,128,128]{2,1,0:T(8,128)(2,1)}, bf16[2048,640]{1,0:T(8,128)(2,1)}, f32[2,2048]{1,0:T(2,128)S(1)}) custom-call(s32[1]{0:T(128)} %bitcast.1.sc, bf16[128,2048]{1,0:T(8,128)(2,1)S(1)} %copy-done, bf16[128,2048]{1,0:T(8,128)(2,1)S(1)} %collective-permute-done.t1, ...), custom_call_target="tpu_custom_call" | custom-call | flops 1048576 | bytes 65536 | tf_op jit(solution)/shard_map/project/pallas_call | solution.py:312
  92.2 5.6 %collective-permute-done.6 = bf16[8,128,128]{2,1,0:T(8,128)(2,1)S(1)} collective-permute-done((bf16[8,128,128]{2,1,0:T(8,128)(2,1)S(1)}, bf16[8,128,128]{2,1,0:T(8,128)(2,1)S(1)}, u32[]{:S(2)}, u32[]{:S(2)}) %collective-permute-start.6) | collective-permute-done | bytes 262176 | tf_op jit(solution)/shard_map/ppermute | solution.py:43
  97.8 5.9 %collective-permute-start.11 = (bf16[128,2048]{1,0:T(8,128)(2,1)}, bf16[128,2048]{1,0:T(8,128)(2,1)}, u32[]{:S(2)}, u32[]{:S(2)}) collective-permute-start(bf16[128,2048]{1,0:T(8,128)(2,1)} %get-tuple-element.90), channel_id=1, source_target_pairs={{0,0},{2,4},{4,2},{6,6},{1,1},{3,5},{5,3},{7,7},{8,8},{10,12},{12,... | collective-permute-start | bytes 1572872 | tf_op jit(solution)/shard_map/ppermute | solution.py:861
  103.8 8.4 %attention_forward.1 = (f32[512,512]{1,0:T(8,128)S(1)}, bf16[512,512]{1,0:T(8,128)(2,1)S(1)}, bf16[4,64,1024]{2,1,0:T(8,128)(2,1)S(1)}, f32[4,1,1024]{2,1,0:T(1,128)S(1)}) custom-call(s32[11]{0:T(128)S(1)} %concatenate.56.sc, f32[512,512]{1,0:T(8,128)S(1)} %copy-done.8, f32[32,512]{1,0:T(8,128)S(1)} %get-tuple-element.228.cos_ref, ...), custom_call_target="tpu_custom_call" | custom-call | flops 1048576 | bytes 65536 | tf_op jit(solution)/shard_map/attention_forward/pallas_call | solution.py:204
  113.8 8.4 %collective-permute-done.12.b_ref = bf16[128,2048]{1,0:T(8,128)(2,1)} collective-permute-done((bf16[128,2048]{1,0:T(8,128)(2,1)}, bf16[128,2048]{1,0:T(8,128)(2,1)}, u32[]{:S(2)}, u32[]{:S(2)}) %collective-permute-start.12) | collective-permute-done | bytes 524320 | tf_op jit(solution)/shard_map/ppermute | solution.py:862
  133.0 12.0 %collective-permute-start.15 = (bf16[64,2048]{1,0:T(8,128)(2,1)S(1)}, bf16[64,2048]{1,0:T(8,128)(2,1)S(1)}, u32[]{:S(2)}, u32[]{:S(2)}) collective-permute-start(bf16[64,2048]{1,0:T(8,128)(2,1)S(1)} %get-tuple-element.204), channel_id=1, source_target_pairs={{0,2},{2,4},{4,6},{6,0},{1,3},{3,5},{5,7},{7,1},{8,10},{10,12},{12... | collective-permute-start | bytes 786440 | tf_op jit(solution)/shard_map/ppermute | solution.py:753
  145.1 5.2 collective-permute-done.15
  154.0 9.9 %collective-permute-done.16 = bf16[128,2048]{1,0:T(8,128)(2,1)S(1)} collective-permute-done((bf16[128,2048]{1,0:T(8,128)(2,1)S(1)}, bf16[128,2048]{1,0:T(8,128)(2,1)S(1)}, u32[]{:S(2)}, u32[]{:S(2)}) %collective-permute-start.16) | collective-permute-done | bytes 524320 | tf_op jit(solution)/shard_map/ppermute | solution.py:753
  171.0 11.1 %down_back.1 = (f32[512,1408]{1,0:T(8,128)S(1)}, bf16[1408,2048]{1,0:T(8,128)(2,1)}) custom-call(bf16[128,2048]{1,0:T(8,128)(2,1)} %c0.2, bf16[128,2048]{1,0:T(8,128)(2,1)} %collective-permute-done.8.c1, bf16[128,2048]{1,0:T(8,128)(2,1)} %collective-permute-done.9.c2, bf16[128,2048]{1,0:T(8,128)(2,1)} %collective-permute-done.10.c3, ...), custom_call_target="tpu_custom_call" | custom-call | flops 8589934592 | bytes 1048576 | tf_op jit(solution)/shard_map/down_back/pallas_call | solution.py:499
  192.7 25.2 %feed_forward.1 = (bf16[128,2048]{1,0:T(8,128)(2,1)S(1)}, bf16[128,2048]{1,0:T(8,128)(2,1)S(1)}, bf16[128,2048]{1,0:T(8,128)(2,1)S(1)}, bf16[128,2048]{1,0:T(8,1...) custom-call(s32[1]{0:T(128)} %bitcast.3.sc, bf16[128,2048]{1,0:T(8,128)(2,1)S(1)} %multiply_convert_fusion.n0, ...), custom_call_target="tpu_custom_call" | custom-call | flops 1048576 | bytes 65536 | tf_op jit(solution)/shard_map/feed_forward/pallas_call | solution.py:585
  232.5 10.7 %ffn_grads_other.1 = (bf16[4,4,64,2816]{3,2,1,0:T(8,128)(2,1)}, bf16[4,4,32,2816]{3,2,1,0:T(8,128)(2,1)}) custom-call(s32[1]{0:T(128)} %bitcast.19.sc, bf16[128,2048]{1,0:T(8,128)(2,1)S(1)} %multiply_convert_fusion.n0, bf16[128,2048]{1,0:T(8,128)(2,1)S(1)} %collective-permute-done.19.n1, bf16[128,2048]{1,0:T(8,128)(2,1)S(1)} %copy-done.5, ...), custom_call_target="tpu_custom_call" | custom-call | flops 8589934592 | bytes 1048576 | tf_op jit(solution)/shard_map/ffn_grads_other/pallas_call | solution.py:680
  243.2 6.5 %collective-permute-start.33 = (bf16[4,4,64,2816]{3,2,1,0:T(8,128)(2,1)}, bf16[4,4,64,2816]{3,2,1,0:T(8,128)(2,1)}, u32[]{:S(2)}, u32[]{:S(2)}) collective-permute-start(bf16[4,4,64,2816]{3,2,1,0:T(8,128)(2,1)} %get-tuple-element.119), channel_id=1, source_target_pairs={{0,1},{1,0},{2,3},{3,2},{4,5},{5,4},{6,7},{7,6},{8,9},{9,8},{10,11... | collective-permute-start | bytes 17301512 | tf_op jit(solution)/shard_map/ppermute | solution.py:43
  256.8 6.5 %collective-permute-done.34.rest_1_ = bf16[4,4,32,2816]{3,2,1,0:T(8,128)(2,1)} collective-permute-done((bf16[4,4,32,2816]{3,2,1,0:T(8,128)(2,1)}, bf16[4,4,32,2816]{3,2,1,0:T(8,128)(2,1)}, u32[]{:S(2)}, u32[]{:S(2)}) %collective-permute-start.34) | collective-permute-done | bytes 2883616 | tf_op jit(solution)/shard_map/ppermute | solution.py:43
  263.3 12.7 %ffn_grads_mine.1 = (bf16[4,4,64,2816]{3,2,1,0:T(8,128)(2,1)}, bf16[4,4,32,2816]{3,2,1,0:T(8,128)(2,1)}) custom-call(s32[1]{0:T(128)} %bitcast.1.sc, bf16[128,2048]{1,0:T(8,128)(2,1)S(1)} %multiply_convert_fusion.n0, bf16[128,2048]{1,0:T(8,128)(2,1)S(1)} %collective-permute-done.19.n1, bf16[128,2048]{1,0:T(8,128)(2,1)S(1)} %copy-done.6, ...), custom_call_target="tpu_custom_call" | custom-call | flops 8589934592 | bytes 1048576 | tf_op jit(solution)/shard_map/ffn_grads_mine/pallas_call | solution.py:680
  279.7 5.1 all-to-all-start.1
  293.5 11.3 %attention_backward.1 = (bf16[512,512]{1,0:T(8,128)(2,1)S(1)}, bf16[16,128,128]{2,1,0:T(8,128)(2,1)S(1)}) custom-call(s32[11]{0:T(128)S(1)} %concatenate.56.sc, bf16[4,64,1024]{2,1,0:T(8,128)(2,1)S(1)} %copy-done.19, bf16[512,512]{1,0:T(8,128)(2,1)S(1)} %convolution_convert_fusion.2.do_ref, f32[512,512]{1,0:T(8,128)S(1)} %copy-done.10, ...), custom_call_target="tpu_custom_call" | custom-call | flops 1048576 | bytes 65536 | tf_op jit(solution)/shard_map/attention_backward/pallas_call | solution.py:243
  305.5 14.7 %collective-permute-done.38 = bf16[4,32,2816]{2,1,0:T(8,128)(2,1)S(1)} collective-permute-done((bf16[4,32,2816]{2,1,0:T(8,128)(2,1)S(1)}, bf16[4,32,2816]{2,1,0:T(8,128)(2,1)S(1)}, u32[]{:S(2)}, u32[]{:S(2)}) %collective-permute-start.38) | collective-permute-done | bytes 720928 | tf_op jit(solution)/shard_map/ppermute | solution.py:785
  326.2 5.9 %collective-permute-done.41 = bf16[4,128,128]{2,0,1:T(4,128)(2,1)S(1)} collective-permute-done((bf16[4,128,128]{2,0,1:T(4,128)(2,1)S(1)}, bf16[4,128,128]{2,0,1:T(4,128)(2,1)S(1)}, u32[]{:S(2)}, u32[]{:S(2)}) %collective-permute-start.41) | collective-permute-done | bytes 131104 | tf_op jit(solution)/shard_map/ppermute | solution.py:43
  332.6 17.0 %all-to-all-done.1 = bf16[4,256,2816]{2,1,0:T(8,128)(2,1)} async-done(((bf16[4,256,2816]{2,1,0:T(8,128)(2,1)}), bf16[4,256,2816]{2,1,0:T(8,128)(2,1)}, u32[]{:S(2)}, u32[]{:S(2)}) %all-to-all-start.1) | async-done | bytes 5767200 | tf_op jit(solution)/shard_map/all_to_all | solution.py:35
  349.6 5.0 convolution_convert_fusion.1
  366.2 4.7 attention_grads_mine.1
  380.7 5.0 reduce_sum.91
  390.9 10.6 %collective-permute-done.48 = bf16[4,64,1152]{2,1,0:T(8,128)(2,1)} collective-permute-done((bf16[4,64,1152]{2,1,0:T(8,128)(2,1)}, bf16[4,64,1152]{2,1,0:T(8,128)(2,1)}, u32[]{:S(2)}, u32[]{:S(2)}) %collective-permute-start.48) | collective-permute-done | bytes 589856 | tf_op jit(solution)/shard_map/ppermute | solution.py:785
  427.4 15.9 %all-to-all-start.4 = ((f32[16,2,128]{2,1,0:T(2,128)}), f32[16,2,128]{2,1,0:T(2,128)S(1)}, u32[]{:S(2)}, u32[]{:S(2)}) async-start(f32[16,2,128]{2,1,0:T(2,128)} %maximum_bitcast_fusion), calls=%async_computation.4 | async-start | bytes 32768 | tf_op jit(solution)/shard_map/all_to_all | solution.py:35
  453.7 6.3 %convolution_convert_fusion = bf16[512,2048]{1,0:T(8,128)(2,1)S(1)} fusion(bf16[512,1408]{1,0:T(8,128)(2,1)S(1)} %copy-done.36, bf16[1408,2048]{1,0:T(8,128)(2,1)} %get-tuple-element.152), kind=kOutput, calls=%fused_computation.2 | convolution fusion | flops 2953838592 | bytes 9306112 | tf_op jit(solution)/shard_map/dot_general | solution.py:53
  460.1 5.9 %collective-permute-start.57 = (bf16[64,2048]{1,0:T(8,128)(2,1)S(1)}, bf16[64,2048]{1,0:T(8,128)(2,1)S(1)}, u32[]{:S(2)}, u32[]{:S(2)}) collective-permute-start(bf16[64,2048]{1,0:T(8,128)(2,1)S(1)} %get-tuple-element.180), channel_id=1, source_target_pairs={{0,2},{2,4},{4,6},{6,0},{1,3},{3,5},{5,7},{7,1},{8,10},{10,12},{12... | collective-permute-start | bytes 786440 | tf_op jit(solution)/shard_map/ppermute | solution.py:753
  477.3 6.4 %collective-permute-done.58 = bf16[128,2048]{1,0:T(8,128)(2,1)S(1)} collective-permute-done((bf16[128,2048]{1,0:T(8,128)(2,1)S(1)}, bf16[128,2048]{1,0:T(8,128)(2,1)S(1)}, u32[]{:S(2)}, u32[]{:S(2)}) %collective-permute-start.58) | collective-permute-done | bytes 524320 | tf_op jit(solution)/shard_map/ppermute | solution.py:753
  485.9 41.1 %all-gather.7.cloned.1.call-done = bf16[1024,2816]{1,0:T(8,128)(2,1)} async-done(((bf16[128,2816]{1,0:T(8,128)(2,1)}), bf16[1024,2816]{1,0:T(8,128)(2,1)}) %all-gather.7.cloned.1.call-update) | async-done | bytes 5767184 | tf_op jit(solution)/shard_map/all_gather | solution.py:936
  529.7 5.0 spread.1
  (328 shorter events, 200.0 us)
Async XLA Ops:
  7.2 45.2 %collective-permute-start = (bf16[128,2048]{1,0:T(8,128)(2,1)}, bf16[128,2048]{1,0:T(8,128)(2,1)S(1)}, u32[]{:S(2)}, u32[]{:S(2)}) collective-permute-start(bf16[128,2048]{1,0:T(8,128)(2,1)} %t0.1), channel_id=1, source_target_pairs={{0,6},{2,0},{4,2},{6,4},{1,7},{3,1},{5,3},{7,5},{8,14},{10,8},{12,... | collective-permute-start | bytes 1572872 | tf_op jit(solution)/shard_map/ppermute | solution.py:753
  10.5 41.8 %collective-permute-start.2 = (bf16[128,2048]{1,0:T(8,128)(2,1)}, bf16[128,2048]{1,0:T(8,128)(2,1)S(1)}, u32[]{:S(2)}, u32[]{:S(2)}) collective-permute-start(bf16[128,2048]{1,0:T(8,128)(2,1)} %t0.1), channel_id=1, source_target_pairs={{0,2},{2,4},{4,6},{6,0},{1,3},{3,5},{5,7},{7,1},{8,10},{10,12},{12... | collective-permute-start | bytes 1572872 | tf_op jit(solution)/shard_map/ppermute | solution.py:753
  18.5 33.8 %all-to-all-start = ((bf16[8,144,640]{2,1,0:T(8,128)(2,1)}), bf16[8,144,640]{2,1,0:T(8,128)(2,1)S(1)}, u32[]{:S(2)}, u32[]{:S(2)}) async-start(bf16[8,144,640]{2,1,0:T(8,128)(2,1)} %get-tuple-element.84), calls=%async_computation | async-start | bytes 2949120 | tf_op jit(solution)/shard_map/all_to_all | solution.py:35
  25.8 145.2 %all-gather.5.cloned.1.call-start = ((), (), s32[]{:S(2)}) async-start(), calls=%async_computation.5 | async-start | bytes 17842176 | tf_op jit(solution)/shard_map/all_gather | solution.py:838
  25.8 22.3 %collective-permute-start.21 = (bf16[16,2816]{1,0:T(8,128)(2,1)S(1)}, bf16[16,2816]{1,0:T(8,128)(2,1)S(1)}, u32[]{:S(2)}, u32[]{:S(2)}) collective-permute-start(bf16[16,2816]{1,0:T(8,128)(2,1)S(1)} %get-tuple-element.208), channel_id=1, source_target_pairs={{0,2},{2,4},{4,6},{6,0},{1,3},{3,5},{5,7},{7,1},{8,10},{10,12},{12... | collective-permute-start | bytes 270344 | tf_op jit(solution)/shard_map/ppermute | solution.py:785
  27.3 23.0 %collective-permute-start.22 = (bf16[16,2816]{1,0:T(8,128)(2,1)S(1)}, bf16[16,2816]{1,0:T(8,128)(2,1)S(1)}, u32[]{:S(2)}, u32[]{:S(2)}) collective-permute-start(bf16[16,2816]{1,0:T(8,128)(2,1)S(1)} %get-tuple-element.207), channel_id=1, source_target_pairs={{0,4},{2,6},{4,0},{6,2},{1,5},{3,7},{5,1},{7,3},{8,12},{10,14},{12... | collective-permute-start | bytes 270344 | tf_op jit(solution)/shard_map/ppermute | solution.py:785
  29.7 21.3 %collective-permute-start.23 = (bf16[16,2816]{1,0:T(8,128)(2,1)S(1)}, bf16[16,2816]{1,0:T(8,128)(2,1)S(1)}, u32[]{:S(2)}, u32[]{:S(2)}) collective-permute-start(bf16[16,2816]{1,0:T(8,128)(2,1)S(1)} %get-tuple-element.206), channel_id=1, source_target_pairs={{0,6},{2,0},{4,2},{6,4},{1,7},{3,1},{5,3},{7,5},{8,14},{10,8},{12,... | collective-permute-start | bytes 270344 | tf_op jit(solution)/shard_map/ppermute | solution.py:785
  52.4 21.5 %collective-permute-start.4 = (bf16[8,144,640]{2,1,0:T(8,128)(2,1)S(1)}, bf16[8,144,640]{2,1,0:T(8,128)(2,1)}, u32[]{:S(2)}, u32[]{:S(2)}) collective-permute-start(bf16[8,144,640]{2,1,0:T(8,128)(2,1)S(1)} %all-to-all-done.mine), channel_id=1, source_target_pairs={{0,1},{1,0},{2,3},{3,2},{4,5},{5,4},{6,7},{7,6},{8,9},{9,8},{10,11... | collective-permute-start | bytes 4423688 | tf_op jit(solution)/shard_map/ppermute | solution.py:43
  53.3 31.0 %collective-permute-start.7 = (bf16[128,2048]{1,0:T(8,128)(2,1)}, bf16[128,2048]{1,0:T(8,128)(2,1)}, u32[]{:S(2)}, u32[]{:S(2)}) collective-permute-start(bf16[128,2048]{1,0:T(8,128)(2,1)} %param.14), channel_id=1, source_target_pairs={{0,8},{8,0},{1,9},{9,1},{2,10},{10,2},{3,11},{11,3},{4,12},{12,4},... | collective-permute-start | bytes 1572872 | tf_op jit(solution)/shard_map/ppermute | solution.py:43
  86.6 27.2 %collective-permute-start.10 = (bf16[128,2048]{1,0:T(8,128)(2,1)}, bf16[128,2048]{1,0:T(8,128)(2,1)}, u32[]{:S(2)}, u32[]{:S(2)}) collective-permute-start(bf16[128,2048]{1,0:T(8,128)(2,1)} %c0.2), channel_id=1, source_target_pairs={{0,2},{2,4},{4,6},{6,0},{1,3},{3,5},{5,7},{7,1},{8,10},{10,12},{12... | collective-permute-start | bytes 1572872 | tf_op jit(solution)/shard_map/ppermute | solution.py:753
  86.6 27.2 %collective-permute-start.8 = (bf16[128,2048]{1,0:T(8,128)(2,1)}, bf16[128,2048]{1,0:T(8,128)(2,1)}, u32[]{:S(2)}, u32[]{:S(2)}) collective-permute-start(bf16[128,2048]{1,0:T(8,128)(2,1)} %c0.2), channel_id=1, source_target_pairs={{0,6},{2,0},{4,2},{6,4},{1,7},{3,1},{5,3},{7,5},{8,14},{10,8},{12,... | collective-permute-start | bytes 1572872 | tf_op jit(solution)/shard_map/ppermute | solution.py:753
  89.2 24.6 %collective-permute-start.9 = (bf16[128,2048]{1,0:T(8,128)(2,1)}, bf16[128,2048]{1,0:T(8,128)(2,1)}, u32[]{:S(2)}, u32[]{:S(2)}) collective-permute-start(bf16[128,2048]{1,0:T(8,128)(2,1)} %c0.2), channel_id=1, source_target_pairs={{0,4},{2,6},{4,0},{6,2},{1,5},{3,7},{5,1},{7,3},{8,12},{10,14},{12... | collective-permute-start | bytes 1572872 | tf_op jit(solution)/shard_map/ppermute | solution.py:753
  89.2 33.0 %collective-permute-start.12 = (bf16[128,2048]{1,0:T(8,128)(2,1)}, bf16[128,2048]{1,0:T(8,128)(2,1)}, u32[]{:S(2)}, u32[]{:S(2)}) collective-permute-start(bf16[128,2048]{1,0:T(8,128)(2,1)} %get-tuple-element.92), channel_id=1, source_target_pairs={{0,4},{2,0},{4,6},{6,2},{1,5},{3,1},{5,7},{7,3},{8,12},{10,8},{12,... | collective-permute-start | bytes 1572872 | tf_op jit(solution)/shard_map/ppermute | solution.py:862
  97.8 25.9 %collective-permute-start.11 = (bf16[128,2048]{1,0:T(8,128)(2,1)}, bf16[128,2048]{1,0:T(8,128)(2,1)}, u32[]{:S(2)}, u32[]{:S(2)}) collective-permute-start(bf16[128,2048]{1,0:T(8,128)(2,1)} %get-tuple-element.90), channel_id=1, source_target_pairs={{0,0},{2,4},{4,2},{6,6},{1,1},{3,5},{5,3},{7,7},{8,8},{10,12},{12,... | collective-permute-start | bytes 1572872 | tf_op jit(solution)/shard_map/ppermute | solution.py:861
  133.0 17.3 %collective-permute-start.15 = (bf16[64,2048]{1,0:T(8,128)(2,1)S(1)}, bf16[64,2048]{1,0:T(8,128)(2,1)S(1)}, u32[]{:S(2)}, u32[]{:S(2)}) collective-permute-start(bf16[64,2048]{1,0:T(8,128)(2,1)S(1)} %get-tuple-element.204), channel_id=1, source_target_pairs={{0,2},{2,4},{4,6},{6,0},{1,3},{3,5},{5,7},{7,1},{8,10},{10,12},{12... | collective-permute-start | bytes 786440 | tf_op jit(solution)/shard_map/ppermute | solution.py:753
  168.4 15.3 %collective-permute-start.19 = (bf16[128,2048]{1,0:T(8,128)(2,1)S(1)}, bf16[128,2048]{1,0:T(8,128)(2,1)S(1)}, u32[]{:S(2)}, u32[]{:S(2)}) collective-permute-start(bf16[128,2048]{1,0:T(8,128)(2,1)S(1)} %multiply_convert_fusion.n0), channel_id=1, source_target_pairs={{0,6},{2,0},{4,2},{6,4},{1,7},{3,1},{5,3},{7,5},{8,14},{10,8},{12,... | collective-permute-start | bytes 1572872 | tf_op jit(solution)/shard_map/ppermute | solution.py:753
  243.2 20.0 %collective-permute-start.33 = (bf16[4,4,64,2816]{3,2,1,0:T(8,128)(2,1)}, bf16[4,4,64,2816]{3,2,1,0:T(8,128)(2,1)}, u32[]{:S(2)}, u32[]{:S(2)}) collective-permute-start(bf16[4,4,64,2816]{3,2,1,0:T(8,128)(2,1)} %get-tuple-element.119), channel_id=1, source_target_pairs={{0,1},{1,0},{2,3},{3,2},{4,5},{5,4},{6,7},{7,6},{8,9},{9,8},{10,11... | collective-permute-start | bytes 17301512 | tf_op jit(solution)/shard_map/ppermute | solution.py:43
  255.3 20.7 %collective-permute-start.31 = (bf16[128,2048]{1,0:T(8,128)(2,1)S(1)}, bf16[128,2048]{1,0:T(8,128)(2,1)S(1)}, u32[]{:S(2)}, u32[]{:S(2)}) collective-permute-start(bf16[128,2048]{1,0:T(8,128)(2,1)S(1)} %get-tuple-element.167), channel_id=1, source_target_pairs={{0,6},{2,0},{4,2},{6,4},{1,7},{3,1},{5,3},{7,5},{8,14},{10,8},{12,... | collective-permute-start | bytes 1572872 | tf_op jit(solution)/shard_map/ppermute | solution.py:753
  255.3 20.7 %collective-permute-start.32 = (bf16[128,2048]{1,0:T(8,128)(2,1)S(1)}, bf16[128,2048]{1,0:T(8,128)(2,1)S(1)}, u32[]{:S(2)}, u32[]{:S(2)}) collective-permute-start(bf16[128,2048]{1,0:T(8,128)(2,1)S(1)} %get-tuple-element.167), channel_id=1, source_target_pairs={{0,2},{2,4},{4,6},{6,0},{1,3},{3,5},{5,7},{7,1},{8,10},{10,12},{12... | collective-permute-start | bytes 1572872 | tf_op jit(solution)/shard_map/ppermute | solution.py:753
  279.7 70.0 %all-to-all-start.1 = ((bf16[4,256,2816]{2,1,0:T(8,128)(2,1)}), bf16[4,256,2816]{2,1,0:T(8,128)(2,1)}, u32[]{:S(2)}, u32[]{:S(2)}) async-start(bf16[4,256,2816]{2,1,0:T(8,128)(2,1)} %bitcast.154), calls=%async_computation.1 | async-start | bytes 11534336 | tf_op jit(solution)/shard_map/all_to_all | solution.py:35
  287.4 18.1 %collective-permute-start.37 = (bf16[4,32,2816]{2,1,0:T(8,128)(2,1)S(1)}, bf16[4,32,2816]{2,1,0:T(8,128)(2,1)S(1)}, u32[]{:S(2)}, u32[]{:S(2)}) collective-permute-start(bf16[4,32,2816]{2,1,0:T(8,128)(2,1)S(1)} %get-tuple-element.173), channel_id=1, source_target_pairs={{0,8},{8,64},{64,72},{72,0},{1,9},{9,65},{65,73},{73,1},{2,10},{10... | collective-permute-start | bytes 2162696 | tf_op jit(solution)/shard_map/ppermute | solution.py:785
  288.4 31.8 %collective-permute-start.38 = (bf16[4,32,2816]{2,1,0:T(8,128)(2,1)S(1)}, bf16[4,32,2816]{2,1,0:T(8,128)(2,1)S(1)}, u32[]{:S(2)}, u32[]{:S(2)}) collective-permute-start(bf16[4,32,2816]{2,1,0:T(8,128)(2,1)S(1)} %get-tuple-element.172), channel_id=1, source_target_pairs={{0,64},{8,72},{64,0},{72,8},{1,65},{9,73},{65,1},{73,9},{2,66},{10... | collective-permute-start | bytes 2162696 | tf_op jit(solution)/shard_map/ppermute | solution.py:785
  289.4 32.4 %collective-permute-start.39 = (bf16[4,32,2816]{2,1,0:T(8,128)(2,1)S(1)}, bf16[4,32,2816]{2,1,0:T(8,128)(2,1)S(1)}, u32[]{:S(2)}, u32[]{:S(2)}) collective-permute-start(bf16[4,32,2816]{2,1,0:T(8,128)(2,1)S(1)} %get-tuple-element.171), channel_id=1, source_target_pairs={{0,72},{8,0},{64,8},{72,64},{1,73},{9,1},{65,9},{73,65},{2,74},{10... | collective-permute-start | bytes 2162696 | tf_op jit(solution)/shard_map/ppermute | solution.py:785
  373.5 16.5 %collective-permute-start.47 = (bf16[4,64,1152]{2,1,0:T(8,128)(2,1)}, bf16[4,64,1152]{2,1,0:T(8,128)(2,1)}, u32[]{:S(2)}, u32[]{:S(2)}) collective-permute-start(bf16[4,64,1152]{2,1,0:T(8,128)(2,1)} %get-tuple-element.175), channel_id=1, source_target_pairs={{0,16},{16,32},{32,48},{48,0},{1,17},{17,33},{33,49},{49,1},{2,18}... | collective-permute-start | bytes 1769480 | tf_op jit(solution)/shard_map/ppermute | solution.py:785
  375.0 26.4 %collective-permute-start.48 = (bf16[4,64,1152]{2,1,0:T(8,128)(2,1)}, bf16[4,64,1152]{2,1,0:T(8,128)(2,1)}, u32[]{:S(2)}, u32[]{:S(2)}) collective-permute-start(bf16[4,64,1152]{2,1,0:T(8,128)(2,1)} %get-tuple-element.177), channel_id=1, source_target_pairs={{0,32},{16,48},{32,0},{48,16},{1,33},{17,49},{33,1},{49,17},{2,34}... | collective-permute-start | bytes 1769480 | tf_op jit(solution)/shard_map/ppermute | solution.py:785
  376.9 26.8 %collective-permute-start.49 = (bf16[4,64,1152]{2,1,0:T(8,128)(2,1)}, bf16[4,64,1152]{2,1,0:T(8,128)(2,1)}, u32[]{:S(2)}, u32[]{:S(2)}) collective-permute-start(bf16[4,64,1152]{2,1,0:T(8,128)(2,1)} %get-tuple-element.176), channel_id=1, source_target_pairs={{0,48},{16,0},{32,16},{48,32},{1,49},{17,1},{33,17},{49,33},{2,50}... | collective-permute-start | bytes 1769480 | tf_op jit(solution)/shard_map/ppermute | solution.py:785
  378.4 45.7 %collective-permute-start.45 = (bf16[128,2048]{1,0:T(8,128)(2,1)}, bf16[128,2048]{1,0:T(8,128)(2,1)S(1)}, u32[]{:S(2)}, u32[]{:S(2)}) collective-permute-start(bf16[128,2048]{1,0:T(8,128)(2,1)} %pad_maximum_fusion.7), channel_id=1, source_target_pairs={{0,6},{2,0},{4,2},{6,4},{1,7},{3,1},{5,3},{7,5},{8,14},{10,8},{12,... | collective-permute-start | bytes 1572872 | tf_op jit(solution)/shard_map/ppermute | solution.py:753
  379.9 44.2 %collective-permute-start.43 = (bf16[128,2048]{1,0:T(8,128)(2,1)}, bf16[128,2048]{1,0:T(8,128)(2,1)}, u32[]{:S(2)}, u32[]{:S(2)}) collective-permute-start(bf16[128,2048]{1,0:T(8,128)(2,1)} %pad_maximum_fusion.6), channel_id=1, source_target_pairs={{0,2},{2,4},{4,6},{6,0},{1,3},{3,5},{5,7},{7,1},{8,10},{10,12},{12... | collective-permute-start | bytes 1572872 | tf_op jit(solution)/shard_map/ppermute | solution.py:753
  385.7 24.4 %all-to-all-start.2 = ((bf16[4,64,2816]{2,1,0:T(8,128)(2,1)}), bf16[4,64,2816]{2,1,0:T(8,128)(2,1)S(1)}, u32[]{:S(2)}, u32[]{:S(2)}) async-start(bf16[4,64,2816]{2,1,0:T(8,128)(2,1)} %bitcast.39), calls=%async_computation.2 | async-start | bytes 2883584 | tf_op jit(solution)/shard_map/all_to_all | solution.py:35
  390.8 23.9 %collective-permute-start.53 = (bf16[32,2816]{1,0:T(8,128)(2,1)}, bf16[32,2816]{1,0:T(8,128)(2,1)}, u32[]{:S(2)}, u32[]{:S(2)}) collective-permute-start(bf16[32,2816]{1,0:T(8,128)(2,1)} %get-tuple-element.192), channel_id=1, source_target_pairs={{0,16},{16,32},{32,48},{48,0},{1,17},{17,33},{33,49},{49,1},{2,18}... | collective-permute-start | bytes 540680 | tf_op jit(solution)/shard_map/ppermute | solution.py:785
  427.4 23.7 %all-to-all-start.4 = ((f32[16,2,128]{2,1,0:T(2,128)}), f32[16,2,128]{2,1,0:T(2,128)S(1)}, u32[]{:S(2)}, u32[]{:S(2)}) async-start(f32[16,2,128]{2,1,0:T(2,128)} %maximum_bitcast_fusion), calls=%async_computation.4 | async-start | bytes 32768 | tf_op jit(solution)/shard_map/all_to_all | solution.py:35
  443.3 83.8 %all-gather.7.cloned.1.call-start = ((), (), s32[]{:S(2)}) async-start(), calls=%async_computation.6 | async-start | bytes 6488064 | tf_op jit(solution)/shard_map/all_gather | solution.py:936
  (85 other events, 653.0 us)
Sparse Core Ops, SparseCore 0:
  52.5 118.4 all-gather.4
  453.9 73.1 all-gather.6

commit v4 on v3

--- a/solution.py
+++ b/solution.py
@@ -358,7 +358,7 @@
     )(sc, o, *w)
 
 
-def spread(in_ref, gu_ref, dn_ref, qkv_ref, out_ref, terms_ref):
+def spread(in_ref, gu_ref, dn_ref, qkv_ref, out_ref):
     def part(row, rows, at, width):
         return in_ref[0, row : row + rows, at : at + width].astype(F32)
 
@@ -381,16 +381,6 @@
             at = 1152 * upper + 640 + 256 * half
             to = 64 * half + 32 * upper
             out_ref[to : to + 32, :] = part(96, 32, at, 256)
-    row = part(96, 16, 2304, 256)
-    terms = jnp.concatenate([row[0:1, :BLOCK], row[0:1, BLOCK:]], axis=0)
-
-    @pl.when(pl.program_id(0) == 0)
-    def _():
-        terms_ref[...] = terms
-
-    @pl.when(pl.program_id(0) > 0)
-    def _():
-        terms_ref[...] += terms
 
 
 def call_spread(both):
@@ -403,14 +393,12 @@
             pl.BlockSpec((352, 256), lambda r: (0, r)),
             pl.BlockSpec((16, 2560), lambda r: (r, 0)),
             pl.BlockSpec((BLOCK, 256), lambda r: (0, r)),
-            pl.BlockSpec((2, BLOCK), lambda r: (0, 0)),
         ],
         out_shape=[
             jax.ShapeDtypeStruct((BLOCK, 8 * FF_TILE), F32),
             jax.ShapeDtypeStruct((352, 2048), F32),
             jax.ShapeDtypeStruct((BLOCK, 2560), F32),
             jax.ShapeDtypeStruct((BLOCK, 2048), F32),
-            jax.ShapeDtypeStruct((2, BLOCK), F32),
         ],
         compiler_params=params("arbitrary"),
         cost_estimate=cost(1 << 20, 1 << 16),
@@ -926,15 +914,17 @@
     g_out = lax.ppermute(g_attn[:, 640:], CHIP, to_owners(True))
     g_qkv = jnp.stack(sent(g_attn[:, :640].reshape(NX, slab, qkv_cols), "x", x))
     g_qkv = g_qkv[(x - jnp.arange(NX, dtype=jnp.int32)) % NX]
-    terms = jnp.stack([gain_one_term, gain_two_term]).reshape(2, 16, rows).transpose(1, 0, 2)
-    terms = exchange(terms, SHARD).sum(axis=0).reshape(1, 2 * rows)
-    terms = jnp.broadcast_to(terms, (32, 2 * rows)).astype(BF16)
     g_qkv = g_qkv.reshape(NX * slab, qkv_cols)
-    attn = [g_qkv[:32], g_out[:32], g_qkv[32:], g_out[32:], terms, jnp.zeros_like(terms)]
+    attn = [g_qkv[:32], g_out[:32], g_qkv[32:], g_out[32:], jnp.zeros((32, 512), BF16)]
     attn = jnp.concatenate(attn, axis=1)
     both = jnp.concatenate([g_gu.reshape(NX * slab, 2 * FF_TILE), g_dn, attn])
+    payload = both = after(both, input_grad)
     both = lax.all_gather(both, REP, axis=0)
-    g_gu, g_dn, g_qkv, g_out, terms = call_spread(both)
+    g_gu, g_dn, g_qkv, g_out = call_spread(both)
+
+    terms = jnp.stack([gain_one_term, gain_two_term]).reshape(2, 16, rows).transpose(1, 0, 2)
+    terms = exchange(after(terms, payload), SHARD).sum(axis=0)
+    terms = everywhere(terms.astype(BF16), REP, 8).astype(F32).sum(axis=0)
     mixed = hidden + added(mixed)
 
     return (

time: 551 us -> 541 us (0.982)
  blocking collectives: 0 us -> 35.4 us
  starting transfers between devices: 149 us -> 126 us
  waiting for transfers between devices: 178 us -> 156 us
    all_to_all x0 -> x2, blocking collectives: none -> 35.4 us  [exchange(): return lax.all_to_all(a, axes, split_axis=0, concat_axis=0, tiled=True)]
    all_gather x1, waiting for transfers between devices: 41.1 us -> 21 us  [body(): both = lax.all_gather(both, REP, axis=0)]
    all_to_all x5 -> x4, starting transfers between devices: 35.3 us -> 19.9 us  [exchange(): return lax.all_to_all(a, axes, split_axis=0, concat_axis=0, tiled=True)]
    unnamed x106 -> x107, local copies, waits for them, and re-layouts: 28.4 us -> 29.1 us
    all_to_all x5 -> x4, waiting for transfers between devices: 17 us -> 17 us  [exchange(): return lax.all_to_all(a, axes, split_axis=0, concat_axis=0, tiled=True)]
  transfers between devices with their start and end apart: 72 -> 71, of which waited for: 30 -> 27; matrix products, arithmetic and copies ran while one was open for 11% -> 12% of each run, Pallas kernels for 13% -> 13%
where the time goes in v4:
time: 541 us; the launch traced here: 532 us
  waiting for transfers between devices  156 us (29%)
  starting transfers between devices  126 us (23%)
  Pallas kernels  103 us (19%)
  local copies, waits for them, and re-layouts  47.7 us (9%)
  other arithmetic  36.6 us (7%)
  blocking collectives  35.4 us (7%)
  between operations  15.4 us (3%)
  matrix products  12.6 us (2%)
    ppermute x31, starting transfers between devices, shift_x(): return lax.ppermute(a, 'x', [(i, (i + k) % NX) for i in range(NX)])  48.5 us
    ppermute x18, waiting for transfers between devices, sent(): lax.ppermute(part, axes, [(i, (i + j) % 4) for i in range(4)])  48 us
    ppermute x31, waiting for transfers between devices, shift_x(): return lax.ppermute(a, 'x', [(i, (i + k) % NX) for i in range(NX)])  39.1 us
    all_to_all x2, blocking collectives, exchange(): return lax.all_to_all(a, axes, split_axis=0, concat_axis=0, tiled=True)  35.4 us
    unnamed x107, local copies, waits for them, and re-layouts  29.1 us
    ppermute x11, starting transfers between devices, swap(): return lax.ppermute(a, axis, [(0, 1), (1, 0)])  25.5 us
    pallas_call x1, Pallas kernels, call_feed_forward(): pl.pallas_call(feed_forward, grid_spec=pltpu.PrefetchScalarGridSpec(num_s...  25.2 us
    pallas_call x2, Pallas kernels, call_ffn_grads(): pl.pallas_call(ffn_grads, grid_spec=pltpu.PrefetchScalarGridSpec(num_scal...  23.2 us
  transfers between devices with their start and end apart: 71, of which 27 were waited for; matrix products, arithmetic and copies ran while one was open for 12% of the time, Pallas kernels for 13%

profile of v4, /device:TPU:1, one launch (start us, length us, event | category | flops | bytes accessed | tf_op | source)
XLA Modules:
  0.0 531.7 jit_solution(15746074487174233425)
XLA Ops:
  18.5 7.3 %all-to-all-start = ((bf16[8,144,640]{2,1,0:T(8,128)(2,1)}), bf16[8,144,640]{2,1,0:T(8,128)(2,1)S(1)}, u32[]{:S(2)}, u32[]{:S(2)}) async-start(bf16[8,144,640]{2,1,0:T(8,128)(2,1)} %get-tuple-element.85), calls=%async_computation | async-start | bytes 2949120 | tf_op jit(solution)/shard_map/all_to_all | solution.py:35
  31.5 16.6 %collective-permute-done.21 = bf16[16,2816]{1,0:T(8,128)(2,1)S(1)} collective-permute-done((bf16[16,2816]{1,0:T(8,128)(2,1)S(1)}, bf16[16,2816]{1,0:T(8,128)(2,1)S(1)}, u32[]{:S(2)}, u32[]{:S(2)}) %collective-permute-start.21) | collective-permute-done | bytes 90144 | tf_op jit(solution)/shard_map/ppermute | solution.py:773
  53.3 9.8 %collective-permute-start.7 = (bf16[128,2048]{1,0:T(8,128)(2,1)}, bf16[128,2048]{1,0:T(8,128)(2,1)}, u32[]{:S(2)}, u32[]{:S(2)}) collective-permute-start(bf16[128,2048]{1,0:T(8,128)(2,1)} %param.14), channel_id=1, source_target_pairs={{0,8},{8,0},{1,9},{9,1},{2,10},{10,2},{3,11},{11,3},{4,12},{12,4},... | collective-permute-start | bytes 1572872 | tf_op jit(solution)/shard_map/ppermute | solution.py:43
  67.1 4.6 collective-permute-done.1.t2a
  73.9 5.6 %project.1 = (bf16[512,2048]{1,0:T(8,128)(2,1)}, f32[512,512]{1,0:T(8,128)S(1)}, bf16[4,128,128]{2,1,0:T(8,128)(2,1)}, bf16[2048,640]{1,0:T(8,128)(2,1)}, f32[2,2048]{1,0:T(2,128)S(1)}) custom-call(s32[1]{0:T(128)} %bitcast.1.sc, bf16[128,2048]{1,0:T(8,128)(2,1)S(1)} %copy-done, bf16[128,2048]{1,0:T(8,128)(2,1)S(1)} %collective-permute-done.t1, ...), custom_call_target="tpu_custom_call" | custom-call | flops 1048576 | bytes 65536 | tf_op jit(solution)/shard_map/project/pallas_call | solution.py:312
  92.2 5.6 %collective-permute-done.6 = bf16[8,128,128]{2,1,0:T(8,128)(2,1)S(1)} collective-permute-done((bf16[8,128,128]{2,1,0:T(8,128)(2,1)S(1)}, bf16[8,128,128]{2,1,0:T(8,128)(2,1)S(1)}, u32[]{:S(2)}, u32[]{:S(2)}) %collective-permute-start.6) | collective-permute-done | bytes 262176 | tf_op jit(solution)/shard_map/ppermute | solution.py:43
  97.8 5.6 %collective-permute-start.11 = (bf16[128,2048]{1,0:T(8,128)(2,1)}, bf16[128,2048]{1,0:T(8,128)(2,1)}, u32[]{:S(2)}, u32[]{:S(2)}) collective-permute-start(bf16[128,2048]{1,0:T(8,128)(2,1)} %get-tuple-element.91), channel_id=1, source_target_pairs={{0,0},{2,4},{4,2},{6,6},{1,1},{3,5},{5,3},{7,7},{8,8},{10,12},{12,... | collective-permute-start | bytes 1572872 | tf_op jit(solution)/shard_map/ppermute | solution.py:849
  103.5 8.3 %attention_forward.1 = (f32[512,512]{1,0:T(8,128)S(1)}, bf16[512,512]{1,0:T(8,128)(2,1)S(1)}, bf16[4,64,1024]{2,1,0:T(8,128)(2,1)S(1)}, f32[4,1,1024]{2,1,0:T(1,128)S(1)}) custom-call(s32[11]{0:T(128)S(1)} %concatenate.56.sc, f32[512,512]{1,0:T(8,128)S(1)} %copy-done.8, f32[32,512]{1,0:T(8,128)S(1)} %get-tuple-element.230.cos_ref, ...), custom_call_target="tpu_custom_call" | custom-call | flops 1048576 | bytes 65536 | tf_op jit(solution)/shard_map/attention_forward/pallas_call | solution.py:204
  113.5 8.7 %collective-permute-done.12.b_ref = bf16[128,2048]{1,0:T(8,128)(2,1)} collective-permute-done((bf16[128,2048]{1,0:T(8,128)(2,1)}, bf16[128,2048]{1,0:T(8,128)(2,1)}, u32[]{:S(2)}, u32[]{:S(2)}) %collective-permute-start.12) | collective-permute-done | bytes 524320 | tf_op jit(solution)/shard_map/ppermute | solution.py:850
  133.0 12.0 %collective-permute-start.15 = (bf16[64,2048]{1,0:T(8,128)(2,1)S(1)}, bf16[64,2048]{1,0:T(8,128)(2,1)S(1)}, u32[]{:S(2)}, u32[]{:S(2)}) collective-permute-start(bf16[64,2048]{1,0:T(8,128)(2,1)S(1)} %get-tuple-element.206), channel_id=1, source_target_pairs={{0,2},{2,4},{4,6},{6,0},{1,3},{3,5},{5,7},{7,1},{8,10},{10,12},{12... | collective-permute-start | bytes 786440 | tf_op jit(solution)/shard_map/ppermute | solution.py:741
  145.2 5.2 collective-permute-done.15
  154.0 9.9 %collective-permute-done.16 = bf16[128,2048]{1,0:T(8,128)(2,1)S(1)} collective-permute-done((bf16[128,2048]{1,0:T(8,128)(2,1)S(1)}, bf16[128,2048]{1,0:T(8,128)(2,1)S(1)}, u32[]{:S(2)}, u32[]{:S(2)}) %collective-permute-start.16) | collective-permute-done | bytes 524320 | tf_op jit(solution)/shard_map/ppermute | solution.py:741
  171.0 11.1 %down_back.1 = (f32[512,1408]{1,0:T(8,128)S(1)}, bf16[1408,2048]{1,0:T(8,128)(2,1)}) custom-call(bf16[128,2048]{1,0:T(8,128)(2,1)} %c0.2, bf16[128,2048]{1,0:T(8,128)(2,1)} %collective-permute-done.8.c1, bf16[128,2048]{1,0:T(8,128)(2,1)} %collective-permute-done.9.c2, bf16[128,2048]{1,0:T(8,128)(2,1)} %collective-permute-done.10.c3, ...), custom_call_target="tpu_custom_call" | custom-call | flops 8589934592 | bytes 1048576 | tf_op jit(solution)/shard_map/down_back/pallas_call | solution.py:487
  192.2 25.2 %feed_forward.1 = (bf16[128,2048]{1,0:T(8,128)(2,1)S(1)}, bf16[128,2048]{1,0:T(8,128)(2,1)S(1)}, bf16[128,2048]{1,0:T(8,128)(2,1)S(1)}, bf16[128,2048]{1,0:T(8,1...) custom-call(s32[1]{0:T(128)} %bitcast.3.sc, bf16[128,2048]{1,0:T(8,128)(2,1)S(1)} %multiply_convert_fusion.n0, ...), custom_call_target="tpu_custom_call" | custom-call | flops 1048576 | bytes 65536 | tf_op jit(solution)/shard_map/feed_forward/pallas_call | solution.py:573
  232.2 10.7 %ffn_grads_other.1 = (bf16[4,4,64,2816]{3,2,1,0:T(8,128)(2,1)}, bf16[4,4,32,2816]{3,2,1,0:T(8,128)(2,1)}) custom-call(s32[1]{0:T(128)} %bitcast.19.sc, bf16[128,2048]{1,0:T(8,128)(2,1)S(1)} %multiply_convert_fusion.n0, bf16[128,2048]{1,0:T(8,128)(2,1)S(1)} %collective-permute-done.19.n1, bf16[128,2048]{1,0:T(8,128)(2,1)S(1)} %copy-done.5, ...), custom_call_target="tpu_custom_call" | custom-call | flops 8589934592 | bytes 1048576 | tf_op jit(solution)/shard_map/ffn_grads_other/pallas_call | solution.py:668
  242.9 6.5 %collective-permute-start.33 = (bf16[4,4,64,2816]{3,2,1,0:T(8,128)(2,1)}, bf16[4,4,64,2816]{3,2,1,0:T(8,128)(2,1)}, u32[]{:S(2)}, u32[]{:S(2)}) collective-permute-start(bf16[4,4,64,2816]{3,2,1,0:T(8,128)(2,1)} %get-tuple-element.120), channel_id=1, source_target_pairs={{0,1},{1,0},{2,3},{3,2},{4,5},{5,4},{6,7},{7,6},{8,9},{9,8},{10,11... | collective-permute-start | bytes 17301512 | tf_op jit(solution)/shard_map/ppermute | solution.py:43
  256.5 6.4 %collective-permute-done.34.rest_1_ = bf16[4,4,32,2816]{3,2,1,0:T(8,128)(2,1)} collective-permute-done((bf16[4,4,32,2816]{3,2,1,0:T(8,128)(2,1)}, bf16[4,4,32,2816]{3,2,1,0:T(8,128)(2,1)}, u32[]{:S(2)}, u32[]{:S(2)}) %collective-permute-start.34) | collective-permute-done | bytes 2883616 | tf_op jit(solution)/shard_map/ppermute | solution.py:43
  262.9 12.5 %ffn_grads_mine.1 = (bf16[4,4,64,2816]{3,2,1,0:T(8,128)(2,1)}, bf16[4,4,32,2816]{3,2,1,0:T(8,128)(2,1)}) custom-call(s32[1]{0:T(128)} %bitcast.1.sc, bf16[128,2048]{1,0:T(8,128)(2,1)S(1)} %multiply_convert_fusion.n0, bf16[128,2048]{1,0:T(8,128)(2,1)S(1)} %collective-permute-done.19.n1, bf16[128,2048]{1,0:T(8,128)(2,1)S(1)} %copy-done.6, ...), custom_call_target="tpu_custom_call" | custom-call | flops 8589934592 | bytes 1048576 | tf_op jit(solution)/shard_map/ffn_grads_mine/pallas_call | solution.py:668
  279.2 5.1 all-to-all-start.1
  293.0 11.3 %attention_backward.1 = (bf16[512,512]{1,0:T(8,128)(2,1)S(1)}, bf16[16,128,128]{2,1,0:T(8,128)(2,1)S(1)}) custom-call(s32[11]{0:T(128)S(1)} %concatenate.56.sc, bf16[4,64,1024]{2,1,0:T(8,128)(2,1)S(1)} %copy-done.19, bf16[512,512]{1,0:T(8,128)(2,1)S(1)} %convolution_convert_fusion.2.do_ref, f32[512,512]{1,0:T(8,128)S(1)} %copy-done.10, ...), custom_call_target="tpu_custom_call" | custom-call | flops 1048576 | bytes 65536 | tf_op jit(solution)/shard_map/attention_backward/pallas_call | solution.py:243
  305.0 14.7 %collective-permute-done.38 = bf16[4,32,2816]{2,1,0:T(8,128)(2,1)S(1)} collective-permute-done((bf16[4,32,2816]{2,1,0:T(8,128)(2,1)S(1)}, bf16[4,32,2816]{2,1,0:T(8,128)(2,1)S(1)}, u32[]{:S(2)}, u32[]{:S(2)}) %collective-permute-start.38) | collective-permute-done | bytes 720928 | tf_op jit(solution)/shard_map/ppermute | solution.py:773
  325.6 5.9 %collective-permute-done.41 = bf16[4,128,128]{2,0,1:T(4,128)(2,1)S(1)} collective-permute-done((bf16[4,128,128]{2,0,1:T(4,128)(2,1)S(1)}, bf16[4,128,128]{2,0,1:T(4,128)(2,1)S(1)}, u32[]{:S(2)}, u32[]{:S(2)}) %collective-permute-start.41) | collective-permute-done | bytes 131104 | tf_op jit(solution)/shard_map/ppermute | solution.py:43
  332.1 17.0 %all-to-all-done.1 = bf16[4,256,2816]{2,1,0:T(8,128)(2,1)} async-done(((bf16[4,256,2816]{2,1,0:T(8,128)(2,1)}), bf16[4,256,2816]{2,1,0:T(8,128)(2,1)}, u32[]{:S(2)}, u32[]{:S(2)}) %all-to-all-start.1) | async-done | bytes 5767200 | tf_op jit(solution)/shard_map/all_to_all | solution.py:35
  349.1 5.0 convolution_convert_fusion.1
  366.8 4.7 attention_grads_mine.1
  379.0 5.1 reduce_sum.100
  391.7 10.4 %collective-permute-done.48 = bf16[4,64,1152]{2,1,0:T(8,128)(2,1)} collective-permute-done((bf16[4,64,1152]{2,1,0:T(8,128)(2,1)}, bf16[4,64,1152]{2,1,0:T(8,128)(2,1)}, u32[]{:S(2)}, u32[]{:S(2)}) %collective-permute-start.48) | collective-permute-done | bytes 589856 | tf_op jit(solution)/shard_map/ppermute | solution.py:773
  441.7 6.3 %convolution_convert_fusion = bf16[512,2048]{1,0:T(8,128)(2,1)S(1)} fusion(bf16[512,1408]{1,0:T(8,128)(2,1)S(1)} %copy-done.36, bf16[1408,2048]{1,0:T(8,128)(2,1)} %get-tuple-element.153), kind=kOutput, calls=%fused_computation.2 | convolution fusion | flops 2953838592 | bytes 9306112 | tf_op jit(solution)/shard_map/dot_general | solution.py:53
  457.6 25.9 %all_to_all.30 = f32[16,2,128]{2,1,0:T(2,128)S(1)} all-to-all(f32[16,2,128]{2,1,0:T(2,128)S(1)} %maximum_bitcast_fusion), channel_id=1, replica_groups=mesh['zlo'=2,'y'=4,'zhi'=2,'x'=4,'core'=2] {'zhi','x','core'}, dimensions={0} | all-to-all | bytes 32768 | tf_op jit(solution)/shard_map/all_to_all | solution.py:35
  483.6 9.4 %all_to_all.31 = bf16[8,2,128]{2,1,0:T(2,128)(2,1)S(1)} all-to-all(bf16[8,2,128]{2,1,0:T(2,128)(2,1)S(1)} %broadcast_in_dim.26), channel_id=1, replica_groups=mesh['zlo'=2,'y'=4,'zhi'=2,'x'=4,'core'=2] {'zlo','y'}, dimensions={0} | all-to-all | bytes 8192 | tf_op jit(solution)/shard_map/all_to_all | solution.py:35
  496.0 21.0 %all-gather.7.cloned.1.call-done = bf16[1024,2816]{1,0:T(8,128)(2,1)} async-done(((bf16[128,2816]{1,0:T(8,128)(2,1)}), bf16[1024,2816]{1,0:T(8,128)(2,1)}) %all-gather.7.cloned.1.call-update) | async-done | bytes 5767184 | tf_op jit(solution)/shard_map/all_gather | solution.py:922
  519.7 4.7 spread.1
  (331 shorter events, 198.1 us)
Async XLA Ops:
  7.2 45.2 %collective-permute-start = (bf16[128,2048]{1,0:T(8,128)(2,1)}, bf16[128,2048]{1,0:T(8,128)(2,1)S(1)}, u32[]{:S(2)}, u32[]{:S(2)}) collective-permute-start(bf16[128,2048]{1,0:T(8,128)(2,1)} %t0.1), channel_id=1, source_target_pairs={{0,6},{2,0},{4,2},{6,4},{1,7},{3,1},{5,3},{7,5},{8,14},{10,8},{12,... | collective-permute-start | bytes 1572872 | tf_op jit(solution)/shard_map/ppermute | solution.py:741
  10.5 41.8 %collective-permute-start.2 = (bf16[128,2048]{1,0:T(8,128)(2,1)}, bf16[128,2048]{1,0:T(8,128)(2,1)S(1)}, u32[]{:S(2)}, u32[]{:S(2)}) collective-permute-start(bf16[128,2048]{1,0:T(8,128)(2,1)} %t0.1), channel_id=1, source_target_pairs={{0,2},{2,4},{4,6},{6,0},{1,3},{3,5},{5,7},{7,1},{8,10},{10,12},{12... | collective-permute-start | bytes 1572872 | tf_op jit(solution)/shard_map/ppermute | solution.py:741
  18.5 33.8 %all-to-all-start = ((bf16[8,144,640]{2,1,0:T(8,128)(2,1)}), bf16[8,144,640]{2,1,0:T(8,128)(2,1)S(1)}, u32[]{:S(2)}, u32[]{:S(2)}) async-start(bf16[8,144,640]{2,1,0:T(8,128)(2,1)} %get-tuple-element.85), calls=%async_computation | async-start | bytes 2949120 | tf_op jit(solution)/shard_map/all_to_all | solution.py:35
  25.8 145.2 %all-gather.5.cloned.1.call-start = ((), (), s32[]{:S(2)}) async-start(), calls=%async_computation.6 | async-start | bytes 17842176 | tf_op jit(solution)/shard_map/all_gather | solution.py:826
  25.8 22.3 %collective-permute-start.21 = (bf16[16,2816]{1,0:T(8,128)(2,1)S(1)}, bf16[16,2816]{1,0:T(8,128)(2,1)S(1)}, u32[]{:S(2)}, u32[]{:S(2)}) collective-permute-start(bf16[16,2816]{1,0:T(8,128)(2,1)S(1)} %get-tuple-element.210), channel_id=1, source_target_pairs={{0,2},{2,4},{4,6},{6,0},{1,3},{3,5},{5,7},{7,1},{8,10},{10,12},{12... | collective-permute-start | bytes 270344 | tf_op jit(solution)/shard_map/ppermute | solution.py:773
  27.3 23.0 %collective-permute-start.22 = (bf16[16,2816]{1,0:T(8,128)(2,1)S(1)}, bf16[16,2816]{1,0:T(8,128)(2,1)S(1)}, u32[]{:S(2)}, u32[]{:S(2)}) collective-permute-start(bf16[16,2816]{1,0:T(8,128)(2,1)S(1)} %get-tuple-element.209), channel_id=1, source_target_pairs={{0,4},{2,6},{4,0},{6,2},{1,5},{3,7},{5,1},{7,3},{8,12},{10,14},{12... | collective-permute-start | bytes 270344 | tf_op jit(solution)/shard_map/ppermute | solution.py:773
  29.7 21.3 %collective-permute-start.23 = (bf16[16,2816]{1,0:T(8,128)(2,1)S(1)}, bf16[16,2816]{1,0:T(8,128)(2,1)S(1)}, u32[]{:S(2)}, u32[]{:S(2)}) collective-permute-start(bf16[16,2816]{1,0:T(8,128)(2,1)S(1)} %get-tuple-element.208), channel_id=1, source_target_pairs={{0,6},{2,0},{4,2},{6,4},{1,7},{3,1},{5,3},{7,5},{8,14},{10,8},{12,... | collective-permute-start | bytes 270344 | tf_op jit(solution)/shard_map/ppermute | solution.py:773
  52.4 21.5 %collective-permute-start.4 = (bf16[8,144,640]{2,1,0:T(8,128)(2,1)S(1)}, bf16[8,144,640]{2,1,0:T(8,128)(2,1)}, u32[]{:S(2)}, u32[]{:S(2)}) collective-permute-start(bf16[8,144,640]{2,1,0:T(8,128)(2,1)S(1)} %all-to-all-done.mine), channel_id=1, source_target_pairs={{0,1},{1,0},{2,3},{3,2},{4,5},{5,4},{6,7},{7,6},{8,9},{9,8},{10,11... | collective-permute-start | bytes 4423688 | tf_op jit(solution)/shard_map/ppermute | solution.py:43
  53.3 31.0 %collective-permute-start.7 = (bf16[128,2048]{1,0:T(8,128)(2,1)}, bf16[128,2048]{1,0:T(8,128)(2,1)}, u32[]{:S(2)}, u32[]{:S(2)}) collective-permute-start(bf16[128,2048]{1,0:T(8,128)(2,1)} %param.14), channel_id=1, source_target_pairs={{0,8},{8,0},{1,9},{9,1},{2,10},{10,2},{3,11},{11,3},{4,12},{12,4},... | collective-permute-start | bytes 1572872 | tf_op jit(solution)/shard_map/ppermute | solution.py:43
  86.6 27.0 %collective-permute-start.10 = (bf16[128,2048]{1,0:T(8,128)(2,1)}, bf16[128,2048]{1,0:T(8,128)(2,1)}, u32[]{:S(2)}, u32[]{:S(2)}) collective-permute-start(bf16[128,2048]{1,0:T(8,128)(2,1)} %c0.2), channel_id=1, source_target_pairs={{0,2},{2,4},{4,6},{6,0},{1,3},{3,5},{5,7},{7,1},{8,10},{10,12},{12... | collective-permute-start | bytes 1572872 | tf_op jit(solution)/shard_map/ppermute | solution.py:741
  86.6 27.0 %collective-permute-start.8 = (bf16[128,2048]{1,0:T(8,128)(2,1)}, bf16[128,2048]{1,0:T(8,128)(2,1)}, u32[]{:S(2)}, u32[]{:S(2)}) collective-permute-start(bf16[128,2048]{1,0:T(8,128)(2,1)} %c0.2), channel_id=1, source_target_pairs={{0,6},{2,0},{4,2},{6,4},{1,7},{3,1},{5,3},{7,5},{8,14},{10,8},{12,... | collective-permute-start | bytes 1572872 | tf_op jit(solution)/shard_map/ppermute | solution.py:741
  89.2 24.3 %collective-permute-start.9 = (bf16[128,2048]{1,0:T(8,128)(2,1)}, bf16[128,2048]{1,0:T(8,128)(2,1)}, u32[]{:S(2)}, u32[]{:S(2)}) collective-permute-start(bf16[128,2048]{1,0:T(8,128)(2,1)} %c0.2), channel_id=1, source_target_pairs={{0,4},{2,6},{4,0},{6,2},{1,5},{3,7},{5,1},{7,3},{8,12},{10,14},{12... | collective-permute-start | bytes 1572872 | tf_op jit(solution)/shard_map/ppermute | solution.py:741
  89.2 33.0 %collective-permute-start.12 = (bf16[128,2048]{1,0:T(8,128)(2,1)}, bf16[128,2048]{1,0:T(8,128)(2,1)}, u32[]{:S(2)}, u32[]{:S(2)}) collective-permute-start(bf16[128,2048]{1,0:T(8,128)(2,1)} %get-tuple-element.93), channel_id=1, source_target_pairs={{0,4},{2,0},{4,6},{6,2},{1,5},{3,1},{5,7},{7,3},{8,12},{10,8},{12,... | collective-permute-start | bytes 1572872 | tf_op jit(solution)/shard_map/ppermute | solution.py:850
  97.8 25.9 %collective-permute-start.11 = (bf16[128,2048]{1,0:T(8,128)(2,1)}, bf16[128,2048]{1,0:T(8,128)(2,1)}, u32[]{:S(2)}, u32[]{:S(2)}) collective-permute-start(bf16[128,2048]{1,0:T(8,128)(2,1)} %get-tuple-element.91), channel_id=1, source_target_pairs={{0,0},{2,4},{4,2},{6,6},{1,1},{3,5},{5,3},{7,7},{8,8},{10,12},{12,... | collective-permute-start | bytes 1572872 | tf_op jit(solution)/shard_map/ppermute | solution.py:849
  133.0 17.3 %collective-permute-start.15 = (bf16[64,2048]{1,0:T(8,128)(2,1)S(1)}, bf16[64,2048]{1,0:T(8,128)(2,1)S(1)}, u32[]{:S(2)}, u32[]{:S(2)}) collective-permute-start(bf16[64,2048]{1,0:T(8,128)(2,1)S(1)} %get-tuple-element.206), channel_id=1, source_target_pairs={{0,2},{2,4},{4,6},{6,0},{1,3},{3,5},{5,7},{7,1},{8,10},{10,12},{12... | collective-permute-start | bytes 786440 | tf_op jit(solution)/shard_map/ppermute | solution.py:741
  242.9 20.0 %collective-permute-start.33 = (bf16[4,4,64,2816]{3,2,1,0:T(8,128)(2,1)}, bf16[4,4,64,2816]{3,2,1,0:T(8,128)(2,1)}, u32[]{:S(2)}, u32[]{:S(2)}) collective-permute-start(bf16[4,4,64,2816]{3,2,1,0:T(8,128)(2,1)} %get-tuple-element.120), channel_id=1, source_target_pairs={{0,1},{1,0},{2,3},{3,2},{4,5},{5,4},{6,7},{7,6},{8,9},{9,8},{10,11... | collective-permute-start | bytes 17301512 | tf_op jit(solution)/shard_map/ppermute | solution.py:43
  255.0 20.4 %collective-permute-start.31 = (bf16[128,2048]{1,0:T(8,128)(2,1)S(1)}, bf16[128,2048]{1,0:T(8,128)(2,1)S(1)}, u32[]{:S(2)}, u32[]{:S(2)}) collective-permute-start(bf16[128,2048]{1,0:T(8,128)(2,1)S(1)} %get-tuple-element.169), channel_id=1, source_target_pairs={{0,6},{2,0},{4,2},{6,4},{1,7},{3,1},{5,3},{7,5},{8,14},{10,8},{12,... | collective-permute-start | bytes 1572872 | tf_op jit(solution)/shard_map/ppermute | solution.py:741
  255.0 20.5 %collective-permute-start.32 = (bf16[128,2048]{1,0:T(8,128)(2,1)S(1)}, bf16[128,2048]{1,0:T(8,128)(2,1)S(1)}, u32[]{:S(2)}, u32[]{:S(2)}) collective-permute-start(bf16[128,2048]{1,0:T(8,128)(2,1)S(1)} %get-tuple-element.169), channel_id=1, source_target_pairs={{0,2},{2,4},{4,6},{6,0},{1,3},{3,5},{5,7},{7,1},{8,10},{10,12},{12... | collective-permute-start | bytes 1572872 | tf_op jit(solution)/shard_map/ppermute | solution.py:741
  279.2 70.0 %all-to-all-start.1 = ((bf16[4,256,2816]{2,1,0:T(8,128)(2,1)}), bf16[4,256,2816]{2,1,0:T(8,128)(2,1)}, u32[]{:S(2)}, u32[]{:S(2)}) async-start(bf16[4,256,2816]{2,1,0:T(8,128)(2,1)} %bitcast.151), calls=%async_computation.1 | async-start | bytes 11534336 | tf_op jit(solution)/shard_map/all_to_all | solution.py:35
  286.9 18.1 %collective-permute-start.37 = (bf16[4,32,2816]{2,1,0:T(8,128)(2,1)S(1)}, bf16[4,32,2816]{2,1,0:T(8,128)(2,1)S(1)}, u32[]{:S(2)}, u32[]{:S(2)}) collective-permute-start(bf16[4,32,2816]{2,1,0:T(8,128)(2,1)S(1)} %get-tuple-element.175), channel_id=1, source_target_pairs={{0,8},{8,64},{64,72},{72,0},{1,9},{9,65},{65,73},{73,1},{2,10},{10... | collective-permute-start | bytes 2162696 | tf_op jit(solution)/shard_map/ppermute | solution.py:773
  287.6 32.1 %collective-permute-start.38 = (bf16[4,32,2816]{2,1,0:T(8,128)(2,1)S(1)}, bf16[4,32,2816]{2,1,0:T(8,128)(2,1)S(1)}, u32[]{:S(2)}, u32[]{:S(2)}) collective-permute-start(bf16[4,32,2816]{2,1,0:T(8,128)(2,1)S(1)} %get-tuple-element.174), channel_id=1, source_target_pairs={{0,64},{8,72},{64,0},{72,8},{1,65},{9,73},{65,1},{73,9},{2,66},{10... | collective-permute-start | bytes 2162696 | tf_op jit(solution)/shard_map/ppermute | solution.py:773
  288.9 32.4 %collective-permute-start.39 = (bf16[4,32,2816]{2,1,0:T(8,128)(2,1)S(1)}, bf16[4,32,2816]{2,1,0:T(8,128)(2,1)S(1)}, u32[]{:S(2)}, u32[]{:S(2)}) collective-permute-start(bf16[4,32,2816]{2,1,0:T(8,128)(2,1)S(1)} %get-tuple-element.173), channel_id=1, source_target_pairs={{0,72},{8,0},{64,8},{72,64},{1,73},{9,1},{65,9},{73,65},{2,74},{10... | collective-permute-start | bytes 2162696 | tf_op jit(solution)/shard_map/ppermute | solution.py:773
  374.5 27.6 %collective-permute-start.48 = (bf16[4,64,1152]{2,1,0:T(8,128)(2,1)}, bf16[4,64,1152]{2,1,0:T(8,128)(2,1)}, u32[]{:S(2)}, u32[]{:S(2)}) collective-permute-start(bf16[4,64,1152]{2,1,0:T(8,128)(2,1)} %get-tuple-element.179), channel_id=1, source_target_pairs={{0,32},{16,48},{32,0},{48,16},{1,33},{17,49},{33,1},{49,17},{2,34}... | collective-permute-start | bytes 1769480 | tf_op jit(solution)/shard_map/ppermute | solution.py:773
  376.2 26.8 %collective-permute-start.49 = (bf16[4,64,1152]{2,1,0:T(8,128)(2,1)}, bf16[4,64,1152]{2,1,0:T(8,128)(2,1)}, u32[]{:S(2)}, u32[]{:S(2)}) collective-permute-start(bf16[4,64,1152]{2,1,0:T(8,128)(2,1)} %get-tuple-element.178), channel_id=1, source_target_pairs={{0,48},{16,0},{32,16},{48,32},{1,49},{17,1},{33,17},{49,33},{2,50}... | collective-permute-start | bytes 1769480 | tf_op jit(solution)/shard_map/ppermute | solution.py:773
  378.9 51.3 %collective-permute-start.45 = (bf16[128,2048]{1,0:T(8,128)(2,1)}, bf16[128,2048]{1,0:T(8,128)(2,1)}, u32[]{:S(2)}, u32[]{:S(2)}) collective-permute-start(bf16[128,2048]{1,0:T(8,128)(2,1)} %pad_maximum_fusion.7), channel_id=1, source_target_pairs={{0,6},{2,0},{4,2},{6,4},{1,7},{3,1},{5,3},{7,5},{8,14},{10,8},{12,... | collective-permute-start | bytes 1572872 | tf_op jit(solution)/shard_map/ppermute | solution.py:741
  384.0 22.8 %all-to-all-start.2 = ((bf16[4,64,2816]{2,1,0:T(8,128)(2,1)}), bf16[4,64,2816]{2,1,0:T(8,128)(2,1)S(1)}, u32[]{:S(2)}, u32[]{:S(2)}) async-start(bf16[4,64,2816]{2,1,0:T(8,128)(2,1)} %bitcast.39), calls=%async_computation.2 | async-start | bytes 2883584 | tf_op jit(solution)/shard_map/all_to_all | solution.py:35
  391.4 20.4 %collective-permute-start.53 = (bf16[32,2816]{1,0:T(8,128)(2,1)}, bf16[32,2816]{1,0:T(8,128)(2,1)}, u32[]{:S(2)}, u32[]{:S(2)}) collective-permute-start(bf16[32,2816]{1,0:T(8,128)(2,1)} %get-tuple-element.194), channel_id=1, source_target_pairs={{0,16},{16,32},{32,48},{48,0},{1,17},{17,33},{33,49},{49,1},{2,18}... | collective-permute-start | bytes 540680 | tf_op jit(solution)/shard_map/ppermute | solution.py:773
  391.4 20.9 %collective-permute-start.54 = (bf16[32,2816]{1,0:T(8,128)(2,1)}, bf16[32,2816]{1,0:T(8,128)(2,1)}, u32[]{:S(2)}, u32[]{:S(2)}) collective-permute-start(bf16[32,2816]{1,0:T(8,128)(2,1)} %get-tuple-element.196), channel_id=1, source_target_pairs={{0,32},{16,48},{32,0},{48,16},{1,33},{17,49},{33,1},{49,17},{2,34}... | collective-permute-start | bytes 540680 | tf_op jit(solution)/shard_map/ppermute | solution.py:773
  411.8 105.2 %all-gather.7.cloned.1.call-start = ((), (), s32[]{:S(2)}) async-start(), calls=%async_computation.7 | async-start | bytes 6488064 | tf_op jit(solution)/shard_map/all_gather | solution.py:922
  417.4 17.8 %collective-permute-start.43 = (bf16[128,2048]{1,0:T(8,128)(2,1)}, bf16[128,2048]{1,0:T(8,128)(2,1)S(1)}, u32[]{:S(2)}, u32[]{:S(2)}) collective-permute-start(bf16[128,2048]{1,0:T(8,128)(2,1)} %pad_maximum_fusion.6), channel_id=1, source_target_pairs={{0,2},{2,4},{4,6},{6,0},{1,3},{3,5},{5,7},{7,1},{8,10},{10,12},{12... | collective-permute-start | bytes 1572872 | tf_op jit(solution)/shard_map/ppermute | solution.py:741
  454.7 38.8 %collective-permute-start.58 = (bf16[128,2048]{1,0:T(8,128)(2,1)S(1)}, bf16[128,2048]{1,0:T(8,128)(2,1)S(1)}, u32[]{:S(2)}, u32[]{:S(2)}) collective-permute-start(bf16[128,2048]{1,0:T(8,128)(2,1)S(1)} %pad_maximum_fusion.8), channel_id=1, source_target_pairs={{0,2},{2,4},{4,6},{6,0},{1,3},{3,5},{5,7},{7,1},{8,10},{10,12},{12... | collective-permute-start | bytes 1572872 | tf_op jit(solution)/shard_map/ppermute | solution.py:741
  456.1 37.5 %collective-permute-start.60 = (bf16[128,2048]{1,0:T(8,128)(2,1)S(1)}, bf16[128,2048]{1,0:T(8,128)(2,1)S(1)}, u32[]{:S(2)}, u32[]{:S(2)}) collective-permute-start(bf16[128,2048]{1,0:T(8,128)(2,1)S(1)} %pad_maximum_fusion.9), channel_id=1, source_target_pairs={{0,6},{2,0},{4,2},{6,4},{1,7},{3,1},{5,3},{7,5},{8,14},{10,8},{12,... | collective-permute-start | bytes 1572872 | tf_op jit(solution)/shard_map/ppermute | solution.py:741
  (85 other events, 661.5 us)
Sparse Core Ops, SparseCore 0:
  52.5 118.4 all-gather.4
  441.8 75.2 all-gather.6

commit v5 on v4

--- a/solution.py
+++ b/solution.py
@@ -468,10 +468,11 @@
         for c in range(2):
             for j in range(11):
                 at = (2 * p + c) * 352 + 32 * j
-                wdn_ref[at : at + 32, :] = w_ref[0, p, c, :, 256 * j : 256 * (j + 1)]
-    cots = jnp.concatenate([c0[...], c1[...], c2[...], c3[...]], axis=0)
+                wdn_ref[0, at : at + 32, :] = w_ref[0, p, c, :, 256 * j : 256 * (j + 1)]
+    cols = pl.ds(pl.multiple_of(r * 256, 256), 256)
+    cots = jnp.concatenate([c[:, cols] for c in (c0, c1, c2, c3)], axis=0)
     part = lax.dot_general(
-        cots, wdn_ref[...], (((1,), (1,)), ((), ())), preferred_element_type=F32
+        cots, wdn_ref[0], (((1,), (1,)), ((), ())), preferred_element_type=F32
     )
 
     @pl.when(r == 0)
@@ -487,15 +488,15 @@
     return pl.pallas_call(
         down_back,
         grid=(8,),
-        in_specs=[pl.BlockSpec((BLOCK, 256), lambda r: (0, r))] * 4
+        in_specs=[pl.BlockSpec((BLOCK, 2048), lambda r: (0, 0))] * 4
         + [pl.BlockSpec((1, 2, 2, 32, 2 * FF_TILE), lambda r: (r, 0, 0, 2, 0))],
         out_specs=[
             pl.BlockSpec((NX * BLOCK, FF_TILE), lambda r: (0, 0)),
-            pl.BlockSpec((FF_TILE, 256), lambda r: (0, r)),
+            pl.BlockSpec((1, FF_TILE, 256), lambda r: (r, 0, 0)),
         ],
         out_shape=[
             jax.ShapeDtypeStruct((NX * BLOCK, FF_TILE), F32),
-            jax.ShapeDtypeStruct((FF_TILE, 2048), BF16),
+            jax.ShapeDtypeStruct((8, FF_TILE, 256), BF16),
         ],
         compiler_params=params("arbitrary"),
         cost_estimate=cost(1 << 33, 1 << 20),
@@ -503,12 +504,26 @@
     )(*cots, ffn)
 
 
-def natural(w_ref, pick, me):
-    parts = []
-    for zhi, x, c in pick:
-        at = pl.ds(pl.multiple_of(((me - x) & 3) * 16, 16), 16)
-        parts.append(w_ref[:, zhi, c, at, :].reshape(BLOCK, BLOCK))
-    return jnp.concatenate(parts, axis=0)
+def down_forward(act_ref, w_ref, o0, o1, o2, o3):
+    d = jnp.dot(act_ref[...], w_ref[0], preferred_element_type=F32).astype(BF16)
+    for j, o in enumerate((o0, o1, o2, o3)):
+        o[...] = d[BLOCK * j : BLOCK * (j + 1)]
+
+
+def call_down_forward(act, wdn):
+    return pl.pallas_call(
+        down_forward,
+        grid=(8,),
+        in_specs=[
+            pl.BlockSpec((NX * BLOCK, FF_TILE), lambda r: (0, 0)),
+            pl.BlockSpec((1, FF_TILE, 256), lambda r: (r, 0, 0)),
+        ],
+        out_specs=[pl.BlockSpec((BLOCK, 256), lambda r: (0, r))] * 4,
+        out_shape=[jax.ShapeDtypeStruct((BLOCK, 2048), BF16)] * 4,
+        compiler_params=params("arbitrary"),
+        cost_estimate=cost(1 << 20, 1 << 16),
+        name="down_forward",
+    )(act, wdn)
 
 
 ORDER = [(zhi, x, c) for zhi in range(2) for x in range(NX) for c in range(2)]
@@ -516,43 +531,54 @@
 
 
 def feed_forward(
-    sc, n0, n1, n2, n3, wg_ref, wu_ref, w_ref, d_ref, o0, o1, o2, o3, act_ref, dgu_ref, n_s, act_s, dg_s
+    sc, n0, n1, n2, n3, ffn_ref, d_ref, o0, o1, o2, o3, act_ref, dgu_ref, n_s, w_s, sems
 ):
     k = pl.program_id(0)
 
+    def natural(at):
+        parts = []
+        for zhi, x, c in ORDER:
+            rows = pl.ds(pl.multiple_of(((sc[0] - x) & 3) * 16, 16), 16)
+            parts.append(w_s[:, zhi, c, rows, at].reshape(BLOCK, BLOCK))
+        return jnp.concatenate(parts, axis=0)
+
     @pl.when(k == 0)
     def _():
+        copies = [
+            pltpu.make_async_copy(ffn_ref.at[r, :, :, :64, :], w_s.at[r], sems.at[r])
+            for r in range(8)
+        ]
+        for copy in copies:
+            copy.start()
         for j, n in enumerate((n0, n1, n2, n3)):
             n_s[BLOCK * j : BLOCK * (j + 1), :] = n[...]
+        for copy in copies:
+            copy.wait()
 
     @pl.when(k < FF_STEPS)
     def _():
-        w = [natural(ref, ORDER, sc[0]) for ref in (wg_ref, wu_ref)]
-        w = jnp.concatenate(w, axis=1)
+        at = pl.ds(pl.multiple_of(k * BLOCK, BLOCK), BLOCK)
+        up_at = pl.ds(pl.multiple_of(FF_TILE + k * BLOCK, BLOCK), BLOCK)
+        w = jnp.concatenate([natural(at), natural(up_at)], axis=1)
         both = jnp.dot(n_s[...], w, preferred_element_type=F32)
         gate, up = both[:, :BLOCK], both[:, BLOCK:]
         d_act = d_ref[...]
         sig = 1.0 / (1.0 + jnp.exp(-gate))
         silu = gate * sig
-        at = pl.ds(pl.multiple_of(k * BLOCK, BLOCK), BLOCK)
-        up_at = pl.ds(pl.multiple_of(FF_TILE + k * BLOCK, BLOCK), BLOCK)
-        act_s[:, at] = (silu * up).astype(BF16)
+        act_ref[:, at] = (silu * up).astype(BF16)
         d_gate = d_act * up * (sig * (1.0 + gate * (1.0 - sig)))
-        dg_s[:, at] = d_gate.astype(BF16)
-        dg_s[:, up_at] = (d_act * silu).astype(BF16)
-
-    @pl.when(k == FF_STEPS)
-    def _():
-        act_ref[...] = act_s[...]
-        dgu_ref[...] = dg_s[...]
+        dgu_ref[:, at] = d_gate.astype(BF16)
+        dgu_ref[:, up_at] = (d_act * silu).astype(BF16)
 
     @pl.when(k >= FF_STEPS)
     def _():
+        i = k - FF_STEPS
+        rows = pl.ds(pl.multiple_of(((sc[0] - i) & 3) * 16, 16), 16)
         w = jnp.concatenate(
-            [w_ref[:, 0, c].reshape(BLOCK, 2 * FF_TILE) for c in range(2)], axis=0
+            [w_s[:, i >> 2, c, rows, :].reshape(BLOCK, 2 * FF_TILE) for c in range(2)], axis=0
         )
         d = lax.dot_general(
-            dg_s[...], w, (((1,), (1,)), ((), ())), preferred_element_type=F32
+            dgu_ref[...], w, (((1,), (1,)), ((), ())), preferred_element_type=F32
         ).astype(BF16)
         for j, o in enumerate((o0, o1, o2, o3)):
             o[...] = d[BLOCK * j : BLOCK * (j + 1)]
@@ -564,9 +590,6 @@
 
     def later(k):
         return jnp.maximum(k - FF_STEPS, 0)
-
-    def row_block(k, s):
-        return (0, later(k) >> 2, 0, (s[0] - later(k)) & 3, 0)
 
     whole = pl.BlockSpec((BLOCK, 2048), lambda k, s: (0, 0))
     out = pl.BlockSpec((BLOCK, 256), lambda k, s: (0, later(k)))
@@ -577,9 +600,7 @@
             grid=(FF_STEPS + 8,),
             in_specs=[whole] * 4
             + [
-                pl.BlockSpec((8, 2, 2, 64, BLOCK), lambda k, s: (0, 0, 0, 0, tile(k))),
-                pl.BlockSpec((8, 2, 2, 64, BLOCK), lambda k, s: (0, 0, 0, 0, FF_STEPS + tile(k))),
-                pl.BlockSpec((8, 1, 2, 16, 2 * FF_TILE), row_block),
+                pl.BlockSpec(memory_space=pl.ANY),
                 pl.BlockSpec((NX * BLOCK, BLOCK), lambda k, s: (0, tile(k))),
             ],
             out_specs=[out] * 4
@@ -589,8 +610,8 @@
             ],
             scratch_shapes=[
                 pltpu.VMEM((NX * BLOCK, 2048), BF16),
-                pltpu.VMEM((NX * BLOCK, FF_TILE), BF16),
-                pltpu.VMEM((NX * BLOCK, 2 * FF_TILE), BF16),
+                pltpu.VMEM((8, 2, 2, 64, 2 * FF_TILE), BF16),
+                pltpu.SemaphoreType.DMA((8,)),
             ],
         ),
         out_shape=[jax.ShapeDtypeStruct((BLOCK, 2048), BF16)] * 4
@@ -601,7 +622,7 @@
         compiler_params=params("arbitrary"),
         cost_estimate=cost(1 << 20, 1 << 16),
         name="feed_forward",
-    )(x[None], *n2, ffn, ffn, ffn, d_act)
+    )(x[None], *n2, ffn, d_act)
 
 
 def ffn_grads(sc, n0, n1, n2, n3, dgu_ref, act_ref, c0, c1, c2, c3, *rest):
@@ -907,7 +928,7 @@
     *g_attn, g_gu, g_dn = lax.optimization_barrier((*g_attn, g_gu, g_dn))
     d_n1 = lax.optimization_barrier((*d_n1, *g_attn))[:3]
     act = after(act, *d_n1)
-    mixed = moved_x(pieces(mm(act, wdn, ((1,), (0,)), BF16)))
+    mixed = moved_x(call_down_forward(act, wdn))
     d_in, gain_one_term = rms_backward(added(d_n1), scaled_one, rstd_one, gain_one)
     input_grad = (d_mid + d_in).astype(BF16)
     g_attn = added(g_attn).astype(BF16)

time: 541 us -> 547 us (1.011)
  starting transfers between devices: 126 us -> 138 us
  waiting for transfers between devices: 156 us -> 145 us
  Pallas kernels: 103 us -> 110 us
  matrix products: 12.6 us -> 6.42 us
    ppermute x18, waiting for transfers between devices: 48 us -> 38.7 us  [sent(): lax.ppermute(part, axes, [(i, (i + j) % 4) for i in range(4)])]
    pallas_call x1 -> x2, Pallas kernels: 11.1 us -> 18.8 us  [the longest x1 11.2 us: call_down_back(): pl.pallas_call(down_back, grid=(8,), in_specs=[pl.BlockSpec((BLOCK, 2048)...]
    ppermute x18, starting transfers between devices: 20.2 us -> 27.5 us  [sent(): lax.ppermute(part, axes, [(i, (i + j) % 4) for i in range(4)])]
    dot_general x3 -> x2, matrix products: 12.6 us -> 6.42 us  [mm(): lax.dot_general(left, right, ((dims[0], dims[1]), ((), ())), preferred_el...]
    unnamed x107 -> x147, local copies, waits for them, and re-layouts: 29.1 us -> 29.9 us
  transfers between devices with their start and end apart: 71 -> 71, of which waited for: 27 -> 27; matrix products, arithmetic and copies ran while one was open for 12% -> 12% of each run, Pallas kernels for 13% -> 14%
where the time goes in v5:
time: 547 us; the launch traced here: 538 us
  waiting for transfers between devices  145 us (27%)
  starting transfers between devices  138 us (25%)
  Pallas kernels  110 us (20%)
  local copies, waits for them, and re-layouts  51.5 us (9%)
  other arithmetic  38 us (7%)
  blocking collectives  33.2 us (6%)
  between operations  15.5 us (3%)
  matrix products  6.42 us (1%)
    ppermute x31, starting transfers between devices, shift_x(): return lax.ppermute(a, 'x', [(i, (i + k) % NX) for i in range(NX)])  47.9 us
    ppermute x18, waiting for transfers between devices, sent(): lax.ppermute(part, axes, [(i, (i + j) % 4) for i in range(4)])  38.7 us
    ppermute x31, waiting for transfers between devices, shift_x(): return lax.ppermute(a, 'x', [(i, (i + k) % NX) for i in range(NX)])  37.5 us
    all_to_all x2, blocking collectives, exchange(): return lax.all_to_all(a, axes, split_axis=0, concat_axis=0, tiled=True)  33.2 us
    unnamed x147, local copies, waits for them, and re-layouts  29.9 us
    ppermute x18, starting transfers between devices, sent(): lax.ppermute(part, axes, [(i, (i + j) % 4) for i in range(4)])  27.5 us
    ppermute x11, starting transfers between devices, swap(): return lax.ppermute(a, axis, [(0, 1), (1, 0)])  25.7 us
    pallas_call x1, Pallas kernels, call_feed_forward(): pl.pallas_call(feed_forward, grid_spec=pltpu.PrefetchScalarGridSpec(num_s...  25.1 us
  transfers between devices with their start and end apart: 71, of which 27 were waited for; matrix products, arithmetic and copies ran while one was open for 12% of the time, Pallas kernels for 14%

profile of v5, /device:TPU:1, one launch (start us, length us, event | category | flops | bytes accessed | tf_op | source)
XLA Modules:
  0.0 537.5 jit_solution(2058988868173853197)
XLA Ops:
  18.5 7.3 %all-to-all-start = ((bf16[8,144,640]{2,1,0:T(8,128)(2,1)}), bf16[8,144,640]{2,1,0:T(8,128)(2,1)S(1)}, u32[]{:S(2)}, u32[]{:S(2)}) async-start(bf16[8,144,640]{2,1,0:T(8,128)(2,1)} %get-tuple-element.89), calls=%async_computation | async-start | bytes 2949120 | tf_op jit(solution)/shard_map/all_to_all | solution.py:35
  31.5 16.6 %collective-permute-done.21 = bf16[16,2816]{1,0:T(8,128)(2,1)S(1)} collective-permute-done((bf16[16,2816]{1,0:T(8,128)(2,1)S(1)}, bf16[16,2816]{1,0:T(8,128)(2,1)S(1)}, u32[]{:S(2)}, u32[]{:S(2)}) %collective-permute-start.21) | collective-permute-done | bytes 90144 | tf_op jit(solution)/shard_map/ppermute | solution.py:794
  53.3 9.8 %collective-permute-start.7 = (bf16[128,2048]{1,0:T(8,128)(2,1)}, bf16[128,2048]{1,0:T(8,128)(2,1)}, u32[]{:S(2)}, u32[]{:S(2)}) collective-permute-start(bf16[128,2048]{1,0:T(8,128)(2,1)} %param.14), channel_id=1, source_target_pairs={{0,8},{8,0},{1,9},{9,1},{2,10},{10,2},{3,11},{11,3},{4,12},{12,4},... | collective-permute-start | bytes 1572872 | tf_op jit(solution)/shard_map/ppermute | solution.py:43
  67.2 4.6 collective-permute-done.1.t2a
  73.9 5.6 %project.1 = (bf16[512,2048]{1,0:T(8,128)(2,1)}, f32[512,512]{1,0:T(8,128)S(1)}, bf16[4,128,128]{2,1,0:T(8,128)(2,1)}, bf16[2048,640]{1,0:T(8,128)(2,1)}, f32[2,2048]{1,0:T(2,128)S(1)}) custom-call(s32[1]{0:T(128)} %bitcast.1.sc, bf16[128,2048]{1,0:T(8,128)(2,1)S(1)} %copy-done, bf16[128,2048]{1,0:T(8,128)(2,1)S(1)} %collective-permute-done.t1, ...), custom_call_target="tpu_custom_call" | custom-call | flops 1048576 | bytes 65536 | tf_op jit(solution)/shard_map/project/pallas_call | solution.py:312
  92.9 5.6 %collective-permute-done.6 = bf16[8,128,128]{2,1,0:T(8,128)(2,1)S(1)} collective-permute-done((bf16[8,128,128]{2,1,0:T(8,128)(2,1)S(1)}, bf16[8,128,128]{2,1,0:T(8,128)(2,1)S(1)}, u32[]{:S(2)}, u32[]{:S(2)}) %collective-permute-start.6) | collective-permute-done | bytes 262176 | tf_op jit(solution)/shard_map/ppermute | solution.py:43
  98.5 5.8 %collective-permute-start.11 = (bf16[128,2048]{1,0:T(8,128)(2,1)}, bf16[128,2048]{1,0:T(8,128)(2,1)}, u32[]{:S(2)}, u32[]{:S(2)}) collective-permute-start(bf16[128,2048]{1,0:T(8,128)(2,1)} %get-tuple-element.95), channel_id=1, source_target_pairs={{0,0},{2,4},{4,2},{6,6},{1,1},{3,5},{5,3},{7,7},{8,8},{10,12},{12,... | collective-permute-start | bytes 1572872 | tf_op jit(solution)/shard_map/ppermute | solution.py:870
  104.5 8.4 %attention_forward.1 = (f32[512,512]{1,0:T(8,128)S(1)}, bf16[512,512]{1,0:T(8,128)(2,1)S(1)}, bf16[4,64,1024]{2,1,0:T(8,128)(2,1)S(1)}, f32[4,1,1024]{2,1,0:T(1,128)S(1)}) custom-call(s32[11]{0:T(128)S(1)} %concatenate.56.sc, f32[512,512]{1,0:T(8,128)S(1)} %copy-done.20, f32[32,512]{1,0:T(8,128)S(1)} %get-tuple-element.234.cos_ref, ...), custom_call_target="tpu_custom_call" | custom-call | flops 1048576 | bytes 65536 | tf_op jit(solution)/shard_map/attention_forward/pallas_call | solution.py:204
  115.5 7.2 %collective-permute-done.12.b_ref = bf16[128,2048]{1,0:T(8,128)(2,1)} collective-permute-done((bf16[128,2048]{1,0:T(8,128)(2,1)}, bf16[128,2048]{1,0:T(8,128)(2,1)}, u32[]{:S(2)}, u32[]{:S(2)}) %collective-permute-start.12) | collective-permute-done | bytes 524320 | tf_op jit(solution)/shard_map/ppermute | solution.py:871
  130.7 11.8 %collective-permute-start.15 = (bf16[64,2048]{1,0:T(8,128)(2,1)S(1)}, bf16[64,2048]{1,0:T(8,128)(2,1)S(1)}, u32[]{:S(2)}, u32[]{:S(2)}) collective-permute-start(bf16[64,2048]{1,0:T(8,128)(2,1)S(1)} %get-tuple-element.210), channel_id=1, source_target_pairs={{0,2},{2,4},{4,6},{6,0},{1,3},{3,5},{5,7},{7,1},{8,10},{10,12},{12... | collective-permute-start | bytes 786440 | tf_op jit(solution)/shard_map/ppermute | solution.py:762
  142.6 5.2 collective-permute-done.15
  152.1 9.3 %collective-permute-done.16 = bf16[128,2048]{1,0:T(8,128)(2,1)S(1)} collective-permute-done((bf16[128,2048]{1,0:T(8,128)(2,1)S(1)}, bf16[128,2048]{1,0:T(8,128)(2,1)S(1)}, u32[]{:S(2)}, u32[]{:S(2)}) %collective-permute-start.16) | collective-permute-done | bytes 524320 | tf_op jit(solution)/shard_map/ppermute | solution.py:762
  171.0 11.2 %down_back.1 = (f32[512,1408]{1,0:T(8,128)S(1)}, bf16[8,1408,256]{2,1,0:T(8,128)(2,1)}) custom-call(bf16[128,2048]{1,0:T(8,128)(2,1)S(1)} %copy-done.25, bf16[128,2048]{1,0:T(8,128)(2,1)} %collective-permute-done.8.c1, bf16[128,2048]{1,0:T(8,128)(2,1)} %collective-permute-done.9.c2, bf16[128,2048]{1,0:T(8,128)(2,1)} %collective-permute-done.10.c3, ...), custom_call_target="tpu_custom_call" | custom-call | flops 8589934592 | bytes 1048576 | tf_op jit(solution)/shard_map/down_back/pallas_call | solution.py:488
  185.4 6.1 %collective-permute-done.25 = bf16[64,2048]{1,0:T(8,128)(2,1)S(1)} collective-permute-done((bf16[64,2048]{1,0:T(8,128)(2,1)S(1)}, bf16[64,2048]{1,0:T(8,128)(2,1)S(1)}, u32[]{:S(2)}, u32[]{:S(2)}) %collective-permute-start.25) | collective-permute-done | bytes 262176 | tf_op jit(solution)/shard_map/ppermute | solution.py:762
  193.9 25.1 %feed_forward.1 = (bf16[128,2048]{1,0:T(8,128)(2,1)S(1)}, bf16[128,2048]{1,0:T(8,128)(2,1)S(1)}, bf16[128,2048]{1,0:T(8,128)(2,1)S(1)}, bf16[128,2048]{1,0:T(8,1...) custom-call(s32[1]{0:T(128)} %bitcast.3.sc, bf16[128,2048]{1,0:T(8,128)(2,1)S(1)} %multiply_convert_fusion.n0, ...), custom_call_target="tpu_custom_call" | custom-call | flops 1048576 | bytes 65536 | tf_op jit(solution)/shard_map/feed_forward/pallas_call | solution.py:596
  232.3 10.6 %ffn_grads_other.1 = (bf16[4,4,64,2816]{3,2,1,0:T(8,128)(2,1)}, bf16[4,4,32,2816]{3,2,1,0:T(8,128)(2,1)}) custom-call(s32[1]{0:T(128)} %bitcast.19.sc, bf16[128,2048]{1,0:T(8,128)(2,1)S(1)} %multiply_convert_fusion.n0, bf16[128,2048]{1,0:T(8,128)(2,1)S(1)} %copy-done.6, bf16[128,2048]{1,0:T(8,128)(2,1)S(1)} %copy-done.13, bf16[128,2048]{1,0:T(8,128)(2,1)S(1)} %copy-done.10, ...), custom_call_target="tpu_custom_call" | custom-call | flops 8589934592 | bytes 1048576 | tf_op jit(solution)/shard_map/ffn_grads_other/pallas_call | solution.py:689
  254.4 6.2 %collective-permute-done.34.rest_1_ = bf16[4,4,32,2816]{3,2,1,0:T(8,128)(2,1)} collective-permute-done((bf16[4,4,32,2816]{3,2,1,0:T(8,128)(2,1)}, bf16[4,4,32,2816]{3,2,1,0:T(8,128)(2,1)}, u32[]{:S(2)}, u32[]{:S(2)}) %collective-permute-start.34) | collective-permute-done | bytes 2883616 | tf_op jit(solution)/shard_map/ppermute | solution.py:43
  260.6 12.4 %ffn_grads_mine.1 = (bf16[4,4,64,2816]{3,2,1,0:T(8,128)(2,1)}, bf16[4,4,32,2816]{3,2,1,0:T(8,128)(2,1)}) custom-call(s32[1]{0:T(128)} %bitcast.1.sc, bf16[128,2048]{1,0:T(8,128)(2,1)S(1)} %multiply_convert_fusion.n0, bf16[128,2048]{1,0:T(8,128)(2,1)S(1)} %copy-done.7, bf16[128,2048]{1,0:T(8,128)(2,1)S(1)} %copy-done.14, bf16[128,2048]{1,0:T(8,128)(2,1)S(1)} %copy-done.11, ...), custom_call_target="tpu_custom_call" | custom-call | flops 8589934592 | bytes 1048576 | tf_op jit(solution)/shard_map/ffn_grads_mine/pallas_call | solution.py:689
  276.7 5.2 all-to-all-start.1
  293.3 11.4 %attention_backward.1 = (bf16[512,512]{1,0:T(8,128)(2,1)S(1)}, bf16[16,128,128]{2,1,0:T(8,128)(2,1)S(1)}) custom-call(s32[11]{0:T(128)S(1)} %concatenate.56.sc, bf16[4,64,1024]{2,1,0:T(8,128)(2,1)S(1)} %copy-done.35, bf16[512,512]{1,0:T(8,128)(2,1)S(1)} %convolution_convert_fusion.1.do_ref, f32[512,512]{1,0:T(8,128)S(1)} %copy-done.22, ...), custom_call_target="tpu_custom_call" | custom-call | flops 1048576 | bytes 65536 | tf_op jit(solution)/shard_map/attention_backward/pallas_call | solution.py:243
  304.7 14.2 %collective-permute-done.38 = bf16[4,32,2816]{2,1,0:T(8,128)(2,1)S(1)} collective-permute-done((bf16[4,32,2816]{2,1,0:T(8,128)(2,1)S(1)}, bf16[4,32,2816]{2,1,0:T(8,128)(2,1)S(1)}, u32[]{:S(2)}, u32[]{:S(2)}) %collective-permute-start.38) | collective-permute-done | bytes 720928 | tf_op jit(solution)/shard_map/ppermute | solution.py:794
  330.0 16.7 %all-to-all-done.1 = bf16[4,256,2816]{2,1,0:T(8,128)(2,1)} async-done(((bf16[4,256,2816]{2,1,0:T(8,128)(2,1)}), bf16[4,256,2816]{2,1,0:T(8,128)(2,1)}, u32[]{:S(2)}, u32[]{:S(2)}) %all-to-all-start.1) | async-done | bytes 5767200 | tf_op jit(solution)/shard_map/all_to_all | solution.py:35
  346.7 5.0 convolution_convert_fusion
  366.1 4.7 attention_grads_mine.1
  379.8 5.1 reduce_sum.100
  384.8 5.9 %all-to-all-start.2 = ((bf16[4,64,2816]{2,1,0:T(8,128)(2,1)}), bf16[4,64,2816]{2,1,0:T(8,128)(2,1)S(1)}, u32[]{:S(2)}, u32[]{:S(2)}) async-start(bf16[4,64,2816]{2,1,0:T(8,128)(2,1)} %bitcast.39), calls=%async_computation.2 | async-start | bytes 2883584 | tf_op jit(solution)/shard_map/all_to_all | solution.py:35
  395.0 6.4 %collective-permute-done.48 = bf16[4,64,1152]{2,1,0:T(8,128)(2,1)} collective-permute-done((bf16[4,64,1152]{2,1,0:T(8,128)(2,1)}, bf16[4,64,1152]{2,1,0:T(8,128)(2,1)}, u32[]{:S(2)}, u32[]{:S(2)}) %collective-permute-start.48) | collective-permute-done | bytes 589856 | tf_op jit(solution)/shard_map/ppermute | solution.py:794
  447.5 7.6 %down_forward.1 = (bf16[128,2048]{1,0:T(8,128)(2,1)S(1)}, bf16[128,2048]{1,0:T(8,128)(2,1)S(1)}, bf16[128,2048]{1,0:T(8,128)(2,1)S(1)}, bf16[128,2048]{1,0:T(8,128)(2,1)S(1)}) custom-call(bf16[512,1408]{1,0:T(8,128)(2,1)S(1)} %get-tuple-element.156.act_ref, bf16[8,1408,256]{2,1,0:T(8,128)(2,1)} %get-tuple-element.157.w_ref), custom_call_target="tpu_custom_call" | custom-call | flops 1048576 | bytes 65536 | tf_op jit(solution)/shard_map/down_forward/pallas_call | solution.py:514
  464.7 23.8 %all_to_all.30 = f32[16,2,128]{2,1,0:T(2,128)S(1)} all-to-all(f32[16,2,128]{2,1,0:T(2,128)S(1)} %maximum_bitcast_fusion), channel_id=1, replica_groups=mesh['zlo'=2,'y'=4,'zhi'=2,'x'=4,'core'=2] {'zhi','x','core'}, dimensions={0} | all-to-all | bytes 32768 | tf_op jit(solution)/shard_map/all_to_all | solution.py:35
  488.5 9.4 %all_to_all.31 = bf16[8,2,128]{2,1,0:T(2,128)(2,1)S(1)} all-to-all(bf16[8,2,128]{2,1,0:T(2,128)(2,1)S(1)} %broadcast_in_dim.26), channel_id=1, replica_groups=mesh['zlo'=2,'y'=4,'zhi'=2,'x'=4,'core'=2] {'zlo','y'}, dimensions={0} | all-to-all | bytes 8192 | tf_op jit(solution)/shard_map/all_to_all | solution.py:35
  500.6 22.3 %all-gather.7.cloned.1.call-done = bf16[1024,2816]{1,0:T(8,128)(2,1)} async-done(((bf16[128,2816]{1,0:T(8,128)(2,1)}), bf16[1024,2816]{1,0:T(8,128)(2,1)}) %all-gather.7.cloned.1.call-update) | async-done | bytes 5767184 | tf_op jit(solution)/shard_map/all_gather | solution.py:943
  525.5 4.7 spread.1
  (374 shorter events, 211.1 us)
Async XLA Ops:
  7.2 45.2 %collective-permute-start = (bf16[128,2048]{1,0:T(8,128)(2,1)}, bf16[128,2048]{1,0:T(8,128)(2,1)S(1)}, u32[]{:S(2)}, u32[]{:S(2)}) collective-permute-start(bf16[128,2048]{1,0:T(8,128)(2,1)} %t0.1), channel_id=1, source_target_pairs={{0,6},{2,0},{4,2},{6,4},{1,7},{3,1},{5,3},{7,5},{8,14},{10,8},{12,... | collective-permute-start | bytes 1572872 | tf_op jit(solution)/shard_map/ppermute | solution.py:762
  10.5 41.8 %collective-permute-start.2 = (bf16[128,2048]{1,0:T(8,128)(2,1)}, bf16[128,2048]{1,0:T(8,128)(2,1)S(1)}, u32[]{:S(2)}, u32[]{:S(2)}) collective-permute-start(bf16[128,2048]{1,0:T(8,128)(2,1)} %t0.1), channel_id=1, source_target_pairs={{0,2},{2,4},{4,6},{6,0},{1,3},{3,5},{5,7},{7,1},{8,10},{10,12},{12... | collective-permute-start | bytes 1572872 | tf_op jit(solution)/shard_map/ppermute | solution.py:762
  18.5 33.8 %all-to-all-start = ((bf16[8,144,640]{2,1,0:T(8,128)(2,1)}), bf16[8,144,640]{2,1,0:T(8,128)(2,1)S(1)}, u32[]{:S(2)}, u32[]{:S(2)}) async-start(bf16[8,144,640]{2,1,0:T(8,128)(2,1)} %get-tuple-element.89), calls=%async_computation | async-start | bytes 2949120 | tf_op jit(solution)/shard_map/all_to_all | solution.py:35
  25.8 145.2 %all-gather.5.cloned.1.call-start = ((), (), s32[]{:S(2)}) async-start(), calls=%async_computation.6 | async-start | bytes 17842176 | tf_op jit(solution)/shard_map/all_gather | solution.py:847
  25.8 22.3 %collective-permute-start.21 = (bf16[16,2816]{1,0:T(8,128)(2,1)S(1)}, bf16[16,2816]{1,0:T(8,128)(2,1)S(1)}, u32[]{:S(2)}, u32[]{:S(2)}) collective-permute-start(bf16[16,2816]{1,0:T(8,128)(2,1)S(1)} %get-tuple-element.214), channel_id=1, source_target_pairs={{0,2},{2,4},{4,6},{6,0},{1,3},{3,5},{5,7},{7,1},{8,10},{10,12},{12... | collective-permute-start | bytes 270344 | tf_op jit(solution)/shard_map/ppermute | solution.py:794
  27.3 23.0 %collective-permute-start.22 = (bf16[16,2816]{1,0:T(8,128)(2,1)S(1)}, bf16[16,2816]{1,0:T(8,128)(2,1)S(1)}, u32[]{:S(2)}, u32[]{:S(2)}) collective-permute-start(bf16[16,2816]{1,0:T(8,128)(2,1)S(1)} %get-tuple-element.213), channel_id=1, source_target_pairs={{0,4},{2,6},{4,0},{6,2},{1,5},{3,7},{5,1},{7,3},{8,12},{10,14},{12... | collective-permute-start | bytes 270344 | tf_op jit(solution)/shard_map/ppermute | solution.py:794
  29.7 21.3 %collective-permute-start.23 = (bf16[16,2816]{1,0:T(8,128)(2,1)S(1)}, bf16[16,2816]{1,0:T(8,128)(2,1)S(1)}, u32[]{:S(2)}, u32[]{:S(2)}) collective-permute-start(bf16[16,2816]{1,0:T(8,128)(2,1)S(1)} %get-tuple-element.212), channel_id=1, source_target_pairs={{0,6},{2,0},{4,2},{6,4},{1,7},{3,1},{5,3},{7,5},{8,14},{10,8},{12,... | collective-permute-start | bytes 270344 | tf_op jit(solution)/shard_map/ppermute | solution.py:794
  52.4 21.5 %collective-permute-start.4 = (bf16[8,144,640]{2,1,0:T(8,128)(2,1)S(1)}, bf16[8,144,640]{2,1,0:T(8,128)(2,1)}, u32[]{:S(2)}, u32[]{:S(2)}) collective-permute-start(bf16[8,144,640]{2,1,0:T(8,128)(2,1)S(1)} %all-to-all-done.mine), channel_id=1, source_target_pairs={{0,1},{1,0},{2,3},{3,2},{4,5},{5,4},{6,7},{7,6},{8,9},{9,8},{10,11... | collective-permute-start | bytes 4423688 | tf_op jit(solution)/shard_map/ppermute | solution.py:43
  53.3 31.7 %collective-permute-start.7 = (bf16[128,2048]{1,0:T(8,128)(2,1)}, bf16[128,2048]{1,0:T(8,128)(2,1)}, u32[]{:S(2)}, u32[]{:S(2)}) collective-permute-start(bf16[128,2048]{1,0:T(8,128)(2,1)} %param.14), channel_id=1, source_target_pairs={{0,8},{8,0},{1,9},{9,1},{2,10},{10,2},{3,11},{11,3},{4,12},{12,4},... | collective-permute-start | bytes 1572872 | tf_op jit(solution)/shard_map/ppermute | solution.py:43
  87.2 28.3 %collective-permute-start.10 = (bf16[128,2048]{1,0:T(8,128)(2,1)S(1)}, bf16[128,2048]{1,0:T(8,128)(2,1)}, u32[]{:S(2)}, u32[]{:S(2)}) collective-permute-start(bf16[128,2048]{1,0:T(8,128)(2,1)S(1)} %copy-done.24), channel_id=1, source_target_pairs={{0,2},{2,4},{4,6},{6,0},{1,3},{3,5},{5,7},{7,1},{8,10},{10,12},{12... | collective-permute-start | bytes 1572872 | tf_op jit(solution)/shard_map/ppermute | solution.py:762
  87.2 28.3 %collective-permute-start.8 = (bf16[128,2048]{1,0:T(8,128)(2,1)S(1)}, bf16[128,2048]{1,0:T(8,128)(2,1)}, u32[]{:S(2)}, u32[]{:S(2)}) collective-permute-start(bf16[128,2048]{1,0:T(8,128)(2,1)S(1)} %copy-done.24), channel_id=1, source_target_pairs={{0,6},{2,0},{4,2},{6,4},{1,7},{3,1},{5,3},{7,5},{8,14},{10,8},{12,... | collective-permute-start | bytes 1572872 | tf_op jit(solution)/shard_map/ppermute | solution.py:762
  89.9 25.6 %collective-permute-start.9 = (bf16[128,2048]{1,0:T(8,128)(2,1)S(1)}, bf16[128,2048]{1,0:T(8,128)(2,1)}, u32[]{:S(2)}, u32[]{:S(2)}) collective-permute-start(bf16[128,2048]{1,0:T(8,128)(2,1)S(1)} %copy-done.24), channel_id=1, source_target_pairs={{0,4},{2,6},{4,0},{6,2},{1,5},{3,7},{5,1},{7,3},{8,12},{10,14},{12... | collective-permute-start | bytes 1572872 | tf_op jit(solution)/shard_map/ppermute | solution.py:762
  89.9 32.8 %collective-permute-start.12 = (bf16[128,2048]{1,0:T(8,128)(2,1)}, bf16[128,2048]{1,0:T(8,128)(2,1)}, u32[]{:S(2)}, u32[]{:S(2)}) collective-permute-start(bf16[128,2048]{1,0:T(8,128)(2,1)} %get-tuple-element.97), channel_id=1, source_target_pairs={{0,4},{2,0},{4,6},{6,2},{1,5},{3,1},{5,7},{7,3},{8,12},{10,8},{12,... | collective-permute-start | bytes 1572872 | tf_op jit(solution)/shard_map/ppermute | solution.py:871
  98.5 25.7 %collective-permute-start.11 = (bf16[128,2048]{1,0:T(8,128)(2,1)}, bf16[128,2048]{1,0:T(8,128)(2,1)}, u32[]{:S(2)}, u32[]{:S(2)}) collective-permute-start(bf16[128,2048]{1,0:T(8,128)(2,1)} %get-tuple-element.95), channel_id=1, source_target_pairs={{0,0},{2,4},{4,2},{6,6},{1,1},{3,5},{5,3},{7,7},{8,8},{10,12},{12,... | collective-permute-start | bytes 1572872 | tf_op jit(solution)/shard_map/ppermute | solution.py:870
  164.6 19.1 %collective-permute-start.19 = (bf16[128,2048]{1,0:T(8,128)(2,1)S(1)}, bf16[128,2048]{1,0:T(8,128)(2,1)S(1)}, u32[]{:S(2)}, u32[]{:S(2)}) collective-permute-start(bf16[128,2048]{1,0:T(8,128)(2,1)S(1)} %multiply_convert_fusion.n0), channel_id=1, source_target_pairs={{0,6},{2,0},{4,2},{6,4},{1,7},{3,1},{5,3},{7,5},{8,14},{10,8},{12,... | collective-permute-start | bytes 1572872 | tf_op jit(solution)/shard_map/ppermute | solution.py:762
  242.9 17.7 %collective-permute-start.33 = (bf16[4,4,64,2816]{3,2,1,0:T(8,128)(2,1)}, bf16[4,4,64,2816]{3,2,1,0:T(8,128)(2,1)}, u32[]{:S(2)}, u32[]{:S(2)}) collective-permute-start(bf16[4,4,64,2816]{3,2,1,0:T(8,128)(2,1)} %get-tuple-element.124), channel_id=1, source_target_pairs={{0,1},{1,0},{2,3},{3,2},{4,5},{5,4},{6,7},{7,6},{8,9},{9,8},{10,11... | collective-permute-start | bytes 17301512 | tf_op jit(solution)/shard_map/ppermute | solution.py:43
  252.9 20.1 %collective-permute-start.31 = (bf16[128,2048]{1,0:T(8,128)(2,1)S(1)}, bf16[128,2048]{1,0:T(8,128)(2,1)S(1)}, u32[]{:S(2)}, u32[]{:S(2)}) collective-permute-start(bf16[128,2048]{1,0:T(8,128)(2,1)S(1)} %get-tuple-element.177), channel_id=1, source_target_pairs={{0,6},{2,0},{4,2},{6,4},{1,7},{3,1},{5,3},{7,5},{8,14},{10,8},{12,... | collective-permute-start | bytes 1572872 | tf_op jit(solution)/shard_map/ppermute | solution.py:762
  253.7 19.3 %collective-permute-start.32 = (bf16[128,2048]{1,0:T(8,128)(2,1)S(1)}, bf16[128,2048]{1,0:T(8,128)(2,1)S(1)}, u32[]{:S(2)}, u32[]{:S(2)}) collective-permute-start(bf16[128,2048]{1,0:T(8,128)(2,1)S(1)} %get-tuple-element.177), channel_id=1, source_target_pairs={{0,2},{2,4},{4,6},{6,0},{1,3},{3,5},{5,7},{7,1},{8,10},{10,12},{12... | collective-permute-start | bytes 1572872 | tf_op jit(solution)/shard_map/ppermute | solution.py:762
  276.7 70.0 %all-to-all-start.1 = ((bf16[4,256,2816]{2,1,0:T(8,128)(2,1)}), bf16[4,256,2816]{2,1,0:T(8,128)(2,1)}, u32[]{:S(2)}, u32[]{:S(2)}) async-start(bf16[4,256,2816]{2,1,0:T(8,128)(2,1)} %bitcast.147), calls=%async_computation.1 | async-start | bytes 11534336 | tf_op jit(solution)/shard_map/all_to_all | solution.py:35
  284.5 20.2 %collective-permute-start.37 = (bf16[4,32,2816]{2,1,0:T(8,128)(2,1)S(1)}, bf16[4,32,2816]{2,1,0:T(8,128)(2,1)S(1)}, u32[]{:S(2)}, u32[]{:S(2)}) collective-permute-start(bf16[4,32,2816]{2,1,0:T(8,128)(2,1)S(1)} %get-tuple-element.183), channel_id=1, source_target_pairs={{0,8},{8,64},{64,72},{72,0},{1,9},{9,65},{65,73},{73,1},{2,10},{10... | collective-permute-start | bytes 2162696 | tf_op jit(solution)/shard_map/ppermute | solution.py:794
  288.6 30.3 %collective-permute-start.38 = (bf16[4,32,2816]{2,1,0:T(8,128)(2,1)S(1)}, bf16[4,32,2816]{2,1,0:T(8,128)(2,1)S(1)}, u32[]{:S(2)}, u32[]{:S(2)}) collective-permute-start(bf16[4,32,2816]{2,1,0:T(8,128)(2,1)S(1)} %get-tuple-element.182), channel_id=1, source_target_pairs={{0,64},{8,72},{64,0},{72,8},{1,65},{9,73},{65,1},{73,9},{2,66},{10... | collective-permute-start | bytes 2162696 | tf_op jit(solution)/shard_map/ppermute | solution.py:794
  288.6 30.9 %collective-permute-start.39 = (bf16[4,32,2816]{2,1,0:T(8,128)(2,1)S(1)}, bf16[4,32,2816]{2,1,0:T(8,128)(2,1)S(1)}, u32[]{:S(2)}, u32[]{:S(2)}) collective-permute-start(bf16[4,32,2816]{2,1,0:T(8,128)(2,1)S(1)} %get-tuple-element.181), channel_id=1, source_target_pairs={{0,72},{8,0},{64,8},{72,64},{1,73},{9,1},{65,9},{73,65},{2,74},{10... | collective-permute-start | bytes 2162696 | tf_op jit(solution)/shard_map/ppermute | solution.py:794
  373.8 27.7 %collective-permute-start.48 = (bf16[4,64,1152]{2,1,0:T(8,128)(2,1)}, bf16[4,64,1152]{2,1,0:T(8,128)(2,1)}, u32[]{:S(2)}, u32[]{:S(2)}) collective-permute-start(bf16[4,64,1152]{2,1,0:T(8,128)(2,1)} %get-tuple-element.187), channel_id=1, source_target_pairs={{0,32},{16,48},{32,0},{48,16},{1,33},{17,49},{33,1},{49,17},{2,34}... | collective-permute-start | bytes 1769480 | tf_op jit(solution)/shard_map/ppermute | solution.py:794
  375.5 26.8 %collective-permute-start.49 = (bf16[4,64,1152]{2,1,0:T(8,128)(2,1)}, bf16[4,64,1152]{2,1,0:T(8,128)(2,1)}, u32[]{:S(2)}, u32[]{:S(2)}) collective-permute-start(bf16[4,64,1152]{2,1,0:T(8,128)(2,1)} %get-tuple-element.186), channel_id=1, source_target_pairs={{0,48},{16,0},{32,16},{48,32},{1,49},{17,1},{33,17},{49,33},{2,50}... | collective-permute-start | bytes 1769480 | tf_op jit(solution)/shard_map/ppermute | solution.py:794
  378.9 54.6 %collective-permute-start.45 = (bf16[128,2048]{1,0:T(8,128)(2,1)}, bf16[128,2048]{1,0:T(8,128)(2,1)}, u32[]{:S(2)}, u32[]{:S(2)}) collective-permute-start(bf16[128,2048]{1,0:T(8,128)(2,1)} %pad_maximum_fusion.7), channel_id=1, source_target_pairs={{0,6},{2,0},{4,2},{6,4},{1,7},{3,1},{5,3},{7,5},{8,14},{10,8},{12,... | collective-permute-start | bytes 1572872 | tf_op jit(solution)/shard_map/ppermute | solution.py:762
  384.8 25.0 %all-to-all-start.2 = ((bf16[4,64,2816]{2,1,0:T(8,128)(2,1)}), bf16[4,64,2816]{2,1,0:T(8,128)(2,1)S(1)}, u32[]{:S(2)}, u32[]{:S(2)}) async-start(bf16[4,64,2816]{2,1,0:T(8,128)(2,1)} %bitcast.39), calls=%async_computation.2 | async-start | bytes 2883584 | tf_op jit(solution)/shard_map/all_to_all | solution.py:35
  392.6 22.5 %collective-permute-start.53 = (bf16[32,2816]{1,0:T(8,128)(2,1)}, bf16[32,2816]{1,0:T(8,128)(2,1)}, u32[]{:S(2)}, u32[]{:S(2)}) collective-permute-start(bf16[32,2816]{1,0:T(8,128)(2,1)} %get-tuple-element.196), channel_id=1, source_target_pairs={{0,16},{16,32},{32,48},{48,0},{1,17},{17,33},{33,49},{49,1},{2,18}... | collective-permute-start | bytes 540680 | tf_op jit(solution)/shard_map/ppermute | solution.py:794
  393.7 21.6 %collective-permute-start.54 = (bf16[32,2816]{1,0:T(8,128)(2,1)}, bf16[32,2816]{1,0:T(8,128)(2,1)}, u32[]{:S(2)}, u32[]{:S(2)}) collective-permute-start(bf16[32,2816]{1,0:T(8,128)(2,1)} %get-tuple-element.198), channel_id=1, source_target_pairs={{0,32},{16,48},{32,0},{48,16},{1,33},{17,49},{33,1},{49,17},{2,34}... | collective-permute-start | bytes 540680 | tf_op jit(solution)/shard_map/ppermute | solution.py:794
  415.1 107.7 %all-gather.7.cloned.1.call-start = ((), (), s32[]{:S(2)}) async-start(), calls=%async_computation.7 | async-start | bytes 6488064 | tf_op jit(solution)/shard_map/all_gather | solution.py:943
  420.8 18.2 %collective-permute-start.43 = (bf16[128,2048]{1,0:T(8,128)(2,1)}, bf16[128,2048]{1,0:T(8,128)(2,1)}, u32[]{:S(2)}, u32[]{:S(2)}) collective-permute-start(bf16[128,2048]{1,0:T(8,128)(2,1)} %pad_maximum_fusion.6), channel_id=1, source_target_pairs={{0,2},{2,4},{4,6},{6,0},{1,3},{3,5},{5,7},{7,1},{8,10},{10,12},{12... | collective-permute-start | bytes 1572872 | tf_op jit(solution)/shard_map/ppermute | solution.py:762
  461.8 36.7 %collective-permute-start.58 = (bf16[128,2048]{1,0:T(8,128)(2,1)S(1)}, bf16[128,2048]{1,0:T(8,128)(2,1)S(1)}, u32[]{:S(2)}, u32[]{:S(2)}) collective-permute-start(bf16[128,2048]{1,0:T(8,128)(2,1)S(1)} %pad_maximum_fusion.8), channel_id=1, source_target_pairs={{0,2},{2,4},{4,6},{6,0},{1,3},{3,5},{5,7},{7,1},{8,10},{10,12},{12... | collective-permute-start | bytes 1572872 | tf_op jit(solution)/shard_map/ppermute | solution.py:762
  462.0 36.5 %collective-permute-start.60 = (bf16[128,2048]{1,0:T(8,128)(2,1)S(1)}, bf16[128,2048]{1,0:T(8,128)(2,1)}, u32[]{:S(2)}, u32[]{:S(2)}) collective-permute-start(bf16[128,2048]{1,0:T(8,128)(2,1)S(1)} %pad_maximum_fusion.9), channel_id=1, source_target_pairs={{0,6},{2,0},{4,2},{6,4},{1,7},{3,1},{5,3},{7,5},{8,14},{10,8},{12,... | collective-permute-start | bytes 1572872 | tf_op jit(solution)/shard_map/ppermute | solution.py:762
  (105 other events, 951.6 us)
Sparse Core Ops, SparseCore 0:
  52.5 118.4 all-gather.4
  447.6 75.2 all-gather.6
